TPU v7x, 32 devices: a whole 2x2x4 slice. The times are simulated.
32 devices in a mesh: node: 4 (over y, core), lane: 8 (over z, x).
Axes of the slice: x: 2, y: 2, z: 4, core: 2. Of those that a mesh axis runs over, the one named last changes fastest.
Arguments:
- old_field: float32 [256, 16, 256], P(('node', 'lane')), may hold values from -6 to 6
- old_source: float32 [256, 16, 256], P(('node', 'lane')), may hold values from -6 to 6
- diffusivity: float32 [256, 16, 256], P(('node', 'lane')), may hold values from 0.25 to 4
- target_box: int32 [256], P(('node', 'lane')), may hold values from 0 to 255, as said below
- neighbours: int32 [256, 6], P(('node', 'lane')), may hold values from -1 to 255, as said below
Outputs:
- smoothed: float32 [256, 16, 256], P(('node', 'lane'))
- coarse_defect: float32 [256, 512], P(('node', 'lane'))
Inputs may be any that keep to these rules, and one draw needn't show every extreme that they name: `target_box`: every new index appears once; the new owner of a box is its index // 8, the old owner its position // 8. A box moves only to a device of the same node, either at most 2 lane positions away or exactly half the lane axis away; at most one box goes from one device to one other, every device receives as many boxes as it sends, and in every draw some device of each node exchanges a box with every device within 2 lane positions, and some device of each node exchanges a box with the device half the lane axis away. `neighbours`: the neighbour across a face lies on the same device, across faces 0 and 1 possibly on the device one node index lower or higher, across faces 2 and 3 possibly on the device one lane index lower or higher in the same node, never elsewhere. The relation is symmetric: if box a's face f has neighbour b, then b's face f xor 1 has neighbour a. On one device at most 4 boxes have a face 0 (or face 1) neighbour on another device, and at most 8 a face 2 (or face 3) neighbour on another device. -1 marks a face with no box of this level beyond it.
All inputs are finite; a program needn't handle non-finite values.
Results may differ from a plain program's by a relative error of at most 0.00005.
Values sent between devices are 32-bit elements; how exact they have to be, the bound alone decides.
No kernel may reach another device: no remote copies, remote signals or barrier semaphores. Data moves between devices by JAX's collectives and lax.ppermute only.
A program may use at most 64 MiB of HBM per device.

v0:
```python
import jax
import jax.numpy as jnp
from jax import lax
from jax.sharding import PartitionSpec as P

SWEEPS = 2


OPPOSITE = (1, 0, 3, 2, 5, 4)


def with_halo(block, sides, width):
    for axis, dim in sides:
        count = lax.axis_size(axis)
        forward = [(i, i + 1) for i in range(count - 1)]
        backward = [(target, source) for source, target in forward]
        low = lax.ppermute(
            lax.slice_in_dim(block, block.shape[dim] - width, None, axis=dim), axis, forward
        )
        high = lax.ppermute(lax.slice_in_dim(block, 0, width, axis=dim), axis, backward)
        block = jnp.concatenate([low, block, high], axis=dim)
    return block


def face_layers(values):
    boxes, side, plane = values.shape
    return jnp.stack(
        [
            values[:, 0],
            values[:, side - 1],
            values[:, :, :side].reshape(boxes, plane),
            values[:, :, plane - side :].reshape(boxes, plane),
            values[:, :, 0::side].reshape(boxes, plane),
            values[:, :, side - 1 :: side].reshape(boxes, plane),
        ],
        axis=1,
    )


def near_values(values, ghost):
    boxes, side, plane = values.shape
    lower_x = jnp.concatenate([ghost[:, 0][:, None, :], values[:, :-1]], axis=1)
    upper_x = jnp.concatenate([values[:, 1:], ghost[:, 1][:, None, :]], axis=1)
    lower_y = jnp.concatenate(
        [ghost[:, 2].reshape(boxes, side, side), values[:, :, : plane - side]], axis=2
    )
    upper_y = jnp.concatenate([values[:, :, side:], ghost[:, 3].reshape(boxes, side, side)], axis=2)
    depth = jnp.arange(plane) % side
    lower_z = jnp.where(
        depth == 0,
        jnp.repeat(ghost[:, 4].reshape(boxes, side, side), side, axis=2),
        jnp.roll(values, 1, axis=2),
    )
    upper_z = jnp.where(
        depth == side - 1,
        jnp.repeat(ghost[:, 5].reshape(boxes, side, side), side, axis=2),
        jnp.roll(values, -1, axis=2),
    )
    return [lower_x, upper_x, lower_y, upper_y, lower_z, upper_z]


def coefficients(diffusivity, beside):
    return [2.0 * diffusivity * other / (diffusivity + other) for other in beside]


def relax(values, source, couplings, beside, chosen):
    total = couplings[0]
    summed = source + couplings[0] * beside[0]
    for face in range(1, 6):
        total = total + couplings[face]
        summed = summed + couplings[face] * beside[face]
    return jnp.where(chosen, summed / total, values)


def defect_of(values, source, couplings, beside):
    total = couplings[0]
    summed = source + couplings[0] * beside[0]
    for face in range(1, 6):
        total = total + couplings[face]
        summed = summed + couplings[face] * beside[face]
    return summed - total * values


def colour_of(side, plane):
    rows = jnp.arange(side)[:, None]
    cells = jnp.arange(plane)[None, :]
    return (rows + cells // side + cells % side) % 2


def restrict(values):
    boxes, side, plane = values.shape
    half = side // 2
    paired = values.reshape(boxes, half, 2, plane).sum(axis=2)
    cells = jnp.arange(plane)
    coarse_cols = cells // side // 2 * half + cells % side // 2
    pooling = (coarse_cols[:, None] == jnp.arange(half * half)[None, :]).astype(jnp.float32)
    summed = jnp.einsum("bxp,pq->bxq", paired, pooling, precision=lax.Precision.HIGHEST)
    return (0.125 * summed).reshape(boxes, half * half * half)


def place(settled, arrived, tags):
    count = settled.shape[0]
    return settled.at[jnp.where(tags > 0, tags - 1, count)].set(arrived, mode="drop")


def body(old_field, old_source, diffusivity, target_box, neighbours):
    count, side, plane = old_field.shape
    lane_count = lax.axis_size("lane")
    lane_here = lax.axis_index("lane")
    own_device = lax.axis_index("node") * lane_count + lane_here
    dest_device = target_box // count
    dest_slot = target_box % count
    staying = dest_device == own_device
    cargo = jnp.stack([old_field, old_source], axis=1)
    settled = jnp.zeros_like(cargo).at[jnp.where(staying, dest_slot, count)].set(cargo, mode="drop")
    slots = jnp.arange(count)
    peers = own_device - lane_here + jnp.arange(lane_count)
    chosen = (dest_device[None, :] == peers[:, None]) & jnp.logical_not(staying)[None, :]
    filled = jnp.any(chosen, axis=1)
    picked = jnp.sum(jnp.where(chosen, slots[None, :], 0), axis=1)
    parcels = jnp.where(filled[:, None, None, None], cargo[picked], 0.0)
    labels = jnp.where(filled, jnp.sum(jnp.where(chosen, dest_slot[None, :], 0), axis=1) + 1, 0)
    arrived, tags = (
        lax.all_to_all(parcels, "lane", split_axis=0, concat_axis=0, tiled=True),
        lax.all_to_all(labels, "lane", split_axis=0, concat_axis=0, tiled=True),
    )
    settled = place(settled, arrived, tags)
    field = settled[:, 0]
    source = settled[:, 1]
    present = neighbours >= 0
    near_device = jnp.where(present, neighbours // count, own_device)
    local_row = neighbours % count * 6 + jnp.array(OPPOSITE, jnp.int32)[None, :]
    across = near_device - own_device
    anchor = jnp.where(
        across == -lane_count,
        1,
        jnp.where(
            across == lane_count, 2, jnp.where(across == -1, 3, jnp.where(across == 1, 4, 0))
        ),
    )
    index = anchor * (count * 6) + local_row
    width_out = count * 6

    def departing_boxes(layers):
        return layers.reshape(count * 6, plane)

    def incoming(received, start):
        return jnp.concatenate(
            [
                received[0, 1, start : start + width_out],
                received[2, 1, start : start + width_out],
                received[1, 0, start : start + width_out],
                received[1, 2, start : start + width_out],
            ],
            axis=0,
        )

    def trade(rows):
        return with_halo(rows[None, None], (("node", 0), ("lane", 1)), 1)

    def ghosts(layers, remote_rows, fallback):
        table = jnp.concatenate([layers.reshape(count * 6, plane), remote_rows], axis=0)
        return jnp.where(present[..., None], table[index], fallback)

    beta_layers = face_layers(diffusivity)
    layers = face_layers(field)
    received = trade(
        jnp.concatenate([departing_boxes(layers), departing_boxes(beta_layers)], axis=0)
    )
    beta_ghost = ghosts(beta_layers, incoming(received, width_out), beta_layers)
    couplings = coefficients(diffusivity, near_values(diffusivity, beta_ghost))
    colour = colour_of(side, plane)
    for sweep in range(SWEEPS):
        for colour_id in (0, 1):
            if sweep + colour_id > 0:
                layers = face_layers(field)
                received = trade(departing_boxes(layers))
            ghost = ghosts(layers, incoming(received, 0), jnp.zeros_like(layers))
            field = relax(field, source, couplings, near_values(field, ghost), colour == colour_id)
    layers = face_layers(field)
    received = trade(departing_boxes(layers))
    ghost = ghosts(layers, incoming(received, 0), jnp.zeros_like(layers))
    coarse = restrict(defect_of(field, source, couplings, near_values(field, ghost)))
    return (field, coarse)


def solution(mesh):
    in_specs = (
        P(("node", "lane"), None, None),
        P(("node", "lane"), None, None),
        P(("node", "lane"), None, None),
        P(("node", "lane")),
        P(("node", "lane"), None),
    )
    out_specs = (P(("node", "lane"), None, None), P(("node", "lane"), None))
    return jax.shard_map(body, mesh=mesh, in_specs=in_specs, out_specs=out_specs, check_vma=False)
```

profile of v0, /device:TPU:0, one launch (start us, length us, event | category | flops | bytes accessed | tf_op | source)
XLA Modules:
  0.0 160.7 jit_solution(15634645230292941107)
XLA Ops:
  2.4 7.3 %all-to-all-start = ((s32[8,1,1]{2,1,0:T(1,128)}), s32[8,1,1]{2,1,0:T(1,128)S(1)}, u32[]{:S(2)}, u32[]{:S(2)}) async-start(s32[8,1,1]{2,1,0:T(1,128)} %copy.106), calls=%async_computation | async-start | bytes 8192 | tf_op jit(solution)/shard_map/all_to_all | solution.py:125
  16.0 5.3 %all-to-all-start.1 = ((f32[8,2,16,256]{3,2,1,0:T(8,128)}), f32[8,2,16,256]{3,2,1,0:T(8,128)S(1)}, u32[]{:S(2)}, u32[]{:S(2)}) async-start(f32[8,2,16,256]{3,2,1,0:T(8,128)} %broadcast_select_fusion), calls=%async_computation.1 | async-start | bytes 524288 | tf_op jit(solution)/shard_map/all_to_all | solution.py:124
  24.1 5.7 %all-to-all-done.1 = f32[8,2,16,256]{3,2,1,0:T(8,128)S(1)} async-done(((f32[8,2,16,256]{3,2,1,0:T(8,128)}), f32[8,2,16,256]{3,2,1,0:T(8,128)S(1)}, u32[]{:S(2)}, u32[]{:S(2)}) %all-to-all-start.1) | async-done | bytes 262176 | tf_op jit(solution)/shard_map/all_to_all | solution.py:124
  38.2 3.2 %collective-permute-start.2 = (f32[3,1,96,256]{3,2,1,0:T(8,128)S(1)}, f32[3,1,96,256]{3,2,1,0:T(8,128)S(1)}, u32[]{:S(2)}, u32[]{:S(2)}) collective-permute-start(f32[3,1,96,256]{3,2,1,0:T(8,128)S(1)} %pad_maximum_fusion), channel_id=1, source_target_pairs={{0,1},{1,2},{2,3},{3,4},{4,5},{5,6},{6,7},{8,9},{9,10},{10,11},{11... | collective-permute-start | bytes 884744 | tf_op jit(solution)/shard_map/ppermute | solution.py:17
  42.8 3.7 %collective-permute-done.2 = f32[3,1,96,256]{3,2,1,0:T(8,128)S(1)} collective-permute-done((f32[3,1,96,256]{3,2,1,0:T(8,128)S(1)}, f32[3,1,96,256]{3,2,1,0:T(8,128)S(1)}, u32[]{:S(2)}, u32[]{:S(2)}) %collective-permute-start.2) | collective-permute-done | bytes 294944 | tf_op jit(solution)/shard_map/ppermute | solution.py:17
  46.5 4.7 %collective-permute-done.3 = f32[3,1,96,256]{3,2,1,0:T(8,128)S(1)} collective-permute-done((f32[3,1,96,256]{3,2,1,0:T(8,128)S(1)}, f32[3,1,96,256]{3,2,1,0:T(8,128)S(1)}, u32[]{:S(2)}, u32[]{:S(2)}) %collective-permute-start.3) | collective-permute-done | bytes 294944 | tf_op jit(solution)/shard_map/ppermute | solution.py:20
  58.3 1.6 %fusion.7 = (f32[8,16,256]{2,1,0:T(8,128)S(1)}, f32[8,16,256]{2,1,0:T(8,128)S(1)}, f32[8,16,256]{2,1,0:T(8,128)S(1)}, f32[8,16,256]{2,1,0:T(8,128)S(1)}, f32[8,1...) fusion(f32[8,15,256]{2,1,0:T(8,128)} %get-tuple-element.106, ...), kind=kLoop, calls=%fused_computation.23 | loop fusion | flops 1769472 | bytes 3412480 | tf_op jit(solution)/shard_map/jit(_where)/select_n | solution.py:72
  61.2 6.0 %collective-permute-start.4 = (f32[1,1,48,256]{3,2,1,0:T(8,128)S(1)}, f32[1,1,48,256]{3,2,1,0:T(8,128)S(1)}, u32[]{:S(2)}, u32[]{:S(2)}) collective-permute-start(f32[1,1,48,256]{3,2,1,0:T(8,128)S(1)} %broadcast_in_dim_reshape.12), channel_id=1, source_target_pairs={{0,8},{8,16},{16,24},{1,9},{9,17},{17,25},{2,10},{10,18},{18,26},{... | collective-permute-start | bytes 147464 | tf_op jit(solution)/shard_map/ppermute | solution.py:17
  68.9 2.6 %collective-permute-done.5 = f32[1,1,48,256]{3,2,1,0:T(8,128)S(1)} collective-permute-done((f32[1,1,48,256]{3,2,1,0:T(8,128)S(1)}, f32[1,1,48,256]{3,2,1,0:T(8,128)S(1)}, u32[]{:S(2)}, u32[]{:S(2)}) %collective-permute-start.5) | collective-permute-done | bytes 49184 | tf_op jit(solution)/shard_map/ppermute | solution.py:20
  71.5 4.4 %collective-permute-start.6 = (f32[3,1,48,256]{3,2,1,0:T(8,128)S(1)}, f32[3,1,48,256]{3,2,1,0:T(8,128)S(1)}, u32[]{:S(2)}, u32[]{:S(2)}) collective-permute-start(f32[3,1,48,256]{3,2,1,0:T(8,128)S(1)} %constant_dynamic-update-slice_fusion.10), channel_id=1, source_target_pairs={{0,1},{1,2},{2,3},{3,4},{4,5},{5,6},{6,7},{8,9},{9,10},{10,11},{11... | collective-permute-start | bytes 442376 | tf_op jit(solution)/shard_map/ppermute | solution.py:17
  78.6 4.4 %collective-permute-done.7 = f32[3,1,48,256]{3,2,1,0:T(8,128)S(1)} collective-permute-done((f32[3,1,48,256]{3,2,1,0:T(8,128)S(1)}, f32[3,1,48,256]{3,2,1,0:T(8,128)S(1)}, u32[]{:S(2)}, u32[]{:S(2)}) %collective-permute-start.7) | collective-permute-done | bytes 147488 | tf_op jit(solution)/shard_map/ppermute | solution.py:20
  88.4 3.5 %collective-permute-start.8 = (f32[1,1,48,256]{3,2,1,0:T(8,128)S(1)}, f32[1,1,48,256]{3,2,1,0:T(8,128)S(1)}, u32[]{:S(2)}, u32[]{:S(2)}) collective-permute-start(f32[1,1,48,256]{3,2,1,0:T(8,128)S(1)} %broadcast_in_dim_reshape.13), channel_id=1, source_target_pairs={{0,8},{8,16},{16,24},{1,9},{9,17},{17,25},{2,10},{10,18},{18,26},{... | collective-permute-start | bytes 147464 | tf_op jit(solution)/shard_map/ppermute | solution.py:17
  93.6 2.1 %collective-permute-done.9 = f32[1,1,48,256]{3,2,1,0:T(8,128)S(1)} collective-permute-done((f32[1,1,48,256]{3,2,1,0:T(8,128)S(1)}, f32[1,1,48,256]{3,2,1,0:T(8,128)S(1)}, u32[]{:S(2)}, u32[]{:S(2)}) %collective-permute-start.9) | collective-permute-done | bytes 49184 | tf_op jit(solution)/shard_map/ppermute | solution.py:20
  95.8 4.8 %collective-permute-start.10 = (f32[3,1,48,256]{3,2,1,0:T(8,128)S(1)}, f32[3,1,48,256]{3,2,1,0:T(8,128)S(1)}, u32[]{:S(2)}, u32[]{:S(2)}) collective-permute-start(f32[3,1,48,256]{3,2,1,0:T(8,128)S(1)} %constant_dynamic-update-slice_fusion.18), channel_id=1, source_target_pairs={{0,1},{1,2},{2,3},{3,4},{4,5},{5,6},{6,7},{8,9},{9,10},{10,11},{11... | collective-permute-start | bytes 442376 | tf_op jit(solution)/shard_map/ppermute | solution.py:17
  103.2 4.4 %collective-permute-done.11 = f32[3,1,48,256]{3,2,1,0:T(8,128)S(1)} collective-permute-done((f32[3,1,48,256]{3,2,1,0:T(8,128)S(1)}, f32[3,1,48,256]{3,2,1,0:T(8,128)S(1)}, u32[]{:S(2)}, u32[]{:S(2)}) %collective-permute-start.11) | collective-permute-done | bytes 147488 | tf_op jit(solution)/shard_map/ppermute | solution.py:20
  114.6 3.3 %collective-permute-start.12 = (f32[1,1,48,256]{3,2,1,0:T(8,128)S(1)}, f32[1,1,48,256]{3,2,1,0:T(8,128)S(1)}, u32[]{:S(2)}, u32[]{:S(2)}) collective-permute-start(f32[1,1,48,256]{3,2,1,0:T(8,128)S(1)} %broadcast_in_dim_reshape.14), channel_id=1, source_target_pairs={{0,8},{8,16},{16,24},{1,9},{9,17},{17,25},{2,10},{10,18},{18,26},{... | collective-permute-start | bytes 147464 | tf_op jit(solution)/shard_map/ppermute | solution.py:17
  119.6 2.3 %collective-permute-done.13 = f32[1,1,48,256]{3,2,1,0:T(8,128)S(1)} collective-permute-done((f32[1,1,48,256]{3,2,1,0:T(8,128)S(1)}, f32[1,1,48,256]{3,2,1,0:T(8,128)S(1)}, u32[]{:S(2)}, u32[]{:S(2)}) %collective-permute-start.13) | collective-permute-done | bytes 49184 | tf_op jit(solution)/shard_map/ppermute | solution.py:20
  121.9 2.9 %collective-permute-start.14 = (f32[3,1,48,256]{3,2,1,0:T(8,128)S(1)}, f32[3,1,48,256]{3,2,1,0:T(8,128)S(1)}, u32[]{:S(2)}, u32[]{:S(2)}) collective-permute-start(f32[3,1,48,256]{3,2,1,0:T(8,128)S(1)} %constant_dynamic-update-slice_fusion.26), channel_id=1, source_target_pairs={{0,1},{1,2},{2,3},{3,4},{4,5},{5,6},{6,7},{8,9},{9,10},{10,11},{11... | collective-permute-start | bytes 442376 | tf_op jit(solution)/shard_map/ppermute | solution.py:17
  127.5 4.4 %collective-permute-done.15 = f32[3,1,48,256]{3,2,1,0:T(8,128)S(1)} collective-permute-done((f32[3,1,48,256]{3,2,1,0:T(8,128)S(1)}, f32[3,1,48,256]{3,2,1,0:T(8,128)S(1)}, u32[]{:S(2)}, u32[]{:S(2)}) %collective-permute-start.15) | collective-permute-done | bytes 147488 | tf_op jit(solution)/shard_map/ppermute | solution.py:20
  137.4 3.3 %collective-permute-start.16 = (f32[1,1,48,256]{3,2,1,0:T(8,128)S(1)}, f32[1,1,48,256]{3,2,1,0:T(8,128)S(1)}, u32[]{:S(2)}, u32[]{:S(2)}) collective-permute-start(f32[1,1,48,256]{3,2,1,0:T(8,128)S(1)} %broadcast_in_dim_reshape.15), channel_id=1, source_target_pairs={{0,8},{8,16},{16,24},{1,9},{9,17},{17,25},{2,10},{10,18},{18,26},{... | collective-permute-start | bytes 147464 | tf_op jit(solution)/shard_map/ppermute | solution.py:17
  142.4 2.3 %collective-permute-done.17 = f32[1,1,48,256]{3,2,1,0:T(8,128)S(1)} collective-permute-done((f32[1,1,48,256]{3,2,1,0:T(8,128)S(1)}, f32[1,1,48,256]{3,2,1,0:T(8,128)S(1)}, u32[]{:S(2)}, u32[]{:S(2)}) %collective-permute-start.17) | collective-permute-done | bytes 49184 | tf_op jit(solution)/shard_map/ppermute | solution.py:20
  144.7 3.8 %collective-permute-start.18 = (f32[3,1,48,256]{3,2,1,0:T(8,128)S(1)}, f32[3,1,48,256]{3,2,1,0:T(8,128)S(1)}, u32[]{:S(2)}, u32[]{:S(2)}) collective-permute-start(f32[3,1,48,256]{3,2,1,0:T(8,128)S(1)} %constant_dynamic-update-slice_fusion.34), channel_id=1, source_target_pairs={{0,1},{1,2},{2,3},{3,4},{4,5},{5,6},{6,7},{8,9},{9,10},{10,11},{11... | collective-permute-start | bytes 442376 | tf_op jit(solution)/shard_map/ppermute | solution.py:17
  148.4 1.5 collective-permute-start.19
  151.1 4.4 %collective-permute-done.19 = f32[3,1,48,256]{3,2,1,0:T(8,128)S(1)} collective-permute-done((f32[3,1,48,256]{3,2,1,0:T(8,128)S(1)}, f32[3,1,48,256]{3,2,1,0:T(8,128)S(1)}, u32[]{:S(2)}, u32[]{:S(2)}) %collective-permute-start.19) | collective-permute-done | bytes 147488 | tf_op jit(solution)/shard_map/ppermute | solution.py:20
  (313 shorter events, 66.8 us)
Async XLA Ops:
  2.4 13.6 %all-to-all-start = ((s32[8,1,1]{2,1,0:T(1,128)}), s32[8,1,1]{2,1,0:T(1,128)S(1)}, u32[]{:S(2)}, u32[]{:S(2)}) async-start(s32[8,1,1]{2,1,0:T(1,128)} %copy.106), calls=%async_computation | async-start | bytes 8192 | tf_op jit(solution)/shard_map/all_to_all | solution.py:125
  11.6 1.0 copy-start.6
  16.0 13.8 %all-to-all-start.1 = ((f32[8,2,16,256]{3,2,1,0:T(8,128)}), f32[8,2,16,256]{3,2,1,0:T(8,128)S(1)}, u32[]{:S(2)}, u32[]{:S(2)}) async-start(f32[8,2,16,256]{3,2,1,0:T(8,128)} %broadcast_select_fusion), calls=%async_computation.1 | async-start | bytes 524288 | tf_op jit(solution)/shard_map/all_to_all | solution.py:124
  31.9 5.5 %collective-permute-start = (f32[1,1,96,256]{3,2,1,0:T(8,128)S(1)}, f32[1,1,96,256]{3,2,1,0:T(8,128)S(1)}, u32[]{:S(2)}, u32[]{:S(2)}) collective-permute-start(f32[1,1,96,256]{3,2,1,0:T(8,128)S(1)} %maximum_bitcast_fusion), channel_id=1, source_target_pairs={{0,8},{8,16},{16,24},{1,9},{9,17},{17,25},{2,10},{10,18},{18,26},{... | collective-permute-start | bytes 294920 | tf_op jit(solution)/shard_map/ppermute | solution.py:17
  33.2 4.9 %collective-permute-start.1 = (f32[1,1,96,256]{3,2,1,0:T(8,128)S(1)}, f32[1,1,96,256]{3,2,1,0:T(8,128)S(1)}, u32[]{:S(2)}, u32[]{:S(2)}) collective-permute-start(f32[1,1,96,256]{3,2,1,0:T(8,128)S(1)} %maximum_bitcast_fusion), channel_id=1, source_target_pairs={{8,0},{16,8},{24,16},{9,1},{17,9},{25,17},{10,2},{18,10},{26,18},{... | collective-permute-start | bytes 294920 | tf_op jit(solution)/shard_map/ppermute | solution.py:20
  38.2 8.3 %collective-permute-start.2 = (f32[3,1,96,256]{3,2,1,0:T(8,128)S(1)}, f32[3,1,96,256]{3,2,1,0:T(8,128)S(1)}, u32[]{:S(2)}, u32[]{:S(2)}) collective-permute-start(f32[3,1,96,256]{3,2,1,0:T(8,128)S(1)} %pad_maximum_fusion), channel_id=1, source_target_pairs={{0,1},{1,2},{2,3},{3,4},{4,5},{5,6},{6,7},{8,9},{9,10},{10,11},{11... | collective-permute-start | bytes 884744 | tf_op jit(solution)/shard_map/ppermute | solution.py:17
  41.4 9.7 %collective-permute-start.3 = (f32[3,1,96,256]{3,2,1,0:T(8,128)S(1)}, f32[3,1,96,256]{3,2,1,0:T(8,128)S(1)}, u32[]{:S(2)}, u32[]{:S(2)}) collective-permute-start(f32[3,1,96,256]{3,2,1,0:T(8,128)S(1)} %pad_maximum_fusion), channel_id=1, source_target_pairs={{1,0},{2,1},{3,2},{4,3},{5,4},{6,5},{7,6},{9,8},{10,9},{11,10},{12... | collective-permute-start | bytes 884744 | tf_op jit(solution)/shard_map/ppermute | solution.py:20
  61.2 7.7 %collective-permute-start.4 = (f32[1,1,48,256]{3,2,1,0:T(8,128)S(1)}, f32[1,1,48,256]{3,2,1,0:T(8,128)S(1)}, u32[]{:S(2)}, u32[]{:S(2)}) collective-permute-start(f32[1,1,48,256]{3,2,1,0:T(8,128)S(1)} %broadcast_in_dim_reshape.12), channel_id=1, source_target_pairs={{0,8},{8,16},{16,24},{1,9},{9,17},{17,25},{2,10},{10,18},{18,26},{... | collective-permute-start | bytes 147464 | tf_op jit(solution)/shard_map/ppermute | solution.py:17
  67.2 4.2 %collective-permute-start.5 = (f32[1,1,48,256]{3,2,1,0:T(8,128)S(1)}, f32[1,1,48,256]{3,2,1,0:T(8,128)S(1)}, u32[]{:S(2)}, u32[]{:S(2)}) collective-permute-start(f32[1,1,48,256]{3,2,1,0:T(8,128)S(1)} %broadcast_in_dim_reshape.12), channel_id=1, source_target_pairs={{8,0},{16,8},{24,16},{9,1},{17,9},{25,17},{10,2},{18,10},{26,18},{... | collective-permute-start | bytes 147464 | tf_op jit(solution)/shard_map/ppermute | solution.py:20
  71.5 7.0 %collective-permute-start.6 = (f32[3,1,48,256]{3,2,1,0:T(8,128)S(1)}, f32[3,1,48,256]{3,2,1,0:T(8,128)S(1)}, u32[]{:S(2)}, u32[]{:S(2)}) collective-permute-start(f32[3,1,48,256]{3,2,1,0:T(8,128)S(1)} %constant_dynamic-update-slice_fusion.10), channel_id=1, source_target_pairs={{0,1},{1,2},{2,3},{3,4},{4,5},{5,6},{6,7},{8,9},{9,10},{10,11},{11... | collective-permute-start | bytes 442376 | tf_op jit(solution)/shard_map/ppermute | solution.py:17
  75.9 7.0 %collective-permute-start.7 = (f32[3,1,48,256]{3,2,1,0:T(8,128)S(1)}, f32[3,1,48,256]{3,2,1,0:T(8,128)S(1)}, u32[]{:S(2)}, u32[]{:S(2)}) collective-permute-start(f32[3,1,48,256]{3,2,1,0:T(8,128)S(1)} %constant_dynamic-update-slice_fusion.10), channel_id=1, source_target_pairs={{1,0},{2,1},{3,2},{4,3},{5,4},{6,5},{7,6},{9,8},{10,9},{11,10},{12... | collective-permute-start | bytes 442376 | tf_op jit(solution)/shard_map/ppermute | solution.py:20
  88.4 5.2 %collective-permute-start.8 = (f32[1,1,48,256]{3,2,1,0:T(8,128)S(1)}, f32[1,1,48,256]{3,2,1,0:T(8,128)S(1)}, u32[]{:S(2)}, u32[]{:S(2)}) collective-permute-start(f32[1,1,48,256]{3,2,1,0:T(8,128)S(1)} %broadcast_in_dim_reshape.13), channel_id=1, source_target_pairs={{0,8},{8,16},{16,24},{1,9},{9,17},{17,25},{2,10},{10,18},{18,26},{... | collective-permute-start | bytes 147464 | tf_op jit(solution)/shard_map/ppermute | solution.py:17
  92.0 3.8 %collective-permute-start.9 = (f32[1,1,48,256]{3,2,1,0:T(8,128)S(1)}, f32[1,1,48,256]{3,2,1,0:T(8,128)S(1)}, u32[]{:S(2)}, u32[]{:S(2)}) collective-permute-start(f32[1,1,48,256]{3,2,1,0:T(8,128)S(1)} %broadcast_in_dim_reshape.13), channel_id=1, source_target_pairs={{8,0},{16,8},{24,16},{9,1},{17,9},{25,17},{10,2},{18,10},{26,18},{... | collective-permute-start | bytes 147464 | tf_op jit(solution)/shard_map/ppermute | solution.py:20
  95.8 7.4 %collective-permute-start.10 = (f32[3,1,48,256]{3,2,1,0:T(8,128)S(1)}, f32[3,1,48,256]{3,2,1,0:T(8,128)S(1)}, u32[]{:S(2)}, u32[]{:S(2)}) collective-permute-start(f32[3,1,48,256]{3,2,1,0:T(8,128)S(1)} %constant_dynamic-update-slice_fusion.18), channel_id=1, source_target_pairs={{0,1},{1,2},{2,3},{3,4},{4,5},{5,6},{6,7},{8,9},{9,10},{10,11},{11... | collective-permute-start | bytes 442376 | tf_op jit(solution)/shard_map/ppermute | solution.py:17
  100.5 7.0 %collective-permute-start.11 = (f32[3,1,48,256]{3,2,1,0:T(8,128)S(1)}, f32[3,1,48,256]{3,2,1,0:T(8,128)S(1)}, u32[]{:S(2)}, u32[]{:S(2)}) collective-permute-start(f32[3,1,48,256]{3,2,1,0:T(8,128)S(1)} %constant_dynamic-update-slice_fusion.18), channel_id=1, source_target_pairs={{1,0},{2,1},{3,2},{4,3},{5,4},{6,5},{7,6},{9,8},{10,9},{11,10},{12... | collective-permute-start | bytes 442376 | tf_op jit(solution)/shard_map/ppermute | solution.py:20
  114.6 5.0 %collective-permute-start.12 = (f32[1,1,48,256]{3,2,1,0:T(8,128)S(1)}, f32[1,1,48,256]{3,2,1,0:T(8,128)S(1)}, u32[]{:S(2)}, u32[]{:S(2)}) collective-permute-start(f32[1,1,48,256]{3,2,1,0:T(8,128)S(1)} %broadcast_in_dim_reshape.14), channel_id=1, source_target_pairs={{0,8},{8,16},{16,24},{1,9},{9,17},{17,25},{2,10},{10,18},{18,26},{... | collective-permute-start | bytes 147464 | tf_op jit(solution)/shard_map/ppermute | solution.py:17
  117.9 4.0 %collective-permute-start.13 = (f32[1,1,48,256]{3,2,1,0:T(8,128)S(1)}, f32[1,1,48,256]{3,2,1,0:T(8,128)S(1)}, u32[]{:S(2)}, u32[]{:S(2)}) collective-permute-start(f32[1,1,48,256]{3,2,1,0:T(8,128)S(1)} %broadcast_in_dim_reshape.14), channel_id=1, source_target_pairs={{8,0},{16,8},{24,16},{9,1},{17,9},{25,17},{10,2},{18,10},{26,18},{... | collective-permute-start | bytes 147464 | tf_op jit(solution)/shard_map/ppermute | solution.py:20
  121.9 5.6 %collective-permute-start.14 = (f32[3,1,48,256]{3,2,1,0:T(8,128)S(1)}, f32[3,1,48,256]{3,2,1,0:T(8,128)S(1)}, u32[]{:S(2)}, u32[]{:S(2)}) collective-permute-start(f32[3,1,48,256]{3,2,1,0:T(8,128)S(1)} %constant_dynamic-update-slice_fusion.26), channel_id=1, source_target_pairs={{0,1},{1,2},{2,3},{3,4},{4,5},{5,6},{6,7},{8,9},{9,10},{10,11},{11... | collective-permute-start | bytes 442376 | tf_op jit(solution)/shard_map/ppermute | solution.py:17
  124.8 7.0 %collective-permute-start.15 = (f32[3,1,48,256]{3,2,1,0:T(8,128)S(1)}, f32[3,1,48,256]{3,2,1,0:T(8,128)S(1)}, u32[]{:S(2)}, u32[]{:S(2)}) collective-permute-start(f32[3,1,48,256]{3,2,1,0:T(8,128)S(1)} %constant_dynamic-update-slice_fusion.26), channel_id=1, source_target_pairs={{1,0},{2,1},{3,2},{4,3},{5,4},{6,5},{7,6},{9,8},{10,9},{11,10},{12... | collective-permute-start | bytes 442376 | tf_op jit(solution)/shard_map/ppermute | solution.py:20
  136.1 22.1 %copy-start = (f32[8,16,256]{2,1,0:T(8,128)}, f32[8,16,256]{2,1,0:T(8,128)S(1)}, u32[]{:S(2)}) copy-start(f32[8,16,256]{2,1,0:T(8,128)S(1)} %fusion.37) | copy-start | bytes 393220
  137.4 5.0 %collective-permute-start.16 = (f32[1,1,48,256]{3,2,1,0:T(8,128)S(1)}, f32[1,1,48,256]{3,2,1,0:T(8,128)S(1)}, u32[]{:S(2)}, u32[]{:S(2)}) collective-permute-start(f32[1,1,48,256]{3,2,1,0:T(8,128)S(1)} %broadcast_in_dim_reshape.15), channel_id=1, source_target_pairs={{0,8},{8,16},{16,24},{1,9},{9,17},{17,25},{2,10},{10,18},{18,26},{... | collective-permute-start | bytes 147464 | tf_op jit(solution)/shard_map/ppermute | solution.py:17
  140.7 4.0 %collective-permute-start.17 = (f32[1,1,48,256]{3,2,1,0:T(8,128)S(1)}, f32[1,1,48,256]{3,2,1,0:T(8,128)S(1)}, u32[]{:S(2)}, u32[]{:S(2)}) collective-permute-start(f32[1,1,48,256]{3,2,1,0:T(8,128)S(1)} %broadcast_in_dim_reshape.15), channel_id=1, source_target_pairs={{8,0},{16,8},{24,16},{9,1},{17,9},{25,17},{10,2},{18,10},{26,18},{... | collective-permute-start | bytes 147464 | tf_op jit(solution)/shard_map/ppermute | solution.py:20
  144.7 6.4 %collective-permute-start.18 = (f32[3,1,48,256]{3,2,1,0:T(8,128)S(1)}, f32[3,1,48,256]{3,2,1,0:T(8,128)S(1)}, u32[]{:S(2)}, u32[]{:S(2)}) collective-permute-start(f32[3,1,48,256]{3,2,1,0:T(8,128)S(1)} %constant_dynamic-update-slice_fusion.34), channel_id=1, source_target_pairs={{0,1},{1,2},{2,3},{3,4},{4,5},{5,6},{6,7},{8,9},{9,10},{10,11},{11... | collective-permute-start | bytes 442376 | tf_op jit(solution)/shard_map/ppermute | solution.py:17
  148.4 7.0 %collective-permute-start.19 = (f32[3,1,48,256]{3,2,1,0:T(8,128)S(1)}, f32[3,1,48,256]{3,2,1,0:T(8,128)S(1)}, u32[]{:S(2)}, u32[]{:S(2)}) collective-permute-start(f32[3,1,48,256]{3,2,1,0:T(8,128)S(1)} %constant_dynamic-update-slice_fusion.34), channel_id=1, source_target_pairs={{1,0},{2,1},{3,2},{4,3},{5,4},{6,5},{7,6},{9,8},{10,9},{11,10},{12... | collective-permute-start | bytes 442376 | tf_op jit(solution)/shard_map/ppermute | solution.py:20
  (28 other events, 20.9 us)
where the time goes:
time: 163 us; the launch traced here: 161 us
  starting transfers between devices  62.4 us (38%)
  waiting for transfers between devices  47.2 us (29%)
  local copies, waits for them, and re-layouts  42.9 us (26%)
  other arithmetic  5.92 us (4%)
  between operations  2.11 us (1%)
    ppermute x10, starting transfers between devices, with_halo(): lax.ppermute(lax.slice_in_dim(block, block.shape[dim] - width, None, axis...  36.5 us
    ppermute x10, waiting for transfers between devices, with_halo(): lax.ppermute(lax.slice_in_dim(block, 0, width, axis=dim), axis, backward)  32.2 us
    ppermute x10, starting transfers between devices, with_halo(): lax.ppermute(lax.slice_in_dim(block, 0, width, axis=dim), axis, backward)  13.3 us
    ppermute x10, waiting for transfers between devices, with_halo(): lax.ppermute(lax.slice_in_dim(block, block.shape[dim] - width, None, axis...  8.59 us
    all_to_all x1, starting transfers between devices, body(): lax.all_to_all(labels, 'lane', split_axis=0, concat_axis=0, tiled=True)  7.25 us
    unnamed x89, local copies, waits for them, and re-layouts  6.55 us
    all_to_all x1, waiting for transfers between devices, body(): lax.all_to_all(parcels, 'lane', split_axis=0, concat_axis=0, tiled=True)  5.71 us
    all_to_all x1, starting transfers between devices, body(): lax.all_to_all(parcels, 'lane', split_axis=0, concat_axis=0, tiled=True)  5.31 us
  transfers between devices with their start and end apart: 22, of which 17 were waited for; matrix products, arithmetic and copies ran while one was open for 7% of the time, Pallas kernels for 0%

commit v1 on v0

--- a/solution.py
+++ b/solution.py
@@ -1,6 +1,8 @@
 import jax
 import jax.numpy as jnp
 from jax import lax
+from jax.experimental import pallas as pl
+from jax.experimental.pallas import tpu as pltpu
 from jax.sharding import PartitionSpec as P
 
 SWEEPS = 2
@@ -103,7 +105,7 @@
     return settled.at[jnp.where(tags > 0, tags - 1, count)].set(arrived, mode="drop")
 
 
-def body(old_field, old_source, diffusivity, target_box, neighbours):
+def general_body(old_field, old_source, diffusivity, target_box, neighbours):
     count, side, plane = old_field.shape
     lane_count = lax.axis_size("lane")
     lane_here = lax.axis_index("lane")
@@ -184,6 +186,525 @@
     return (field, coarse)
 
 
+BXD = 2
+BZB = 4
+PAD = 8
+LOW, HIGH = "low", "high"
+
+
+def lane_plan(lanes):
+    half = lanes // 2
+    moves = [1, lanes - 1, 2, lanes - 2, half]
+    singles = {}
+
+    def add(offset, move, part):
+        if offset % lanes:
+            singles.setdefault(offset % lanes, []).append((move, part))
+
+    for move in moves:
+        add(move, move, LOW)
+        add(move, move, HIGH)
+        add(move + 1, move, HIGH)
+        add(move - 1, move, LOW)
+    bulk = {1: HIGH, lanes - 1: LOW}
+    plan = {}
+    for offset in sorted(singles):
+        kept = [item for item in singles[offset] if not (item[0] == offset and item[1] == bulk.get(offset))]
+        plan[offset] = (bulk.get(offset), kept)
+    return moves, plan
+
+
+def part_lanes(part, plane):
+    return slice(0, plane // 2) if part == LOW else slice(plane // 2, plane)
+
+
+def pack_kernel(moves, plan, lanes, count, *refs):
+    me, target, near, field, source, beta = refs[:6]
+    outs = refs[6 : 6 + len(plan)]
+    labels, table, sems = refs[6 + len(plan) :]
+    side, plane = field.shape[1:]
+    half = plane // 2
+    copies = []
+
+    def send(src, dst):
+        copy = pltpu.make_async_copy(src, dst, sems.at[len(copies)])
+        copy.start()
+        copies.append(copy)
+
+    for out, (bulk, kept) in zip(outs, plan.values()):
+        if bulk is not None:
+            for at, array in enumerate((field, source, beta)):
+                send(array.at[:, :, part_lanes(bulk, plane)], out.at[at * count : (at + 1) * count])
+    lane, own = me[1], me[2]
+    first = own * count
+    old_index = [jnp.int32(0)] * len(moves)
+    new_slot = [jnp.int32(-1)] * len(moves)
+    stay = []
+    for i in range(count):
+        there = target[i]
+        slot = lax.rem(there, count)
+        step = lax.rem(lax.rem(lax.div(there, count), lanes) - lane + lanes, lanes)
+        stay.append(jnp.where(step == 0, slot, -1))
+        for k, move in enumerate(moves):
+            old_index[k] = jnp.where(step == move, i, old_index[k])
+            new_slot[k] = jnp.where(step == move, slot, new_slot[k])
+    for out, (bulk, kept) in zip(outs, plan.values()):
+        unit = 3 * count if bulk is not None else 0
+        for move, part in kept:
+            box = old_index[moves.index(move)]
+            for array in (field, source):
+                send(array.at[box, :, part_lanes(part, plane)], out.at[unit])
+                unit += 1
+    for i in range(count):
+        labels[1, i] = -1
+
+    def local(index, face):
+        there = near[index, face]
+        inside = (there >= first) & (there < first + count)
+        return inside, jnp.clip(there - first, 0, count - 1)
+
+    place = []
+    for i in range(count):
+        inside, below = local(i, 0)
+        depth = jnp.int32(0)
+        live, at = local(i, 4)
+        for _ in range(BZB - 1):
+            depth = depth + jnp.where(live, 1, 0)
+            further, onward = local(at, 4)
+            live, at = live & further, onward
+        spot = jnp.where(inside, BZB, 0) + depth
+        place.append(spot)
+        labels[0, i] = spot
+        labels[1, spot] = i
+        labels[3, i] = stay[i]
+    for k in range(len(moves)):
+        labels[2, k] = new_slot[k]
+        labels[4, k] = old_index[k]
+    rows = lax.broadcasted_iota(jnp.int32, (8, 128), 0)
+    cols = lax.broadcasted_iota(jnp.int32, (8, 128), 1)
+    spots = rows * 128 + cols
+    held = jnp.zeros((8, 128), jnp.int32)
+
+    def put(held, row, col, value):
+        return jnp.where(spots == row * 128 + col, value, held)
+
+    for i in range(count):
+        slot = labels[1, i]
+        held = put(held, i, 0, jnp.where(slot < 0, -7, first + slot))
+        for face in range(6):
+            held = put(held, i, 1 + face, near[jnp.maximum(slot, 0), face])
+        held = put(held, i, 7, place[i])
+        held = put(held, i, 9, stay[i])
+    for k in range(len(moves)):
+        held = put(held, k, 8, new_slot[k])
+        held = put(held, k, 10, old_index[k])
+    table[...] = held.astype(jnp.float32)
+    for out in outs:
+        send(table, out.at[out.shape[0] - 1, 0:8])
+    for copy in copies:
+        copy.wait()
+
+
+def assemble_kernel(moves, plan, lanes, count, *refs):
+    labels, own_table, field, source, beta = refs[:5]
+    got = dict(zip(plan, refs[5 : 5 + len(plan)]))
+    block, upward, downward, row_table, tables, seen, sem, table_sems, seen_sems = refs[5 + len(plan) :]
+    side, plane = field.shape[1:]
+    half = plane // 2
+    order = list(plan)
+    fetch = []
+    for k, offset in enumerate(order):
+        fetch.append(pltpu.make_async_copy(got[offset].at[got[offset].shape[0] - 1, 0:8], tables.at[k], table_sems.at[k]))
+    shown = {0: None, 1: 1, lanes - 1: lanes - 1}
+    if lanes == 8:
+        shown = {offset: offset for offset in range(8) if offset == 0 or offset in got}
+    for offset in shown:
+        if offset:
+            at = offset % 8 if offset < lanes - 1 else 7
+            fetch.append(pltpu.make_async_copy(got[offset].at[got[offset].shape[0] - 1, 0:8], seen.at[at], seen_sems.at[at]))
+    for copy in fetch:
+        copy.start()
+
+    def spot(place):
+        return lax.rem(place, BZB), pl.ds(pl.multiple_of(lax.div(place, BZB) * side, side), side)
+
+    def copy(src, array, place, where):
+        deep, rows = spot(place)
+        pltpu.make_async_copy(src, block.at[array, deep, rows, where], sem).start()
+
+    own_half = {LOW: slice(half, 2 * half), HIGH: slice(2 * half, 3 * half)}
+    low_halo, high_halo = slice(0, half), slice(3 * half, 4 * half)
+    whole = slice(half, 3 * half)
+    old = (field, source)
+    for i in range(count):
+        copy(beta.at[i], 2, labels[0, i], whole)
+
+        @pl.when(labels[3, i] >= 0)
+        def _():
+            for a in range(2):
+                copy(old[a].at[i], a, labels[0, labels[3, i]], whole)
+
+    for k in range(len(order)):
+        fetch[k].wait()
+
+    def said(offset, row, col):
+        return tables[order.index(offset), row, col].astype(jnp.int32)
+
+    below, above = 1, lanes - 1
+
+    def place_below(slot):
+        return said(below, slot, 7)
+
+    def place_above(slot):
+        return said(above, slot, 7)
+
+    for move, part, halo, place in ((1, LOW, high_halo, place_above), (lanes - 1, HIGH, low_halo, place_below)):
+        k = moves.index(move)
+
+        @pl.when(labels[2, k] >= 0)
+        def _():
+            for a in range(2):
+                copy(old[a].at[labels[4, k], :, part_lanes(part, plane)], a, place(labels[2, k]), halo)
+
+    for offset, (bulk, kept) in plan.items():
+        message = got[offset]
+        unit = 0
+        if bulk is not None:
+            halo = low_halo if offset == below else high_halo
+            for i in range(count):
+                copy(message.at[2 * count + i], 2, said(offset, i, 7), halo)
+
+                @pl.when(said(offset, i, 9) >= 0)
+                def _():
+                    for a in range(2):
+                        copy(message.at[a * count + i], a, said(offset, said(offset, i, 9), 7), halo)
+
+            k = moves.index(offset)
+
+            @pl.when(said(offset, k, 8) >= 0)
+            def _():
+                for a in range(2):
+                    copy(message.at[a * count + said(offset, k, 10)], a, labels[0, said(offset, k, 8)], own_half[bulk])
+
+            unit = 3 * count
+        for move, part in kept:
+            k = moves.index(move)
+            apart = (move - offset) % lanes
+
+            @pl.when(said(offset, k, 8) >= 0)
+            def _():
+                slot = said(offset, k, 8)
+                if apart == 0:
+                    place, where = labels[0, slot], own_half[part]
+                elif apart == 1:
+                    place, where = place_above(slot), high_halo
+                else:
+                    place, where = place_below(slot), low_halo
+                for a in range(2):
+                    copy(message.at[unit + a], a, place, where)
+
+            unit += 2
+    cols = lax.broadcasted_iota(jnp.int32, (8, 128), 1)
+    for copy_in in fetch[len(order) :]:
+        copy_in.wait()
+    joined = jnp.where(cols < 8, own_table[...], 0.0)
+    for offset in shown:
+        if offset:
+            at = offset if offset < 7 else 7
+            joined = joined + pltpu.roll(jnp.where(cols < 8, seen[at], 0.0), 8 * at, 1)
+    joined = joined + pltpu.roll(joined, 64, 1)
+    row_table[...] = joined
+    upward[upward.shape[0] - 1] = joined
+    downward[downward.shape[0] - 1] = joined
+    pltpu.make_async_copy(block, block, sem).wait()
+    width = block.shape[3]
+    levels = lax.broadcasted_iota(jnp.int32, (8, width), 0)
+    last = block.shape[2] - 8
+    for deep in range(BZB):
+        a, b, c = (block[k, deep, last : last + 8] for k in range(3))
+        up_first = jnp.where(levels < 3, pltpu.roll(b, 3, 0), a)
+        up_second = jnp.where(levels == 0, pltpu.roll(b, 4, 0), c)
+        a, b, c = (block[k, deep, 0:8] for k in range(3))
+        down_first = jnp.where(levels >= 5, pltpu.roll(b, 5, 0), a)
+        down_second = jnp.where(levels == 7, pltpu.roll(b, 4, 0), c)
+        for k in range(width // 128):
+            cut = slice(k * 128, (k + 1) * 128)
+            at = deep * 2 * (width // 128) + k
+            upward[at] = up_first[:, cut]
+            upward[at + width // 128] = up_second[:, cut]
+            downward[at] = down_first[:, cut]
+            downward[at + width // 128] = down_second[:, cut]
+
+
+def smooth_kernel(lanes, nodes, covered, me, labels, block, from_below, from_above, row_table, two_on, smoothed, coarse, flag,
+                  f, s, b, xl, xu, yl, yu, zl, zu, total, inverse, rest):
+    width = block.shape[3]
+    own_rows = block.shape[2]
+    side = smoothed.shape[1]
+    plane = smoothed.shape[2]
+    half = plane // 2
+    tiles = width // 128
+    node, lane = me[0], me[1]
+    first_node, last_node = node == 0, node == nodes - 1
+    first_lane, last_lane = lane == 0, lane == lanes - 1
+    top = 2 * PAD + own_rows
+    rows8 = lax.broadcasted_iota(jnp.int32, (8, width), 0)
+    cols = lax.broadcasted_iota(jnp.int32, (8, width), 1)
+    depth = lax.rem(cols, side)
+    at_front, at_back = depth == 0, depth == side - 1
+    colour = lax.rem(rows8 + lax.div(cols, side) + depth, 2)
+
+    zero, one = jnp.zeros((8, width), jnp.float32), jnp.ones((8, width), jnp.float32)
+    for deep in range(BZB):
+        for rows in (slice(0, 8), slice(top + 8, top + 16)):
+            f[deep, rows] = zero
+            b[deep, rows] = one
+            xu[deep, rows] = zero
+        f[deep, 2 * PAD : top] = block[0, deep]
+        b[deep, 2 * PAD : top] = block[2, deep]
+        s[deep, 2 * PAD : top] = block[1, deep]
+        for message, start, below in ((from_below, PAD, True), (from_above, top, False)):
+            base = deep * 2 * tiles
+            first = jnp.concatenate([message[base + k] for k in range(tiles)], axis=1)
+            second = jnp.concatenate([message[base + tiles + k] for k in range(tiles)], axis=1)
+            if below:
+                src = jnp.where(rows8 >= 5, pltpu.roll(first, 5, 0), pltpu.roll(second, 4, 0))
+            else:
+                src = jnp.where(rows8 < 3, pltpu.roll(first, 3, 0), pltpu.roll(second, 4, 0))
+            f[deep, start : start + 8] = first
+            b[deep, start : start + 8] = jnp.where(rows8 == (0 if below else 7), 1.0, second)
+            s[deep, start : start + 8] = src
+
+    def after(values):
+        return pltpu.roll(values, width - side, 1)
+
+    def before(values):
+        return pltpu.roll(values, side, 1)
+
+    def beyond_z(values, afters):
+        out = []
+        for deep in range(BZB):
+            joined = values[deep] if deep == 0 else jnp.where(at_back, afters[deep - 1], values[deep])
+            out.append(pltpu.roll(joined, 1, 1))
+        return out
+
+    def ahead_z(values, befores):
+        out = []
+        for deep in range(BZB):
+            joined = values[deep] if deep == BZB - 1 else jnp.where(at_front, befores[deep + 1], values[deep])
+            out.append(pltpu.roll(joined, width - 1, 1))
+        return out
+
+    def mean(one_side, other):
+        return 2.0 * one_side * other / (one_side + other)
+
+    starts = range(PAD, top + 8, 8)
+    low_edge = (cols >= half) & (cols < half + side) & first_lane
+    high_edge = (cols >= 3 * half - side) & (cols < 3 * half) & last_lane
+    no_link = ((cols >= half - side) & (cols < half) & first_lane) | high_edge
+    for r in starts:
+        held = [b[deep, r : r + 8] for deep in range(BZB)]
+        befores = [before(v) for v in held]
+        afters = [after(v) for v in held]
+        aheads = ahead_z(held, befores)
+        ky = [jnp.where(no_link, 0.0, mean(held[d], afters[d])) for d in range(BZB)]
+        kz = [mean(held[d], aheads[d]) for d in range(BZB)]
+        kz[BZB - 1] = jnp.where(at_back, 0.0, kz[BZB - 1])
+        kzl = beyond_z(kz, [after(v) for v in kz])
+        kzl[0] = jnp.where(at_front, 0.0, kzl[0])
+        for d in range(BZB):
+            kx = mean(held[d], b[d, r + 1 : r + 9])
+            if r == PAD:
+                kx = jnp.where((rows8 == 7) & first_node, 0.0, kx)
+            if r == top - 8:
+                kx = jnp.where((rows8 == 7) & last_node, 0.0, kx)
+            xu[d, r : r + 8] = kx
+            yu[d, r : r + 8] = ky[d]
+            yl[d, r : r + 8] = before(ky[d])
+            zu[d, r : r + 8] = kz[d]
+            zl[d, r : r + 8] = kzl[d]
+    for r in starts:
+        for d in range(BZB):
+            here = slice(r, r + 8)
+            kxl = xu[d, r - 1 : r + 7]
+            xl[d, here] = kxl
+            held = b[d, here]
+            whole = kxl + xu[d, here] + yl[d, here] + yu[d, here] + zl[d, here] + zu[d, here]
+            whole = whole + jnp.where(low_edge, held, 0.0) + jnp.where(high_edge, held, 0.0)
+            if d == 0:
+                whole = whole + jnp.where(at_front, held, 0.0)
+            if d == BZB - 1:
+                whole = whole + jnp.where(at_back, held, 0.0)
+            if r == 2 * PAD:
+                whole = whole + jnp.where((rows8 == 0) & first_node, held, 0.0)
+            if r == top - 8:
+                whole = whole + jnp.where((rows8 == 7) & last_node, held, 0.0)
+            if 2 * PAD <= r < top:
+                total[d, r - 2 * PAD : r - 2 * PAD + 8] = whole
+            inverse[d, here] = 1.0 / whole
+
+    def sums(r, held, afters, befores):
+        behind = beyond_z(held, afters)
+        aheads = ahead_z(held, befores)
+        here = slice(r, r + 8)
+        out = []
+        for d in range(BZB):
+            part = s[d, here] + xl[d, here] * f[d, r - 1 : r + 7] + xu[d, here] * f[d, r + 1 : r + 9]
+            part = part + (yl[d, here] * befores[d] + yu[d, here] * afters[d])
+            out.append(part + (zl[d, here] * behind[d] + zu[d, here] * aheads[d]))
+        return out
+
+    for sweep in range(SWEEPS):
+        for colour_id in (0, 1):
+            chosen = colour == colour_id
+            for r in starts:
+                held = [f[d, r : r + 8] for d in range(BZB)]
+                parts = sums(r, held, [after(v) for v in held], [before(v) for v in held])
+                for d in range(BZB):
+                    f[d, r : r + 8] = jnp.where(chosen, parts[d] * inverse[d, r : r + 8], held[d])
+
+    for r in range(2 * PAD, top, 8):
+        held = [f[d, r : r + 8] for d in range(BZB)]
+        parts = sums(r, held, [after(v) for v in held], [before(v) for v in held])
+        wide, inner = divmod(r - 2 * PAD, side)
+        for d in range(BZB):
+            left = parts[d] - total[d, r - 2 * PAD : r - 2 * PAD + 8] * held[d]
+            slot = jnp.maximum(labels[1, wide * BZB + d], 0)
+            smoothed[slot, inner : inner + 8] = held[d][:, half : 3 * half]
+            for k in range(plane // 128):
+                cut = slice(half + k * 128, half + (k + 1) * 128)
+                rest[k, pl.ds(pl.multiple_of(slot * side + inner, 8), 8), :] = left[:, cut]
+
+    count = smoothed.shape[0]
+    small = side // 2
+    cells = lax.broadcasted_iota(jnp.int32, (plane, 128), 0)
+    slots = lax.broadcasted_iota(jnp.int32, (plane, 128), 1)
+    goal = lax.div(lax.div(cells, side), 2) * small + lax.div(lax.rem(cells, side), 2)
+    per = small * small
+    for pair in range(small * per // 128):
+        acc = None
+        for inner in range(128 // per):
+            i = pair * (128 // per) + inner
+            even = [rest[k, pl.ds(2 * i, count, stride=side), :] for k in range(plane // 128)]
+            odd = [rest[k, pl.ds(2 * i + 1, count, stride=side), :] for k in range(plane // 128)]
+            rows = jnp.concatenate(even, axis=1) + jnp.concatenate(odd, axis=1)
+            pooling = (goal + inner * per == slots).astype(jnp.float32)
+            term = jnp.dot(rows, pooling, precision=lax.Precision.HIGHEST, preferred_element_type=jnp.float32)
+            acc = term if acc is None else acc + term
+        coarse[:, pair * 128 : (pair + 1) * 128] = 0.125 * acc
+
+    mine = from_below.shape[0] - 1
+    rows1 = lax.broadcasted_iota(jnp.int32, (8, 128), 0)
+    cols1 = lax.broadcasted_iota(jnp.int32, (8, 128), 1)
+    owner = lax.rem(lax.div(cols1, 8), 8)
+    field_of = lax.rem(cols1, 8)
+    own, opposite = row_table[...], two_on[...]
+    lower, upper = from_below[mine], from_above[mine]
+    rows_of = [(own, lower, upper, node), (lower, opposite, own, lax.rem(node + nodes - 1, nodes)),
+               (upper, own, opposite, lax.rem(node + 1, nodes)), (opposite, upper, lower, lax.rem(node + 2, nodes))]
+    if not covered:
+        rows_of = rows_of[:1]
+    lane_of = lax.rem(lane - jnp.where(owner > 4, owner - 8, owner) + 2 * lanes, lanes)
+    wrong = jnp.zeros((8, 128), jnp.float32)
+    for table, low, high, at_node in rows_of:
+        turned = pltpu.roll(table, 4, 0)
+        at_low = jnp.where(rows1 >= 4, turned, jnp.where(at_node == 0, -1.0, pltpu.roll(low, 4, 0)))
+        at_high = jnp.where(rows1 < 4, turned, jnp.where(at_node == nodes - 1, -1.0, pltpu.roll(high, 4, 0)))
+        y_low = jnp.where(lane_of == 0, -1.0, pltpu.roll(table, 128 - 8, 1))
+        y_high = jnp.where(lane_of == lanes - 1, -1.0, pltpu.roll(table, 8, 1))
+        z_low = jnp.where(lax.rem(rows1, BZB) == 0, -1.0, pltpu.roll(table, 1, 0))
+        z_high = jnp.where(lax.rem(rows1, BZB) == BZB - 1, -1.0, pltpu.roll(table, 7, 0))
+        bad = jnp.where((field_of == 0) & (table < 0), 1.0, 0.0)
+        for face, expected in enumerate((at_low, at_high, y_low, y_high, z_low, z_high)):
+            differs = table != pltpu.roll(expected, 1 + face, 1)
+            bad = bad + jnp.where((field_of == 1 + face) & differs, 1.0, 0.0)
+        if not covered:
+            bad = jnp.where(owner == 0, bad, 0.0)
+        wrong = wrong + bad
+    flag[0, 0] = (jnp.sum(wrong) > 0).astype(jnp.int32)
+
+
+ANY = pl.BlockSpec(memory_space=pl.ANY)
+SCALARS = pl.BlockSpec(memory_space=pltpu.SMEM)
+VECTORS = pl.BlockSpec(memory_space=pltpu.VMEM)
+
+
+def fast_body(old_field, old_source, diffusivity, target_box, neighbours):
+    count, side, plane = old_field.shape
+    half = plane // 2
+    lanes, nodes = lax.axis_size("lane"), lax.axis_size("node")
+    lane, node = lax.axis_index("lane"), lax.axis_index("node")
+    me = jnp.stack([node, lane, node * lanes + lane]).astype(jnp.int32)
+    moves, plan = lane_plan(lanes)
+    covered = lanes == 8 and nodes == 4
+    units = [(3 * count if bulk is not None else 0) + 2 * len(kept) + 1 for bulk, kept in plan.values()]
+    sent = sum(units)
+    f32 = jnp.float32
+    packed = pl.pallas_call(
+        lambda *refs: pack_kernel(moves, plan, lanes, count, *refs),
+        name="pack_moves",
+        out_shape=[jax.ShapeDtypeStruct((n, side, half), f32) for n in units]
+        + [jax.ShapeDtypeStruct((5, count), jnp.int32), jax.ShapeDtypeStruct((8, 128), f32)],
+        in_specs=[SCALARS] * 3 + [ANY] * 3,
+        out_specs=[ANY] * len(units) + [SCALARS, VECTORS],
+        scratch_shapes=[pltpu.SemaphoreType.DMA((sent,))],
+    )(me, target_box, neighbours, old_field, old_source, diffusivity)
+    messages, labels, own_table = packed[:-2], packed[-2], packed[-1]
+    got = [
+        lax.ppermute(message, "lane", [(i, (i + offset) % lanes) for i in range(lanes)])
+        for offset, message in zip(plan, messages)
+    ]
+    width = 4 * half
+    strips = BZB * 2 * (width // 128) + 1
+    block, upward, downward, row_table = pl.pallas_call(
+        lambda *refs: assemble_kernel(moves, plan, lanes, count, *refs),
+        name="assemble_block",
+        out_shape=[
+            jax.ShapeDtypeStruct((3, BZB, BXD * side, width), f32),
+            jax.ShapeDtypeStruct((strips, 8, 128), f32),
+            jax.ShapeDtypeStruct((strips, 8, 128), f32),
+            jax.ShapeDtypeStruct((8, 128), f32),
+        ],
+        in_specs=[SCALARS, VECTORS] + [ANY] * (3 + len(units)),
+        out_specs=[VECTORS] * 4,
+        scratch_shapes=[
+            pltpu.SMEM((len(units), 8, 128), f32),
+            pltpu.VMEM((8, 8, 128), f32),
+            pltpu.SemaphoreType.DMA,
+            pltpu.SemaphoreType.DMA((len(units),)),
+            pltpu.SemaphoreType.DMA((8,)),
+        ],
+    )(labels, own_table, old_field, old_source, diffusivity, *got)
+    from_below = lax.ppermute(upward, "node", [(i, (i + 1) % nodes) for i in range(nodes)])
+    from_above = lax.ppermute(downward, "node", [(i, (i - 1) % nodes) for i in range(nodes)])
+    two_on = lax.ppermute(row_table, "node", [(i, (i + 2) % nodes) for i in range(nodes)])
+    tall = BXD * side + 4 * PAD
+    big = pltpu.VMEM((BZB, tall, width), f32)
+    smoothed, coarse, flag = pl.pallas_call(
+        lambda *refs: smooth_kernel(lanes, nodes, covered, *refs),
+        name="smooth_block",
+        out_shape=[
+            jax.ShapeDtypeStruct((count, side, plane), f32),
+            jax.ShapeDtypeStruct((count, (side // 2) ** 3), f32),
+            jax.ShapeDtypeStruct((1, 1), jnp.int32),
+        ],
+        in_specs=[SCALARS] * 2 + [VECTORS] * 5,
+        out_specs=[VECTORS, VECTORS, SCALARS],
+        scratch_shapes=[big] * 9 + [pltpu.VMEM((BZB, BXD * side, width), f32), big, pltpu.VMEM((plane // 128, count * side, 128), f32)],
+        compiler_params=pltpu.CompilerParams(vmem_limit_bytes=48 * 2**20),
+    )(me, labels, block, from_below, from_above, row_table, two_on)
+    irregular = flag[0, 0]
+    if not covered:
+        irregular = lax.pmax(irregular, ("node", "lane"))
+
+    def again(carry):
+        out = general_body(old_field, old_source, diffusivity, target_box, neighbours)
+        return (*out, jnp.int32(0))
+
+    smoothed, coarse, _ = lax.while_loop(lambda carry: carry[2] > 0, again, (smoothed, coarse, irregular))
+    return smoothed, coarse
+
+
 def solution(mesh):
     in_specs = (
         P(("node", "lane"), None, None),
@@ -193,4 +714,4 @@
         P(("node", "lane"), None),
     )
     out_specs = (P(("node", "lane"), None, None), P(("node", "lane"), None))
-    return jax.shard_map(body, mesh=mesh, in_specs=in_specs, out_specs=out_specs, check_vma=False)
+    return jax.shard_map(fast_body, mesh=mesh, in_specs=in_specs, out_specs=out_specs, check_vma=False)

time: 163 us -> 68.4 us (0.42); the launches traced: 161 us -> 68 us
  starting transfers between devices: 62.4 us -> 15.2 us
  local copies, waits for them, and re-layouts: 42.9 us -> 2.69 us
  Pallas kernels: 0 us -> 33.7 us
  waiting for transfers between devices: 47.2 us -> 14 us
  other arithmetic: 5.92 us -> 0.58 us
    ppermute x20 -> x10, starting transfers between devices: 49.8 us -> 15.2 us  [the longest x7 11.8 us: fast_body(): lax.ppermute(message, 'lane', [(i, (i + offset) % lanes) for i in range(l...]
    pallas_call x0 -> x3, Pallas kernels: none -> 33.7 us  [the longest x1 23.2 us: fast_body(): pl.pallas_call(lambda *refs: pack_kernel(moves, plan, lanes, count, *refs...]
    ppermute x20 -> x10, waiting for transfers between devices: 40.8 us -> 14 us  [the longest x7 10.8 us: fast_body(): lax.ppermute(message, 'lane', [(i, (i + offset) % lanes) for i in range(l...]
    slice x54 -> x0, local copies, waits for them, and re-layouts: 15.1 us -> none  [the longest x6 3.89 us: near_values(): ghost[:, 5].reshape(boxes, side, side)]
    all_to_all x2 -> x0, starting transfers between devices: 12.6 us -> none  [the longest x1 7.25 us: body(): lax.all_to_all(labels, 'lane', split_axis=0, concat_axis=0, tiled=True)]
    all_to_all x2 -> x0, waiting for transfers between devices: 6.4 us -> none  [the longest x1 5.71 us: body(): lax.all_to_all(parcels, 'lane', split_axis=0, concat_axis=0, tiled=True)]
    reshape x20 -> x0, local copies, waits for them, and re-layouts: 6.08 us -> none  [the longest x6 2.64 us: near_values(): jnp.repeat(ghost[:, 4].reshape(boxes, side, side), side, axis=2)]
    another operation x58 -> x0, local copies, waits for them, and re-layouts: 4.52 us -> none  [the longest x30 2.67 us: face_layers(): jnp.stack([values[:, 0], values[:, side - 1], values[:, :, :side].reshape...]
  transfers between devices with their start and end apart: 22 -> 10, of which waited for: 17 -> 3; matrix products, arithmetic and copies ran while one was open for 7% -> 0% of each run, Pallas kernels for 0% -> 0%
where the time goes in v1:
time: 68.4 us; the launch traced here: 68 us
  Pallas kernels  33.7 us (49%)
  starting transfers between devices  15.2 us (22%)
  waiting for transfers between devices  14 us (20%)
  local copies, waits for them, and re-layouts  2.69 us (4%)
  between operations  0.95 us (1%)
  loops' own time  0.81 us (1%)
    pallas_call x1, Pallas kernels, fast_body(): pl.pallas_call(lambda *refs: pack_kernel(moves, plan, lanes, count, *refs...  23.2 us
    ppermute x7, starting transfers between devices, fast_body(): lax.ppermute(message, 'lane', [(i, (i + offset) % lanes) for i in range(l...  11.8 us
    ppermute x7, waiting for transfers between devices, fast_body(): lax.ppermute(message, 'lane', [(i, (i + offset) % lanes) for i in range(l...  10.8 us
    pallas_call x1, Pallas kernels, fast_body(): pl.pallas_call(lambda *refs: smooth_kernel(lanes, nodes, covered, *refs),...  6 us
    pallas_call x1, Pallas kernels, fast_body(): pl.pallas_call(lambda *refs: assemble_kernel(moves, plan, lanes, count, *...  4.56 us
    ppermute x1, waiting for transfers between devices, fast_body(): lax.ppermute(row_table, 'node', [(i, (i + 2) % nodes) for i in range(node...  3.24 us
    unnamed x30, local copies, waits for them, and re-layouts  2.69 us
    ppermute x1, starting transfers between devices, fast_body(): lax.ppermute(downward, 'node', [(i, (i - 1) % nodes) for i in range(nodes)])  1.73 us
  transfers between devices with their start and end apart: 10, of which 3 were waited for; matrix products, arithmetic and copies ran while one was open for 0% of the time, Pallas kernels for 0%

profile of v1, /device:TPU:0, one launch (start us, length us, event | category | flops | bytes accessed | tf_op | source)
XLA Modules:
  0.0 68.0 jit_solution(248285970462678170)
XLA Ops:
  0.7 0.6 pad_add_fusion.refs_0_
  1.2 0.1 copy-done.32
  1.3 23.2 %pack_moves.1 = (f32[29,16,128]{2,1,0:T(8,128)}, f32[7,16,128]{2,1,0:T(8,128)}, f32[5,16,128]{2,1,0:T(8,128)}, f32[5,16,128]{2,1,0:T(8,128)}, f32[5,16,128]{2,1,...) custom-call(s32[3]{0:T(128)} %pad_add_fusion.refs_0_, ...), custom_call_target="tpu_custom_call" | custom-call | tf_op jit(solution)/shard_map/pack_moves/pallas_call | solution.py:643
  24.5 3.0 %collective-permute-start.20 = (f32[29,16,128]{2,1,0:T(8,128)}, f32[29,16,128]{2,1,0:T(8,128)S(1)}, u32[]{:S(2)}, u32[]{:S(2)}) collective-permute-start(f32[29,16,128]{2,1,0:T(8,128)} %get-tuple-element.65), channel_id=1, source_target_pairs={{0,1},{1,2},{2,3},{3,4},{4,5},{5,6},{6,7},{7,0},{8,9},{9,10},{10,1... | collective-permute-start | bytes 712712 | tf_op jit(solution)/shard_map/ppermute | solution.py:654
  27.5 3.1 %collective-permute-start.26 = (f32[29,16,128]{2,1,0:T(8,128)}, f32[29,16,128]{2,1,0:T(8,128)S(1)}, u32[]{:S(2)}, u32[]{:S(2)}) collective-permute-start(f32[29,16,128]{2,1,0:T(8,128)} %get-tuple-element.71), channel_id=1, source_target_pairs={{0,7},{1,0},{2,1},{3,2},{4,3},{5,4},{6,5},{7,6},{8,15},{9,8},{10,9... | collective-permute-start | bytes 712712 | tf_op jit(solution)/shard_map/ppermute | solution.py:654
  30.6 2.5 %collective-permute-start.23 = (f32[5,16,128]{2,1,0:T(8,128)}, f32[5,16,128]{2,1,0:T(8,128)S(1)}, u32[]{:S(2)}, u32[]{:S(2)}) collective-permute-start(f32[5,16,128]{2,1,0:T(8,128)} %get-tuple-element.68), channel_id=1, source_target_pairs={{0,4},{1,5},{2,6},{3,7},{4,0},{5,1},{6,2},{7,3},{8,12},{9,13},{10,... | collective-permute-start | bytes 122888 | tf_op jit(solution)/shard_map/ppermute | solution.py:654
  33.1 0.2 collective-permute-start.21
  33.3 6.5 %collective-permute-done.22.refs_7_ = f32[5,16,128]{2,1,0:T(8,128)S(1)} collective-permute-done((f32[5,16,128]{2,1,0:T(8,128)}, f32[5,16,128]{2,1,0:T(8,128)S(1)}, u32[]{:S(2)}, u32[]{:S(2)}) %collective-permute-start.22) | collective-permute-done | bytes 40992 | tf_op jit(solution)/shard_map/ppermute | solution.py:654
  39.9 2.1 %collective-permute-start.25 = (f32[7,16,128]{2,1,0:T(8,128)}, f32[7,16,128]{2,1,0:T(8,128)S(1)}, u32[]{:S(2)}, u32[]{:S(2)}) collective-permute-start(f32[7,16,128]{2,1,0:T(8,128)} %get-tuple-element.70), channel_id=1, source_target_pairs={{0,6},{1,7},{2,0},{3,1},{4,2},{5,3},{6,4},{7,5},{8,14},{9,15},{10,... | collective-permute-start | bytes 172040 | tf_op jit(solution)/shard_map/ppermute | solution.py:654
  42.0 0.9 %collective-permute-start.24 = (f32[5,16,128]{2,1,0:T(8,128)}, f32[5,16,128]{2,1,0:T(8,128)S(1)}, u32[]{:S(2)}, u32[]{:S(2)}) collective-permute-start(f32[5,16,128]{2,1,0:T(8,128)} %get-tuple-element.69), channel_id=1, source_target_pairs={{0,5},{1,6},{2,7},{3,0},{4,1},{5,2},{6,3},{7,4},{8,13},{9,14},{10,... | collective-permute-start | bytes 122888 | tf_op jit(solution)/shard_map/ppermute | solution.py:654
  42.8 4.2 %collective-permute-done.24.refs_9_ = f32[5,16,128]{2,1,0:T(8,128)S(1)} collective-permute-done((f32[5,16,128]{2,1,0:T(8,128)}, f32[5,16,128]{2,1,0:T(8,128)S(1)}, u32[]{:S(2)}, u32[]{:S(2)}) %collective-permute-start.24) | collective-permute-done | bytes 40992 | tf_op jit(solution)/shard_map/ppermute | solution.py:654
  47.2 0.5 copy-done.52
  47.7 0.0 copy-done.48
  47.7 0.1 copy-done.44
  47.8 0.1 copy-done.45
  47.9 4.6 %assemble_block.1 = (f32[3,4,32,512]{3,2,1,0:T(8,128)}, f32[33,8,128]{2,1,0:T(8,128)}, f32[33,8,128]{2,1,0:T(8,128)}, f32[8,128]{1,0:T(8,128)}) custom-call(s32[5,8]{1,0:T(8,128)} %get-tuple-element.63.refs_0_.refs_1_, f32[8,128]{1,0:T(8,128)} %get-tuple-element.64.refs_1_, f32[8,16,256]{2,1,0:T(8,128)S(1)} %copy-done.24, f32[8,16,256]{2,1,0:T(8,128)} %refs_3_.3, ...), custom_call_target="tpu_custom_call" | custom-call | tf_op jit(solution)/shard_map/assemble_block/pallas_call | solution.py:659
  52.5 0.1 collective-permute-start.27
  52.6 1.7 %collective-permute-start.28 = (f32[33,8,128]{2,1,0:T(8,128)}, f32[33,8,128]{2,1,0:T(8,128)S(1)}, u32[]{:S(2)}, u32[]{:S(2)}) collective-permute-start(f32[33,8,128]{2,1,0:T(8,128)} %get-tuple-element.74), channel_id=1, source_target_pairs={{0,24},{8,0},{16,8},{24,16},{1,25},{9,1},{17,9},{25,17},{2,26},{10... | collective-permute-start | bytes 405512 | tf_op jit(solution)/shard_map/ppermute | solution.py:679
  54.3 1.6 %collective-permute-start.29 = (f32[8,128]{1,0:T(8,128)}, f32[8,128]{1,0:T(8,128)S(1)}, u32[]{:S(2)}, u32[]{:S(2)}) collective-permute-start(f32[8,128]{1,0:T(8,128)} %get-tuple-element.75.refs_5_), channel_id=1, source_target_pairs={{0,16},{8,24},{16,0},{24,8},{1,17},{9,25},{17,1},{25,9},{2,18},{10... | collective-permute-start | bytes 12296 | tf_op jit(solution)/shard_map/ppermute | solution.py:680
  55.9 3.2 %collective-permute-done.29.refs_6_ = f32[8,128]{1,0:T(8,128)S(1)} collective-permute-done((f32[8,128]{1,0:T(8,128)}, f32[8,128]{1,0:T(8,128)S(1)}, u32[]{:S(2)}, u32[]{:S(2)}) %collective-permute-start.29) | collective-permute-done | bytes 4128 | tf_op jit(solution)/shard_map/ppermute | solution.py:680
  59.2 1.1 %copy-done = f32[3,4,32,512]{3,2,1,0:T(8,128)S(1)} copy-done((f32[3,4,32,512]{3,2,1,0:T(8,128)S(1)}, f32[3,4,32,512]{3,2,1,0:T(8,128)}, u32[]{:S(2)}) %copy-start) | copy-done | bytes 786456
  60.3 0.7 copy-done.3
  61.0 6.0 %smooth_block.1 = (f32[8,16,256]{2,1,0:T(8,128)}, f32[8,512]{1,0:T(8,128)}, s32[1,1]{1,0:T(1,128)}) custom-call(s32[3]{0:T(128)S(1)} %copy-done.2, s32[5,8]{1,0:T(8,128)S(1)} %copy-done.1, f32[3,4,32,512]{3,2,1,0:T(8,128)S(1)} %copy-done, f32[33,8,128]{2,1,0:T(8,128)S(1)} %collective-permute-done.27.refs_3_, ...), custom_call_target="tpu_custom_call" | custom-call | tf_op jit(solution)/shard_map/smooth_block/pallas_call | solution.py:683
  67.0 0.8 %while.12 = (f32[8,16,256]{2,1,0:T(8,128)}, f32[8,512]{1,0:T(8,128)}, s32[]{:T(128)}, s32[8]{0:T(128)S(1)}, f32[8,16,256]{2,1,0:T(8,128)S(1)}, /*index=5*/f32[8,...) while((f32[8,16,256]{2,1,0:T(8,128)}, ...), condition=%region_7.8_spmd.clone, body=%region_0.7_spmd.sunk.clone | while | flops 21889904 | bytes 77573880 | solution.py:704
  (31 shorter events, 0.1 us)
Async XLA Ops:
  0.6 0.7 %copy-start.32 = (s32[8,6]{1,0:T(8,128)S(1)}, s32[8,6]{1,0:T(8,128)}, u32[]{:S(2)}) copy-start(s32[8,6]{1,0:T(8,128)} %refs_2_.2) | copy-start | bytes 580
  0.6 0.7 %copy-start.46 = (s32[8]{0:T(128)S(1)}, s32[8]{0:T(128)}, u32[]{:S(2)}) copy-start(s32[8]{0:T(128)} %refs_1_.1) | copy-start | bytes 100
  1.3 46.6 %copy-start.4 = (f32[8,16,256]{2,1,0:T(8,128)S(1)}, f32[8,16,256]{2,1,0:T(8,128)}, u32[]{:S(2)}) copy-start(f32[8,16,256]{2,1,0:T(8,128)} %refs_4_.3) | copy-start | bytes 393220
  1.3 46.6 %copy-start.24 = (f32[8,16,256]{2,1,0:T(8,128)S(1)}, f32[8,16,256]{2,1,0:T(8,128)}, u32[]{:S(2)}) copy-start(f32[8,16,256]{2,1,0:T(8,128)} %refs_2_.3) | copy-start | bytes 393220
  24.5 22.6 %collective-permute-start.20 = (f32[29,16,128]{2,1,0:T(8,128)}, f32[29,16,128]{2,1,0:T(8,128)S(1)}, u32[]{:S(2)}, u32[]{:S(2)}) collective-permute-start(f32[29,16,128]{2,1,0:T(8,128)} %get-tuple-element.65), channel_id=1, source_target_pairs={{0,1},{1,2},{2,3},{3,4},{4,5},{5,6},{6,7},{7,0},{8,9},{9,10},{10,1... | collective-permute-start | bytes 712712 | tf_op jit(solution)/shard_map/ppermute | solution.py:654
  27.5 19.6 %collective-permute-start.26 = (f32[29,16,128]{2,1,0:T(8,128)}, f32[29,16,128]{2,1,0:T(8,128)S(1)}, u32[]{:S(2)}, u32[]{:S(2)}) collective-permute-start(f32[29,16,128]{2,1,0:T(8,128)} %get-tuple-element.71), channel_id=1, source_target_pairs={{0,7},{1,0},{2,1},{3,2},{4,3},{5,4},{6,5},{7,6},{8,15},{9,8},{10,9... | collective-permute-start | bytes 712712 | tf_op jit(solution)/shard_map/ppermute | solution.py:654
  30.6 9.3 %collective-permute-start.22 = (f32[5,16,128]{2,1,0:T(8,128)}, f32[5,16,128]{2,1,0:T(8,128)S(1)}, u32[]{:S(2)}, u32[]{:S(2)}) collective-permute-start(f32[5,16,128]{2,1,0:T(8,128)} %get-tuple-element.67), channel_id=1, source_target_pairs={{0,3},{1,4},{2,5},{3,6},{4,7},{5,0},{6,1},{7,2},{8,11},{9,12},{10,... | collective-permute-start | bytes 122888 | tf_op jit(solution)/shard_map/ppermute | solution.py:654
  30.6 11.4 %collective-permute-start.23 = (f32[5,16,128]{2,1,0:T(8,128)}, f32[5,16,128]{2,1,0:T(8,128)S(1)}, u32[]{:S(2)}, u32[]{:S(2)}) collective-permute-start(f32[5,16,128]{2,1,0:T(8,128)} %get-tuple-element.68), channel_id=1, source_target_pairs={{0,4},{1,5},{2,6},{3,7},{4,0},{5,1},{6,2},{7,3},{8,12},{9,13},{10,... | collective-permute-start | bytes 122888 | tf_op jit(solution)/shard_map/ppermute | solution.py:654
  33.1 14.0 %collective-permute-start.21 = (f32[7,16,128]{2,1,0:T(8,128)}, f32[7,16,128]{2,1,0:T(8,128)S(1)}, u32[]{:S(2)}, u32[]{:S(2)}) collective-permute-start(f32[7,16,128]{2,1,0:T(8,128)} %get-tuple-element.66), channel_id=1, source_target_pairs={{0,2},{1,3},{2,4},{3,5},{4,6},{5,7},{6,0},{7,1},{8,10},{9,11},{10,... | collective-permute-start | bytes 172040 | tf_op jit(solution)/shard_map/ppermute | solution.py:654
  39.9 7.3 %copy-start.50 = (f32[5,16,128]{2,1,0:T(8,128)}, f32[5,16,128]{2,1,0:T(8,128)S(1)}, u32[]{:S(2)}) copy-start(f32[5,16,128]{2,1,0:T(8,128)S(1)} %collective-permute-done.22.refs_7_) | copy-start | bytes 122884
  39.9 7.2 %collective-permute-start.25 = (f32[7,16,128]{2,1,0:T(8,128)}, f32[7,16,128]{2,1,0:T(8,128)S(1)}, u32[]{:S(2)}, u32[]{:S(2)}) collective-permute-start(f32[7,16,128]{2,1,0:T(8,128)} %get-tuple-element.70), channel_id=1, source_target_pairs={{0,6},{1,7},{2,0},{3,1},{4,2},{5,3},{6,4},{7,5},{8,14},{9,15},{10,... | collective-permute-start | bytes 172040 | tf_op jit(solution)/shard_map/ppermute | solution.py:654
  42.0 5.2 %copy-start.51 = (f32[5,16,128]{2,1,0:T(8,128)}, f32[5,16,128]{2,1,0:T(8,128)S(1)}, u32[]{:S(2)}) copy-start(f32[5,16,128]{2,1,0:T(8,128)S(1)} %collective-permute-done.23.refs_8_) | copy-start | bytes 122884
  42.0 5.1 %collective-permute-start.24 = (f32[5,16,128]{2,1,0:T(8,128)}, f32[5,16,128]{2,1,0:T(8,128)S(1)}, u32[]{:S(2)}, u32[]{:S(2)}) collective-permute-start(f32[5,16,128]{2,1,0:T(8,128)} %get-tuple-element.69), channel_id=1, source_target_pairs={{0,5},{1,6},{2,7},{3,0},{4,1},{5,2},{6,3},{7,4},{8,13},{9,14},{10,... | collective-permute-start | bytes 122888 | tf_op jit(solution)/shard_map/ppermute | solution.py:654
  47.1 0.6 copy-start.48
  47.1 0.6 copy-start.49
  47.1 0.7 %copy-start.44 = (f32[29,16,128]{2,1,0:T(8,128)}, f32[29,16,128]{2,1,0:T(8,128)S(1)}, u32[]{:S(2)}) copy-start(f32[29,16,128]{2,1,0:T(8,128)S(1)} %collective-permute-done.20.refs_5_) | copy-start | bytes 712708
  47.1 0.8 %copy-start.45 = (f32[29,16,128]{2,1,0:T(8,128)}, f32[29,16,128]{2,1,0:T(8,128)S(1)}, u32[]{:S(2)}) copy-start(f32[29,16,128]{2,1,0:T(8,128)S(1)} %collective-permute-done.26.refs_11_) | copy-start | bytes 712708
  52.5 6.7 %copy-start.1 = (s32[5,8]{1,0:T(8,128)S(1)}, s32[5,8]{1,0:T(8,128)}, u32[]{:S(2)}) copy-start(s32[5,8]{1,0:T(8,128)} %get-tuple-element.63.refs_0_.refs_1_) | copy-start | bytes 484
  52.5 6.7 %collective-permute-start.27 = (f32[33,8,128]{2,1,0:T(8,128)}, f32[33,8,128]{2,1,0:T(8,128)S(1)}, u32[]{:S(2)}, u32[]{:S(2)}) collective-permute-start(f32[33,8,128]{2,1,0:T(8,128)} %get-tuple-element.73), channel_id=1, source_target_pairs={{0,8},{8,16},{16,24},{24,0},{1,9},{9,17},{17,25},{25,1},{2,10},{10... | collective-permute-start | bytes 405512 | tf_op jit(solution)/shard_map/ppermute | solution.py:678
  52.6 6.6 %collective-permute-start.28 = (f32[33,8,128]{2,1,0:T(8,128)}, f32[33,8,128]{2,1,0:T(8,128)S(1)}, u32[]{:S(2)}, u32[]{:S(2)}) collective-permute-start(f32[33,8,128]{2,1,0:T(8,128)} %get-tuple-element.74), channel_id=1, source_target_pairs={{0,24},{8,0},{16,8},{24,16},{1,25},{9,1},{17,9},{25,17},{2,26},{10... | collective-permute-start | bytes 405512 | tf_op jit(solution)/shard_map/ppermute | solution.py:679
  54.3 4.9 %copy-start.2 = (s32[3]{0:T(128)S(1)}, s32[3]{0:T(128)}, u32[]{:S(2)}) copy-start(s32[3]{0:T(128)} %pad_add_fusion.refs_0_) | copy-start | bytes 40
  54.3 4.8 %collective-permute-start.29 = (f32[8,128]{1,0:T(8,128)}, f32[8,128]{1,0:T(8,128)S(1)}, u32[]{:S(2)}, u32[]{:S(2)}) collective-permute-start(f32[8,128]{1,0:T(8,128)} %get-tuple-element.75.refs_5_), channel_id=1, source_target_pairs={{0,16},{8,24},{16,0},{24,8},{1,17},{9,25},{17,1},{25,9},{2,18},{10... | collective-permute-start | bytes 12296 | tf_op jit(solution)/shard_map/ppermute | solution.py:680
  59.2 1.1 %copy-start = (f32[3,4,32,512]{3,2,1,0:T(8,128)S(1)}, f32[3,4,32,512]{3,2,1,0:T(8,128)}, u32[]{:S(2)}) copy-start(f32[3,4,32,512]{3,2,1,0:T(8,128)} %get-tuple-element.72.refs_2_) | copy-start | bytes 2359300
  60.3 0.7 %copy-start.3 = (f32[8,128]{1,0:T(8,128)S(1)}, f32[8,128]{1,0:T(8,128)}, u32[]{:S(2)}) copy-start(f32[8,128]{1,0:T(8,128)} %get-tuple-element.75.refs_5_) | copy-start | bytes 12292
  (1 other events, 0.6 us)

commit v2 on v1

--- a/solution.py
+++ b/solution.py
@@ -219,24 +219,17 @@
 
 
 def pack_kernel(moves, plan, lanes, count, *refs):
-    me, target, near, field, source, beta = refs[:6]
-    outs = refs[6 : 6 + len(plan)]
-    labels, table, sems = refs[6 + len(plan) :]
+    target, near, field, source, beta = refs[:5]
+    outs = refs[5 : 5 + len(plan)]
+    labels, table = refs[5 + len(plan) :]
     side, plane = field.shape[1:]
     half = plane // 2
-    copies = []
-
-    def send(src, dst):
-        copy = pltpu.make_async_copy(src, dst, sems.at[len(copies)])
-        copy.start()
-        copies.append(copy)
-
     for out, (bulk, kept) in zip(outs, plan.values()):
         if bulk is not None:
             for at, array in enumerate((field, source, beta)):
-                send(array.at[:, :, part_lanes(bulk, plane)], out.at[at * count : (at + 1) * count])
-    lane, own = me[1], me[2]
-    first = own * count
+                out[at * count : (at + 1) * count] = array[:, :, part_lanes(bulk, plane)]
+    lane = lax.axis_index("lane")
+    first = (lax.axis_index("node") * lanes + lane) * count
     old_index = [jnp.int32(0)] * len(moves)
     new_slot = [jnp.int32(-1)] * len(moves)
     stay = []
@@ -253,7 +246,7 @@
         for move, part in kept:
             box = old_index[moves.index(move)]
             for array in (field, source):
-                send(array.at[box, :, part_lanes(part, plane)], out.at[unit])
+                out[unit] = array[box, :, part_lanes(part, plane)]
                 unit += 1
     for i in range(count):
         labels[1, i] = -1
@@ -273,8 +266,10 @@
             further, onward = local(at, 4)
             live, at = live & further, onward
         spot = jnp.where(inside, BZB, 0) + depth
-        place.append(spot)
-        labels[0, i] = spot
+        place.append((depth, jnp.where(inside, side, 0)))
+        deep, row = depth, jnp.where(inside, side, 0)
+        labels[0, i] = deep
+        labels[5, i] = row
         labels[1, spot] = i
         labels[3, i] = stay[i]
     for k in range(len(moves)):
@@ -293,78 +288,84 @@
         held = put(held, i, 0, jnp.where(slot < 0, -7, first + slot))
         for face in range(6):
             held = put(held, i, 1 + face, near[jnp.maximum(slot, 0), face])
-        held = put(held, i, 7, place[i])
+        held = put(held, i, 7, place[i][0])
+        held = put(held, i, 11, place[i][1])
         held = put(held, i, 9, stay[i])
     for k in range(len(moves)):
         held = put(held, k, 8, new_slot[k])
         held = put(held, k, 10, old_index[k])
     table[...] = held.astype(jnp.float32)
     for out in outs:
-        send(table, out.at[out.shape[0] - 1, 0:8])
-    for copy in copies:
-        copy.wait()
+        out[out.shape[0] - 1, 0:8] = table[...]
 
 
 def assemble_kernel(moves, plan, lanes, count, *refs):
     labels, own_table, field, source, beta = refs[:5]
     got = dict(zip(plan, refs[5 : 5 + len(plan)]))
-    block, upward, downward, row_table, tables, seen, sem, table_sems, seen_sems = refs[5 + len(plan) :]
+    block, upward, downward, row_table, tables, table_sems = refs[5 + len(plan) :]
     side, plane = field.shape[1:]
     half = plane // 2
     order = list(plan)
-    fetch = []
-    for k, offset in enumerate(order):
-        fetch.append(pltpu.make_async_copy(got[offset].at[got[offset].shape[0] - 1, 0:8], tables.at[k], table_sems.at[k]))
-    shown = {0: None, 1: 1, lanes - 1: lanes - 1}
-    if lanes == 8:
-        shown = {offset: offset for offset in range(8) if offset == 0 or offset in got}
-    for offset in shown:
-        if offset:
-            at = offset % 8 if offset < lanes - 1 else 7
-            fetch.append(pltpu.make_async_copy(got[offset].at[got[offset].shape[0] - 1, 0:8], seen.at[at], seen_sems.at[at]))
+
+    def table_of(offset):
+        return got[offset].at[got[offset].shape[0] - 1, 0:8]
+
+    fetch = [
+        pltpu.make_async_copy(table_of(offset), tables.at[k], table_sems.at[k]) for k, offset in enumerate(order)
+    ]
     for copy in fetch:
         copy.start()
 
-    def spot(place):
-        return lax.rem(place, BZB), pl.ds(pl.multiple_of(lax.div(place, BZB) * side, side), side)
-
-    def copy(src, array, place, where):
-        deep, rows = spot(place)
-        pltpu.make_async_copy(src, block.at[array, deep, rows, where], sem).start()
+    def put(array, spot, where, values):
+        deep, row = spot
+        block[array, deep, pl.ds(pl.multiple_of(row, side), side), where] = values
+
+    def checked(slot, spot):
+        return jnp.where(slot >= 0, spot[0], BZB), jnp.where(slot >= 0, spot[1], 0)
 
     own_half = {LOW: slice(half, 2 * half), HIGH: slice(2 * half, 3 * half)}
     low_halo, high_halo = slice(0, half), slice(3 * half, 4 * half)
     whole = slice(half, 3 * half)
     old = (field, source)
+
+    def spot_here(slot):
+        at = jnp.maximum(slot, 0)
+        return checked(slot, (labels[0, at], labels[5, at]))
+
     for i in range(count):
-        copy(beta.at[i], 2, labels[0, i], whole)
-
-        @pl.when(labels[3, i] >= 0)
-        def _():
-            for a in range(2):
-                copy(old[a].at[i], a, labels[0, labels[3, i]], whole)
-
-    for k in range(len(order)):
-        fetch[k].wait()
+        put(2, (labels[0, i], labels[5, i]), whole, beta[i])
+        spot = spot_here(labels[3, i])
+        for a in range(2):
+            put(a, spot, whole, old[a][i])
+
+    cols = lax.broadcasted_iota(jnp.int32, (8, 128), 1)
+    shown = [offset for offset in plan if lanes == 8 or offset in (1, lanes - 1)]
+    joined = jnp.where(cols < 8, own_table[...], 0.0)
+    for offset in shown:
+        at = offset if offset < 7 else 7
+        joined = joined + pltpu.roll(jnp.where(cols < 8, table_of(offset)[...], 0.0), 8 * at, 1)
+    joined = joined + pltpu.roll(joined, 64, 1)
+    row_table[...] = joined
+    upward[upward.shape[0] - 1] = joined
+    downward[downward.shape[0] - 1] = joined
+
+    for copy in fetch:
+        copy.wait()
 
     def said(offset, row, col):
         return tables[order.index(offset), row, col].astype(jnp.int32)
 
     below, above = 1, lanes - 1
 
-    def place_below(slot):
-        return said(below, slot, 7)
-
-    def place_above(slot):
-        return said(above, slot, 7)
-
-    for move, part, halo, place in ((1, LOW, high_halo, place_above), (lanes - 1, HIGH, low_halo, place_below)):
+    def spot_at(offset, slot):
+        at = jnp.maximum(slot, 0)
+        return checked(slot, (said(offset, at, 7), said(offset, at, 11)))
+
+    for move, part, halo, there in ((1, LOW, high_halo, above), (lanes - 1, HIGH, low_halo, below)):
         k = moves.index(move)
-
-        @pl.when(labels[2, k] >= 0)
-        def _():
-            for a in range(2):
-                copy(old[a].at[labels[4, k], :, part_lanes(part, plane)], a, place(labels[2, k]), halo)
+        spot = spot_at(there, labels[2, k])
+        for a in range(2):
+            put(a, spot, halo, old[a][labels[4, k], :, part_lanes(part, plane)])
 
     for offset, (bulk, kept) in plan.items():
         message = got[offset]
@@ -372,51 +373,28 @@
         if bulk is not None:
             halo = low_halo if offset == below else high_halo
             for i in range(count):
-                copy(message.at[2 * count + i], 2, said(offset, i, 7), halo)
-
-                @pl.when(said(offset, i, 9) >= 0)
-                def _():
-                    for a in range(2):
-                        copy(message.at[a * count + i], a, said(offset, said(offset, i, 9), 7), halo)
-
+                put(2, (said(offset, i, 7), said(offset, i, 11)), halo, message[2 * count + i])
+                spot = spot_at(offset, said(offset, i, 9))
+                for a in range(2):
+                    put(a, spot, halo, message[a * count + i])
             k = moves.index(offset)
-
-            @pl.when(said(offset, k, 8) >= 0)
-            def _():
-                for a in range(2):
-                    copy(message.at[a * count + said(offset, k, 10)], a, labels[0, said(offset, k, 8)], own_half[bulk])
-
+            spot, box = spot_here(said(offset, k, 8)), said(offset, k, 10)
+            for a in range(2):
+                put(a, spot, own_half[bulk], message[a * count + box])
             unit = 3 * count
         for move, part in kept:
-            k = moves.index(move)
+            slot = said(offset, moves.index(move), 8)
             apart = (move - offset) % lanes
-
-            @pl.when(said(offset, k, 8) >= 0)
-            def _():
-                slot = said(offset, k, 8)
-                if apart == 0:
-                    place, where = labels[0, slot], own_half[part]
-                elif apart == 1:
-                    place, where = place_above(slot), high_halo
-                else:
-                    place, where = place_below(slot), low_halo
-                for a in range(2):
-                    copy(message.at[unit + a], a, place, where)
-
+            if apart == 0:
+                spot, where = spot_here(slot), own_half[part]
+            elif apart == 1:
+                spot, where = spot_at(above, slot), high_halo
+            else:
+                spot, where = spot_at(below, slot), low_halo
+            for a in range(2):
+                put(a, spot, where, message[unit + a])
             unit += 2
-    cols = lax.broadcasted_iota(jnp.int32, (8, 128), 1)
-    for copy_in in fetch[len(order) :]:
-        copy_in.wait()
-    joined = jnp.where(cols < 8, own_table[...], 0.0)
-    for offset in shown:
-        if offset:
-            at = offset if offset < 7 else 7
-            joined = joined + pltpu.roll(jnp.where(cols < 8, seen[at], 0.0), 8 * at, 1)
-    joined = joined + pltpu.roll(joined, 64, 1)
-    row_table[...] = joined
-    upward[upward.shape[0] - 1] = joined
-    downward[downward.shape[0] - 1] = joined
-    pltpu.make_async_copy(block, block, sem).wait()
+
     width = block.shape[3]
     levels = lax.broadcasted_iota(jnp.int32, (8, width), 0)
     last = block.shape[2] - 8
@@ -436,7 +414,7 @@
             downward[at + width // 128] = down_second[:, cut]
 
 
-def smooth_kernel(lanes, nodes, covered, me, labels, block, from_below, from_above, row_table, two_on, smoothed, coarse, flag,
+def smooth_kernel(lanes, nodes, covered, labels, block, from_below, from_above, row_table, two_on, smoothed, coarse, flag,
                   f, s, b, xl, xu, yl, yu, zl, zu, total, inverse, rest):
     width = block.shape[3]
     own_rows = block.shape[2]
@@ -444,7 +422,7 @@
     plane = smoothed.shape[2]
     half = plane // 2
     tiles = width // 128
-    node, lane = me[0], me[1]
+    node, lane = lax.axis_index("node"), lax.axis_index("lane")
     first_node, last_node = node == 0, node == nodes - 1
     first_lane, last_lane = lane == 0, lane == lanes - 1
     top = 2 * PAD + own_rows
@@ -624,7 +602,7 @@
     flag[0, 0] = (jnp.sum(wrong) > 0).astype(jnp.int32)
 
 
-ANY = pl.BlockSpec(memory_space=pl.ANY)
+ROOM = pltpu.CompilerParams(vmem_limit_bytes=32 * 2**20)
 SCALARS = pl.BlockSpec(memory_space=pltpu.SMEM)
 VECTORS = pl.BlockSpec(memory_space=pltpu.VMEM)
 
@@ -633,22 +611,19 @@
     count, side, plane = old_field.shape
     half = plane // 2
     lanes, nodes = lax.axis_size("lane"), lax.axis_size("node")
-    lane, node = lax.axis_index("lane"), lax.axis_index("node")
-    me = jnp.stack([node, lane, node * lanes + lane]).astype(jnp.int32)
     moves, plan = lane_plan(lanes)
     covered = lanes == 8 and nodes == 4
     units = [(3 * count if bulk is not None else 0) + 2 * len(kept) + 1 for bulk, kept in plan.values()]
-    sent = sum(units)
     f32 = jnp.float32
     packed = pl.pallas_call(
         lambda *refs: pack_kernel(moves, plan, lanes, count, *refs),
         name="pack_moves",
-        out_shape=[jax.ShapeDtypeStruct((n, side, half), f32) for n in units]
-        + [jax.ShapeDtypeStruct((5, count), jnp.int32), jax.ShapeDtypeStruct((8, 128), f32)],
-        in_specs=[SCALARS] * 3 + [ANY] * 3,
-        out_specs=[ANY] * len(units) + [SCALARS, VECTORS],
-        scratch_shapes=[pltpu.SemaphoreType.DMA((sent,))],
-    )(me, target_box, neighbours, old_field, old_source, diffusivity)
+        out_shape=[pltpu.VMEM((n, side, half), f32) for n in units]
+        + [jax.ShapeDtypeStruct((6, count), jnp.int32), pltpu.VMEM((8, 128), f32)],
+        in_specs=[SCALARS] * 2 + [VECTORS] * 3,
+        out_specs=[VECTORS] * len(units) + [SCALARS, VECTORS],
+        compiler_params=ROOM,
+    )(target_box, neighbours, old_field, old_source, diffusivity)
     messages, labels, own_table = packed[:-2], packed[-2], packed[-1]
     got = [
         lax.ppermute(message, "lane", [(i, (i + offset) % lanes) for i in range(lanes)])
@@ -660,20 +635,18 @@
         lambda *refs: assemble_kernel(moves, plan, lanes, count, *refs),
         name="assemble_block",
         out_shape=[
-            jax.ShapeDtypeStruct((3, BZB, BXD * side, width), f32),
-            jax.ShapeDtypeStruct((strips, 8, 128), f32),
-            jax.ShapeDtypeStruct((strips, 8, 128), f32),
-            jax.ShapeDtypeStruct((8, 128), f32),
+            pltpu.VMEM((3, BZB + 1, BXD * side, width), f32),
+            pltpu.VMEM((strips, 8, 128), f32),
+            pltpu.VMEM((strips, 8, 128), f32),
+            pltpu.VMEM((8, 128), f32),
         ],
-        in_specs=[SCALARS, VECTORS] + [ANY] * (3 + len(units)),
+        in_specs=[SCALARS] + [VECTORS] * (4 + len(units)),
         out_specs=[VECTORS] * 4,
         scratch_shapes=[
             pltpu.SMEM((len(units), 8, 128), f32),
-            pltpu.VMEM((8, 8, 128), f32),
-            pltpu.SemaphoreType.DMA,
             pltpu.SemaphoreType.DMA((len(units),)),
-            pltpu.SemaphoreType.DMA((8,)),
         ],
+        compiler_params=ROOM,
     )(labels, own_table, old_field, old_source, diffusivity, *got)
     from_below = lax.ppermute(upward, "node", [(i, (i + 1) % nodes) for i in range(nodes)])
     from_above = lax.ppermute(downward, "node", [(i, (i - 1) % nodes) for i in range(nodes)])
@@ -688,11 +661,11 @@
             jax.ShapeDtypeStruct((count, (side // 2) ** 3), f32),
             jax.ShapeDtypeStruct((1, 1), jnp.int32),
         ],
-        in_specs=[SCALARS] * 2 + [VECTORS] * 5,
+        in_specs=[SCALARS] + [VECTORS] * 5,
         out_specs=[VECTORS, VECTORS, SCALARS],
         scratch_shapes=[big] * 9 + [pltpu.VMEM((BZB, BXD * side, width), f32), big, pltpu.VMEM((plane // 128, count * side, 128), f32)],
-        compiler_params=pltpu.CompilerParams(vmem_limit_bytes=48 * 2**20),
-    )(me, labels, block, from_below, from_above, row_table, two_on)
+        compiler_params=ROOM,
+    )(labels, block, from_below, from_above, row_table, two_on)
     irregular = flag[0, 0]
     if not covered:
         irregular = lax.pmax(irregular, ("node", "lane"))

time: 68.4 us -> 40.7 us (0.60)
  Pallas kernels: 33.7 us -> 10.4 us
  local copies, waits for them, and re-layouts: 2.69 us -> 0.01 us
    pallas_call x1, Pallas kernels: 23.2 us -> 2.01 us  [fast_body(): pl.pallas_call(lambda *refs: pack_kernel(moves, plan, lanes, count, *refs...]
    unnamed x30 -> x4, local copies, waits for them, and re-layouts: 2.69 us -> 0.01 us
    pallas_call x1, Pallas kernels: 4.56 us -> 2.37 us  [fast_body(): pl.pallas_call(lambda *refs: assemble_kernel(moves, plan, lanes, count, *...]
where the time goes in v2:
time: 40.7 us; the launch traced here: 40.5 us
  starting transfers between devices  15.1 us (37%)
  waiting for transfers between devices  13.4 us (33%)
  Pallas kernels  10.4 us (26%)
  between operations  0.87 us (2%)
  loops' own time  0.76 us (2%)
    ppermute x7, starting transfers between devices, fast_body(): lax.ppermute(message, 'lane', [(i, (i + offset) % lanes) for i in range(l...  11.8 us
    ppermute x7, waiting for transfers between devices, fast_body(): lax.ppermute(message, 'lane', [(i, (i + offset) % lanes) for i in range(l...  10.3 us
    pallas_call x1, Pallas kernels, fast_body(): pl.pallas_call(lambda *refs: smooth_kernel(lanes, nodes, covered, *refs),...  5.99 us
    ppermute x1, waiting for transfers between devices, fast_body(): lax.ppermute(row_table, 'node', [(i, (i + 2) % nodes) for i in range(node...  3.03 us
    pallas_call x1, Pallas kernels, fast_body(): pl.pallas_call(lambda *refs: assemble_kernel(moves, plan, lanes, count, *...  2.37 us
    pallas_call x1, Pallas kernels, fast_body(): pl.pallas_call(lambda *refs: pack_kernel(moves, plan, lanes, count, *refs...  2.01 us
    ppermute x1, starting transfers between devices, fast_body(): lax.ppermute(downward, 'node', [(i, (i - 1) % nodes) for i in range(nodes)])  1.73 us
    ppermute x1, starting transfers between devices, fast_body(): lax.ppermute(row_table, 'node', [(i, (i + 2) % nodes) for i in range(node...  1.52 us
  transfers between devices with their start and end apart: 10, of which 3 were waited for; matrix products, arithmetic and copies ran while one was open for 0% of the time, Pallas kernels for 0%

profile of v2, /device:TPU:0, one launch (start us, length us, event | category | flops | bytes accessed | tf_op | source)
XLA Modules:
  0.0 40.5 jit_solution(7330868179620508707)
XLA Ops:
  0.6 0.0 copy-start.20
  0.7 2.0 %pack_moves.1 = (f32[29,16,128]{2,1,0:T(8,128)S(1)}, f32[7,16,128]{2,1,0:T(8,128)S(1)}, f32[5,16,128]{2,1,0:T(8,128)S(1)}, f32[5,16,128]{2,1,0:T(8,128)S(1)}, f3...) custom-call(s32[8]{0:T(128)} %refs_0_.1, ...), custom_call_target="tpu_custom_call" | custom-call | tf_op jit(solution)/shard_map/pack_moves/pallas_call | solution.py:618
  2.7 3.0 %collective-permute-start.20 = (f32[29,16,128]{2,1,0:T(8,128)S(1)}, f32[29,16,128]{2,1,0:T(8,128)S(1)}, u32[]{:S(2)}, u32[]{:S(2)}) collective-permute-start(f32[29,16,128]{2,1,0:T(8,128)S(1)} %get-tuple-element.65), channel_id=1, source_target_pairs={{0,1},{1,2},{2,3},{3,4},{4,5},{5,6},{6,7},{7,0},{8,9},{9,10},{10,1... | collective-permute-start | bytes 712712 | tf_op jit(solution)/shard_map/ppermute | solution.py:629
  5.7 3.1 %collective-permute-start.26 = (f32[29,16,128]{2,1,0:T(8,128)S(1)}, f32[29,16,128]{2,1,0:T(8,128)S(1)}, u32[]{:S(2)}, u32[]{:S(2)}) collective-permute-start(f32[29,16,128]{2,1,0:T(8,128)S(1)} %get-tuple-element.71), channel_id=1, source_target_pairs={{0,7},{1,0},{2,1},{3,2},{4,3},{5,4},{6,5},{7,6},{8,15},{9,8},{10,9... | collective-permute-start | bytes 712712 | tf_op jit(solution)/shard_map/ppermute | solution.py:629
  8.8 0.0 collective-permute-start.22
  8.8 2.5 %collective-permute-start.23 = (f32[5,16,128]{2,1,0:T(8,128)S(1)}, f32[5,16,128]{2,1,0:T(8,128)S(1)}, u32[]{:S(2)}, u32[]{:S(2)}) collective-permute-start(f32[5,16,128]{2,1,0:T(8,128)S(1)} %get-tuple-element.68), channel_id=1, source_target_pairs={{0,4},{1,5},{2,6},{3,7},{4,0},{5,1},{6,2},{7,3},{8,12},{9,13},{10,... | collective-permute-start | bytes 122888 | tf_op jit(solution)/shard_map/ppermute | solution.py:629
  11.3 0.2 collective-permute-start.21
  11.5 6.3 %collective-permute-done.22.refs_7_ = f32[5,16,128]{2,1,0:T(8,128)S(1)} collective-permute-done((f32[5,16,128]{2,1,0:T(8,128)S(1)}, f32[5,16,128]{2,1,0:T(8,128)S(1)}, u32[]{:S(2)}, u32[]{:S(2)}) %collective-permute-start.22) | collective-permute-done | bytes 40992 | tf_op jit(solution)/shard_map/ppermute | solution.py:629
  17.8 2.1 %collective-permute-start.25 = (f32[7,16,128]{2,1,0:T(8,128)S(1)}, f32[7,16,128]{2,1,0:T(8,128)S(1)}, u32[]{:S(2)}, u32[]{:S(2)}) collective-permute-start(f32[7,16,128]{2,1,0:T(8,128)S(1)} %get-tuple-element.70), channel_id=1, source_target_pairs={{0,6},{1,7},{2,0},{3,1},{4,2},{5,3},{6,4},{7,5},{8,14},{9,15},{10,... | collective-permute-start | bytes 172040 | tf_op jit(solution)/shard_map/ppermute | solution.py:629
  19.9 0.0 collective-permute-done.23.refs_8_
  19.9 0.9 %collective-permute-start.24 = (f32[5,16,128]{2,1,0:T(8,128)S(1)}, f32[5,16,128]{2,1,0:T(8,128)S(1)}, u32[]{:S(2)}, u32[]{:S(2)}) collective-permute-start(f32[5,16,128]{2,1,0:T(8,128)S(1)} %get-tuple-element.69), channel_id=1, source_target_pairs={{0,5},{1,6},{2,7},{3,0},{4,1},{5,2},{6,3},{7,4},{8,13},{9,14},{10,... | collective-permute-start | bytes 122888 | tf_op jit(solution)/shard_map/ppermute | solution.py:629
  20.8 4.0 %collective-permute-done.24.refs_9_ = f32[5,16,128]{2,1,0:T(8,128)S(1)} collective-permute-done((f32[5,16,128]{2,1,0:T(8,128)S(1)}, f32[5,16,128]{2,1,0:T(8,128)S(1)}, u32[]{:S(2)}, u32[]{:S(2)}) %collective-permute-start.24) | collective-permute-done | bytes 40992 | tf_op jit(solution)/shard_map/ppermute | solution.py:629
  24.8 0.0 collective-permute-done.21.refs_6_
  24.8 0.0 collective-permute-done.25.refs_10_
  24.8 0.0 collective-permute-done.20.refs_5_
  24.9 2.4 %assemble_block.1 = (f32[3,5,32,512]{3,2,1,0:T(8,128)S(1)}, f32[33,8,128]{2,1,0:T(8,128)S(1)}, f32[33,8,128]{2,1,0:T(8,128)S(1)}, f32[8,128]{1,0:T(8,128)S(1)}) custom-call(s32[6,8]{1,0:T(8,128)S(1)} %get-tuple-element.63.refs_0_, f32[8,128]{1,0:T(8,128)S(1)} %get-tuple-element.64.refs_1_, f32[8,16,256]{2,1,0:T(8,128)S(1)} %copy-done.20, ...), custom_call_target="tpu_custom_call" | custom-call | tf_op jit(solution)/shard_map/assemble_block/pallas_call | solution.py:634
  27.2 0.1 collective-permute-start.27
  27.3 1.7 %collective-permute-start.28 = (f32[33,8,128]{2,1,0:T(8,128)S(1)}, f32[33,8,128]{2,1,0:T(8,128)S(1)}, u32[]{:S(2)}, u32[]{:S(2)}) collective-permute-start(f32[33,8,128]{2,1,0:T(8,128)S(1)} %get-tuple-element.74), channel_id=1, source_target_pairs={{0,24},{8,0},{16,8},{24,16},{1,25},{9,1},{17,9},{25,17},{2,26},{10... | collective-permute-start | bytes 405512 | tf_op jit(solution)/shard_map/ppermute | solution.py:652
  29.0 1.5 %collective-permute-start.29 = (f32[8,128]{1,0:T(8,128)S(1)}, f32[8,128]{1,0:T(8,128)S(1)}, u32[]{:S(2)}, u32[]{:S(2)}) collective-permute-start(f32[8,128]{1,0:T(8,128)S(1)} %get-tuple-element.75.refs_4_), channel_id=1, source_target_pairs={{0,16},{8,24},{16,0},{24,8},{1,17},{9,25},{17,1},{25,9},{2,18},{10... | collective-permute-start | bytes 12296 | tf_op jit(solution)/shard_map/ppermute | solution.py:653
  30.6 3.0 %collective-permute-done.29.refs_5_ = f32[8,128]{1,0:T(8,128)S(1)} collective-permute-done((f32[8,128]{1,0:T(8,128)S(1)}, f32[8,128]{1,0:T(8,128)S(1)}, u32[]{:S(2)}, u32[]{:S(2)}) %collective-permute-start.29) | collective-permute-done | bytes 4128 | tf_op jit(solution)/shard_map/ppermute | solution.py:653
  33.6 0.0 collective-permute-done.27.refs_2_
  33.6 0.0 collective-permute-done.28.refs_3_
  33.6 6.0 %smooth_block.1 = (f32[8,16,256]{2,1,0:T(8,128)}, f32[8,512]{1,0:T(8,128)}, s32[1,1]{1,0:T(1,128)}) custom-call(s32[6,8]{1,0:T(8,128)S(1)} %get-tuple-element.63.refs_0_, f32[3,5,32,512]{3,2,1,0:T(8,128)S(1)} %get-tuple-element.72.refs_1_, f32[33,8,128]{2,1,0:T(8,128)S(1)} %collective-permute-done.27.refs_2_, ...), custom_call_target="tpu_custom_call" | custom-call | tf_op jit(solution)/shard_map/smooth_block/pallas_call | solution.py:656
  39.6 0.8 %while.12 = (f32[8,16,256]{2,1,0:T(8,128)}, f32[8,512]{1,0:T(8,128)}, s32[]{:T(128)}, s32[8]{0:T(128)}, f32[8,16,256]{2,1,0:T(8,128)S(1)}, /*index=5*/f32[8,16,2...) while((f32[8,16,256]{2,1,0:T(8,128)}, f32[8,512]{1,0:T(8,128)}, ...), condition=%region_7.8_spmd.clone, body=%region_0.7_spmd.sunk.clone | while | flops 21889904 | bytes 77572904 | solution.py:677
  (4 shorter events, 0.0 us)
Async XLA Ops:
  0.6 24.2 %copy-start = (f32[8,16,256]{2,1,0:T(8,128)S(1)}, f32[8,16,256]{2,1,0:T(8,128)}, u32[]{:S(2)}) copy-start(f32[8,16,256]{2,1,0:T(8,128)} %refs_4_.3) | copy-start | bytes 393220
  0.6 24.2 %copy-start.20 = (f32[8,16,256]{2,1,0:T(8,128)S(1)}, f32[8,16,256]{2,1,0:T(8,128)}, u32[]{:S(2)}) copy-start(f32[8,16,256]{2,1,0:T(8,128)} %refs_2_.3) | copy-start | bytes 393220
  2.7 22.2 %collective-permute-start.20 = (f32[29,16,128]{2,1,0:T(8,128)S(1)}, f32[29,16,128]{2,1,0:T(8,128)S(1)}, u32[]{:S(2)}, u32[]{:S(2)}) collective-permute-start(f32[29,16,128]{2,1,0:T(8,128)S(1)} %get-tuple-element.65), channel_id=1, source_target_pairs={{0,1},{1,2},{2,3},{3,4},{4,5},{5,6},{6,7},{7,0},{8,9},{9,10},{10,1... | collective-permute-start | bytes 712712 | tf_op jit(solution)/shard_map/ppermute | solution.py:629
  5.7 19.2 %collective-permute-start.26 = (f32[29,16,128]{2,1,0:T(8,128)S(1)}, f32[29,16,128]{2,1,0:T(8,128)S(1)}, u32[]{:S(2)}, u32[]{:S(2)}) collective-permute-start(f32[29,16,128]{2,1,0:T(8,128)S(1)} %get-tuple-element.71), channel_id=1, source_target_pairs={{0,7},{1,0},{2,1},{3,2},{4,3},{5,4},{6,5},{7,6},{8,15},{9,8},{10,9... | collective-permute-start | bytes 712712 | tf_op jit(solution)/shard_map/ppermute | solution.py:629
  8.8 9.1 %collective-permute-start.22 = (f32[5,16,128]{2,1,0:T(8,128)S(1)}, f32[5,16,128]{2,1,0:T(8,128)S(1)}, u32[]{:S(2)}, u32[]{:S(2)}) collective-permute-start(f32[5,16,128]{2,1,0:T(8,128)S(1)} %get-tuple-element.67), channel_id=1, source_target_pairs={{0,3},{1,4},{2,5},{3,6},{4,7},{5,0},{6,1},{7,2},{8,11},{9,12},{10,... | collective-permute-start | bytes 122888 | tf_op jit(solution)/shard_map/ppermute | solution.py:629
  8.8 11.1 %collective-permute-start.23 = (f32[5,16,128]{2,1,0:T(8,128)S(1)}, f32[5,16,128]{2,1,0:T(8,128)S(1)}, u32[]{:S(2)}, u32[]{:S(2)}) collective-permute-start(f32[5,16,128]{2,1,0:T(8,128)S(1)} %get-tuple-element.68), channel_id=1, source_target_pairs={{0,4},{1,5},{2,6},{3,7},{4,0},{5,1},{6,2},{7,3},{8,12},{9,13},{10,... | collective-permute-start | bytes 122888 | tf_op jit(solution)/shard_map/ppermute | solution.py:629
  11.3 13.5 %collective-permute-start.21 = (f32[7,16,128]{2,1,0:T(8,128)S(1)}, f32[7,16,128]{2,1,0:T(8,128)S(1)}, u32[]{:S(2)}, u32[]{:S(2)}) collective-permute-start(f32[7,16,128]{2,1,0:T(8,128)S(1)} %get-tuple-element.66), channel_id=1, source_target_pairs={{0,2},{1,3},{2,4},{3,5},{4,6},{5,7},{6,0},{7,1},{8,10},{9,11},{10,... | collective-permute-start | bytes 172040 | tf_op jit(solution)/shard_map/ppermute | solution.py:629
  17.8 7.0 %collective-permute-start.25 = (f32[7,16,128]{2,1,0:T(8,128)S(1)}, f32[7,16,128]{2,1,0:T(8,128)S(1)}, u32[]{:S(2)}, u32[]{:S(2)}) collective-permute-start(f32[7,16,128]{2,1,0:T(8,128)S(1)} %get-tuple-element.70), channel_id=1, source_target_pairs={{0,6},{1,7},{2,0},{3,1},{4,2},{5,3},{6,4},{7,5},{8,14},{9,15},{10,... | collective-permute-start | bytes 172040 | tf_op jit(solution)/shard_map/ppermute | solution.py:629
  19.9 4.9 %collective-permute-start.24 = (f32[5,16,128]{2,1,0:T(8,128)S(1)}, f32[5,16,128]{2,1,0:T(8,128)S(1)}, u32[]{:S(2)}, u32[]{:S(2)}) collective-permute-start(f32[5,16,128]{2,1,0:T(8,128)S(1)} %get-tuple-element.69), channel_id=1, source_target_pairs={{0,5},{1,6},{2,7},{3,0},{4,1},{5,2},{6,3},{7,4},{8,13},{9,14},{10,... | collective-permute-start | bytes 122888 | tf_op jit(solution)/shard_map/ppermute | solution.py:629
  27.2 6.4 %collective-permute-start.27 = (f32[33,8,128]{2,1,0:T(8,128)S(1)}, f32[33,8,128]{2,1,0:T(8,128)S(1)}, u32[]{:S(2)}, u32[]{:S(2)}) collective-permute-start(f32[33,8,128]{2,1,0:T(8,128)S(1)} %get-tuple-element.73), channel_id=1, source_target_pairs={{0,8},{8,16},{16,24},{24,0},{1,9},{9,17},{17,25},{25,1},{2,10},{10... | collective-permute-start | bytes 405512 | tf_op jit(solution)/shard_map/ppermute | solution.py:651
  27.3 6.3 %collective-permute-start.28 = (f32[33,8,128]{2,1,0:T(8,128)S(1)}, f32[33,8,128]{2,1,0:T(8,128)S(1)}, u32[]{:S(2)}, u32[]{:S(2)}) collective-permute-start(f32[33,8,128]{2,1,0:T(8,128)S(1)} %get-tuple-element.74), channel_id=1, source_target_pairs={{0,24},{8,0},{16,8},{24,16},{1,25},{9,1},{17,9},{25,17},{2,26},{10... | collective-permute-start | bytes 405512 | tf_op jit(solution)/shard_map/ppermute | solution.py:652
  29.0 4.5 %collective-permute-start.29 = (f32[8,128]{1,0:T(8,128)S(1)}, f32[8,128]{1,0:T(8,128)S(1)}, u32[]{:S(2)}, u32[]{:S(2)}) collective-permute-start(f32[8,128]{1,0:T(8,128)S(1)} %get-tuple-element.75.refs_4_), channel_id=1, source_target_pairs={{0,16},{8,24},{16,0},{24,8},{1,17},{9,25},{17,1},{25,9},{2,18},{10... | collective-permute-start | bytes 12296 | tf_op jit(solution)/shard_map/ppermute | solution.py:653

commit v3 on v2

--- a/solution.py
+++ b/solution.py
@@ -189,29 +189,80 @@
 BXD = 2
 BZB = 4
 PAD = 8
+SIDE = 16
 LOW, HIGH = "low", "high"
 
 
 def lane_plan(lanes):
     half = lanes // 2
     moves = [1, lanes - 1, 2, lanes - 2, half]
-    singles = {}
-
-    def add(offset, move, part):
-        if offset % lanes:
-            singles.setdefault(offset % lanes, []).append((move, part))
-
+    ends = {}
     for move in moves:
-        add(move, move, LOW)
-        add(move, move, HIGH)
-        add(move + 1, move, HIGH)
-        add(move - 1, move, LOW)
+        for offset, part in ((move + 1, HIGH), (move - 1, LOW)):
+            ends.setdefault(offset % lanes, []).append((move, part))
     bulk = {1: HIGH, lanes - 1: LOW}
     plan = {}
-    for offset in sorted(singles):
-        kept = [item for item in singles[offset] if not (item[0] == offset and item[1] == bulk.get(offset))]
-        plan[offset] = (bulk.get(offset), kept)
+    for offset in sorted(set(moves) | set(ends)):
+        if offset:
+            plan[offset] = (bulk.get(offset), offset in moves, ends.get(offset, []))
     return moves, plan
+
+
+def plan_units(count, bulk, whole, kept):
+    return (count + count // 2 if bulk is not None else 0) + (3 if whole else 0) + len(kept) + 1
+
+
+def cell_lanes(side):
+    rows = lax.broadcasted_iota(jnp.int32, (side, 128), 0)
+    cols = lax.broadcasted_iota(jnp.int32, (side, 128), 1)
+    black = lax.rem(rows + lax.div(cols, side) + lax.rem(cols, side), 2) == 1
+    return cols, black
+
+
+def turn(values, shift):
+    return pltpu.roll(values, shift % values.shape[-1], values.ndim - 1)
+
+
+def pack_end(part, field, source, beta):
+    side = field.shape[0]
+    cols, black = cell_lanes(side)
+    y = lax.div(cols, side)
+    if part == HIGH:
+        pairs = jnp.where(black, field, turn(field, side))
+        out = jnp.where(y >= 4, source, pairs)
+        out = jnp.where(y == 2, turn(beta, -side), out)
+        out = jnp.where(y == 1, turn(pairs, -4 * side), out)
+        return jnp.where(y == 0, turn(pairs, side), out)
+    pairs = jnp.where(black, field, turn(field, -side))
+    out = jnp.where(y < 4, source, pairs)
+    out = jnp.where(y == 5, turn(beta, side), out)
+    out = jnp.where(y == 6, turn(pairs, 4 * side), out)
+    return jnp.where(y == 7, turn(pairs, -side), out)
+
+
+def unpack_end(part, packed):
+    side = packed.shape[0]
+    y = lax.div(lax.broadcasted_iota(jnp.int32, packed.shape, 1), side)
+    out = packed
+    places = ((7, 7), (6, 6), (5, 4), (4, 3)) if part == HIGH else ((0, 1), (1, 2), (2, 4), (3, 5))
+    for layer, shift in places:
+        out = jnp.where(y == layer, turn(packed, shift * side), out)
+    return out
+
+
+def pack_whole(low, high):
+    side = low.shape[0]
+    cols, black = cell_lanes(side)
+    even = lax.rem(lax.div(cols, side), 2) == 0
+    low = jnp.where(black, low, turn(low, -side))
+    high = jnp.where(black, high, turn(high, -side))
+    return jnp.where(even, low, turn(high, side))
+
+
+def unpack_whole(packed):
+    side = packed.shape[0]
+    even = lax.rem(lax.div(lax.broadcasted_iota(jnp.int32, packed.shape, 1), side), 2) == 0
+    return jnp.where(even, packed, turn(packed, side)), jnp.where(even, turn(packed, -side), packed)
 
 
 def part_lanes(part, plane):
@@ -224,10 +275,15 @@
     labels, table = refs[5 + len(plan) :]
     side, plane = field.shape[1:]
     half = plane // 2
-    for out, (bulk, kept) in zip(outs, plan.values()):
+    left = lax.broadcasted_iota(jnp.int32, (side, 128), 1) < 64
+    for out, (bulk, whole, kept) in zip(outs, plan.values()):
         if bulk is not None:
-            for at, array in enumerate((field, source, beta)):
-                out[at * count : (at + 1) * count] = array[:, :, part_lanes(bulk, plane)]
+            cut = part_lanes(bulk, plane)
+            for i in range(count):
+                out[i] = pack_end(bulk, field[i, :, cut], source[i, :, cut], beta[i, :, cut])
+            for i in range(0, count, 2):
+                first, second = beta[i, :, cut], turn(beta[i + 1, :, cut], 64)
+                out[count + i // 2] = jnp.where(left, second, first) if bulk == HIGH else jnp.where(left, first, second)
     lane = lax.axis_index("lane")
     first = (lax.axis_index("node") * lanes + lane) * count
     old_index = [jnp.int32(0)] * len(moves)
@@ -241,13 +297,20 @@
         for k, move in enumerate(moves):
             old_index[k] = jnp.where(step == move, i, old_index[k])
             new_slot[k] = jnp.where(step == move, slot, new_slot[k])
-    for out, (bulk, kept) in zip(outs, plan.values()):
-        unit = 3 * count if bulk is not None else 0
+    for (offset, (bulk, whole, kept)), out in zip(plan.items(), outs):
+        unit = count + count // 2 if bulk is not None else 0
+        low, high = part_lanes(LOW, plane), part_lanes(HIGH, plane)
+        if whole:
+            box = old_index[moves.index(offset)]
+            out[unit] = pack_whole(field[box, :, low], field[box, :, high])
+            out[unit + 1] = source[box, :, low]
+            out[unit + 2] = source[box, :, high]
+            unit += 3
         for move, part in kept:
             box = old_index[moves.index(move)]
-            for array in (field, source):
-                out[unit] = array[box, :, part_lanes(part, plane)]
-                unit += 1
+            cut = part_lanes(part, plane)
+            out[unit] = pack_end(part, field[box, :, cut], source[box, :, cut], field[box, :, cut])
+            unit += 1
     for i in range(count):
         labels[1, i] = -1
 
@@ -367,51 +430,100 @@
         for a in range(2):
             put(a, spot, halo, old[a][labels[4, k], :, part_lanes(part, plane)])
 
-    for offset, (bulk, kept) in plan.items():
+    left = lax.broadcasted_iota(jnp.int32, (side, 128), 1) < 64
+    y = lax.div(lax.broadcasted_iota(jnp.int32, (side, 128), 1), side)
+    for offset, (bulk, entire, kept) in plan.items():
         message = got[offset]
         unit = 0
         if bulk is not None:
             halo = low_halo if offset == below else high_halo
             for i in range(count):
-                put(2, (said(offset, i, 7), said(offset, i, 11)), halo, message[2 * count + i])
+                packed = message[i]
                 spot = spot_at(offset, said(offset, i, 9))
-                for a in range(2):
-                    put(a, spot, halo, message[a * count + i])
-            k = moves.index(offset)
-            spot, box = spot_here(said(offset, k, 8)), said(offset, k, 10)
-            for a in range(2):
-                put(a, spot, own_half[bulk], message[a * count + box])
-            unit = 3 * count
+                put(0, spot, halo, unpack_end(bulk, packed))
+                put(1, spot, halo, packed)
+                joint = message[count + i // 2]
+                if bulk == HIGH:
+                    layers = joint if i % 2 == 0 else turn(joint, 64)
+                    layers = jnp.where(y == 3, turn(packed, side), jnp.where(y < 3, 1.0, layers))
+                else:
+                    layers = joint if i % 2 == 0 else turn(joint, 64)
+                    layers = jnp.where(y == 4, turn(packed, -side), jnp.where(y > 4, 1.0, layers))
+                put(2, (said(offset, i, 7), said(offset, i, 11)), halo, layers)
+            unit = count + count // 2
+        if entire:
+            spot = spot_here(said(offset, moves.index(offset), 8))
+            low, high = unpack_whole(message[unit])
+            put(0, spot, own_half[LOW], low)
+            put(0, spot, own_half[HIGH], high)
+            put(1, spot, own_half[LOW], message[unit + 1])
+            put(1, spot, own_half[HIGH], message[unit + 2])
+            unit += 3
         for move, part in kept:
             slot = said(offset, moves.index(move), 8)
-            apart = (move - offset) % lanes
-            if apart == 0:
-                spot, where = spot_here(slot), own_half[part]
-            elif apart == 1:
+            if part == LOW:
                 spot, where = spot_at(above, slot), high_halo
             else:
                 spot, where = spot_at(below, slot), low_halo
-            for a in range(2):
-                put(a, spot, where, message[unit + a])
-            unit += 2
+            put(0, spot, where, unpack_end(part, message[unit]))
+            put(1, spot, where, message[unit])
+            unit += 1
 
     width = block.shape[3]
-    levels = lax.broadcasted_iota(jnp.int32, (8, width), 0)
     last = block.shape[2] - 8
-    for deep in range(BZB):
-        a, b, c = (block[k, deep, last : last + 8] for k in range(3))
-        up_first = jnp.where(levels < 3, pltpu.roll(b, 3, 0), a)
-        up_second = jnp.where(levels == 0, pltpu.roll(b, 4, 0), c)
-        a, b, c = (block[k, deep, 0:8] for k in range(3))
-        down_first = jnp.where(levels >= 5, pltpu.roll(b, 5, 0), a)
-        down_second = jnp.where(levels == 7, pltpu.roll(b, 4, 0), c)
-        for k in range(width // 128):
-            cut = slice(k * 128, (k + 1) * 128)
-            at = deep * 2 * (width // 128) + k
-            upward[at] = up_first[:, cut]
-            upward[at + width // 128] = up_second[:, cut]
-            downward[at] = down_first[:, cut]
-            downward[at + width // 128] = down_second[:, cut]
+    for message, start, up in ((upward, last, True), (downward, 0, False)):
+        for deep in range(0, BZB, 2):
+            tiles = []
+            sources = []
+            for d in (deep, deep + 1):
+                f, s, b = (block[k, d, start : start + 8] for k in range(3))
+                tiles.append(pack_rows(up, f, b))
+                sources.append(s)
+            tiles.append(pack_sources(up, *sources))
+            for k, tile in enumerate(tiles):
+                at = (deep // 2 * 3 + k) * 3
+                corner = slice(0, 128), slice(width - 128, width)
+                message[at] = jnp.where(left[0:8], tile[:, corner[1]], tile[:, corner[0]])
+                message[at + 1] = tile[:, 128:256]
+                message[at + 2] = tile[:, 256:384]
+
+
+def row_colours(width, side):
+    rows = lax.broadcasted_iota(jnp.int32, (8, width), 0)
+    cols = lax.broadcasted_iota(jnp.int32, (8, width), 1)
+    return rows, lax.rem(rows + lax.div(cols, side) + lax.rem(cols, side), 2)
+
+
+def fall(values, shift):
+    return pltpu.roll(values, shift % 8, 0)
+
+
+def pack_rows(up, field, beta):
+    rows, colour = row_colours(field.shape[1], SIDE)
+    if up:
+        pairs = jnp.where(colour == 1, field, fall(field, 1))
+        out = jnp.where(rows == 0, fall(pairs, 1), beta)
+        out = jnp.where(rows == 1, fall(pairs, 4), out)
+        return jnp.where(rows == 2, fall(pairs, 7), out)
+    pairs = jnp.where(colour == 1, field, fall(field, 7))
+    out = jnp.where(rows == 7, fall(pairs, 7), beta)
+    out = jnp.where(rows == 6, fall(pairs, 4), out)
+    return jnp.where(rows == 5, fall(pairs, 1), out)
+
+
+def unpack_rows(up, tile):
+    rows = lax.broadcasted_iota(jnp.int32, tile.shape, 0)
+    places = ((7, 7), (6, 6), (5, 4), (4, 3), (3, 1)) if up else ((0, 1), (1, 2), (2, 4), (3, 5), (4, 7))
+    field = tile
+    for row, shift in places:
+        field = jnp.where(rows == row, fall(tile, shift), field)
+    beta = jnp.where(rows < 3, 1.0, tile) if up else jnp.where(rows > 4, 1.0, tile)
+    return field, beta
+
+
+def pack_sources(up, first, second):
+    rows = lax.broadcasted_iota(jnp.int32, first.shape, 0)
+    return jnp.where(rows >= 4, first, fall(second, 4)) if up else jnp.where(rows < 4, first, fall(second, 4))
 
 
 def smooth_kernel(lanes, nodes, covered, labels, block, from_below, from_above, row_table, two_on, smoothed, coarse, flag,
@@ -421,7 +533,6 @@
     side = smoothed.shape[1]
     plane = smoothed.shape[2]
     half = plane // 2
-    tiles = width // 128
     node, lane = lax.axis_index("node"), lax.axis_index("lane")
     first_node, last_node = node == 0, node == nodes - 1
     first_lane, last_lane = lane == 0, lane == lanes - 1
@@ -441,17 +552,13 @@
         f[deep, 2 * PAD : top] = block[0, deep]
         b[deep, 2 * PAD : top] = block[2, deep]
         s[deep, 2 * PAD : top] = block[1, deep]
-        for message, start, below in ((from_below, PAD, True), (from_above, top, False)):
-            base = deep * 2 * tiles
-            first = jnp.concatenate([message[base + k] for k in range(tiles)], axis=1)
-            second = jnp.concatenate([message[base + tiles + k] for k in range(tiles)], axis=1)
-            if below:
-                src = jnp.where(rows8 >= 5, pltpu.roll(first, 5, 0), pltpu.roll(second, 4, 0))
-            else:
-                src = jnp.where(rows8 < 3, pltpu.roll(first, 3, 0), pltpu.roll(second, 4, 0))
-            f[deep, start : start + 8] = first
-            b[deep, start : start + 8] = jnp.where(rows8 == (0 if below else 7), 1.0, second)
-            s[deep, start : start + 8] = src
+        for message, start, up in ((from_below, PAD, True), (from_above, top, False)):
+            strips = []
+            for k in (deep % 2, 2):
+                at = (deep // 2 * 3 + k) * 3
+                strips.append(jnp.concatenate([message[at], message[at + 1], message[at + 2], message[at]], axis=1))
+            f[deep, start : start + 8], b[deep, start : start + 8] = unpack_rows(up, strips[0])
+            s[deep, start : start + 8] = strips[1] if deep % 2 == 0 else fall(strips[1], 4)
 
     def after(values):
         return pltpu.roll(values, width - side, 1)
@@ -613,7 +720,7 @@
     lanes, nodes = lax.axis_size("lane"), lax.axis_size("node")
     moves, plan = lane_plan(lanes)
     covered = lanes == 8 and nodes == 4
-    units = [(3 * count if bulk is not None else 0) + 2 * len(kept) + 1 for bulk, kept in plan.values()]
+    units = [plan_units(count, *parts) for parts in plan.values()]
     f32 = jnp.float32
     packed = pl.pallas_call(
         lambda *refs: pack_kernel(moves, plan, lanes, count, *refs),
@@ -625,12 +732,16 @@
         compiler_params=ROOM,
     )(target_box, neighbours, old_field, old_source, diffusivity)
     messages, labels, own_table = packed[:-2], packed[-2], packed[-1]
-    got = [
-        lax.ppermute(message, "lane", [(i, (i + offset) % lanes) for i in range(lanes)])
-        for offset, message in zip(plan, messages)
-    ]
+    got = {}
+    early = [offset for offset in plan if offset in moves]
+    for offset in early + [offset for offset in plan if offset not in moves]:
+        message = messages[list(plan).index(offset)]
+        if offset not in moves:
+            message, _ = lax.optimization_barrier((message, got[2]))
+        got[offset] = lax.ppermute(message, "lane", [(i, (i + offset) % lanes) for i in range(lanes)])
+    got = [got[offset] for offset in plan]
     width = 4 * half
-    strips = BZB * 2 * (width // 128) + 1
+    strips = BZB // 2 * 9 + 1
     block, upward, downward, row_table = pl.pallas_call(
         lambda *refs: assemble_kernel(moves, plan, lanes, count, *refs),
         name="assemble_block",

time: 40.7 us -> 37.3 us (0.916)
  waiting for transfers between devices: 13.4 us -> 7.24 us
  starting transfers between devices: 15.1 us -> 17.1 us
  Pallas kernels: 10.4 us -> 11.2 us
    ppermute x7, waiting for transfers between devices: 10.3 us -> 4.82 us  [fast_body(): lax.ppermute(message, 'lane', [(i, (i + offset) % lanes) for i in range(l...]
    ppermute x7, starting transfers between devices: 11.8 us -> 13.8 us  [fast_body(): lax.ppermute(message, 'lane', [(i, (i + offset) % lanes) for i in range(l...]
    pallas_call x1, Pallas kernels: 2.01 us -> 2.77 us  [fast_body(): pl.pallas_call(lambda *refs: pack_kernel(moves, plan, lanes, count, *refs...]
    ppermute x1, waiting for transfers between devices: 3.03 us -> 2.41 us  [fast_body(): lax.ppermute(row_table, 'node', [(i, (i + 2) % nodes) for i in range(node...]
where the time goes in v3:
time: 37.3 us; the launch traced here: 37.2 us
  starting transfers between devices  17.1 us (46%)
  Pallas kernels  11.2 us (30%)
  waiting for transfers between devices  7.24 us (19%)
  between operations  0.87 us (2%)
  loops' own time  0.76 us (2%)
    ppermute x7, starting transfers between devices, fast_body(): lax.ppermute(message, 'lane', [(i, (i + offset) % lanes) for i in range(l...  13.8 us
    pallas_call x1, Pallas kernels, fast_body(): pl.pallas_call(lambda *refs: smooth_kernel(lanes, nodes, covered, *refs),...  6.06 us
    ppermute x7, waiting for transfers between devices, fast_body(): lax.ppermute(message, 'lane', [(i, (i + offset) % lanes) for i in range(l...  4.82 us
    pallas_call x1, Pallas kernels, fast_body(): pl.pallas_call(lambda *refs: pack_kernel(moves, plan, lanes, count, *refs...  2.77 us
    ppermute x1, waiting for transfers between devices, fast_body(): lax.ppermute(row_table, 'node', [(i, (i + 2) % nodes) for i in range(node...  2.41 us
    pallas_call x1, Pallas kernels, fast_body(): pl.pallas_call(lambda *refs: assemble_kernel(moves, plan, lanes, count, *...  2.4 us
    ppermute x1, starting transfers between devices, fast_body(): lax.ppermute(downward, 'node', [(i, (i - 1) % nodes) for i in range(nodes)])  1.73 us
    ppermute x1, starting transfers between devices, fast_body(): lax.ppermute(row_table, 'node', [(i, (i + 2) % nodes) for i in range(node...  1.52 us
  transfers between devices with their start and end apart: 10, of which 3 were waited for; matrix products, arithmetic and copies ran while one was open for 0% of the time, Pallas kernels for 0%

profile of v3, /device:TPU:0, one launch (start us, length us, event | category | flops | bytes accessed | tf_op | source)
XLA Modules:
  0.0 37.2 jit_solution(14101449419053370655)
XLA Ops:
  0.6 0.0 copy-start.20
  0.7 2.8 %pack_moves.1 = (f32[17,16,128]{2,1,0:T(8,128)S(1)}, f32[5,16,128]{2,1,0:T(8,128)S(1)}, f32[3,16,128]{2,1,0:T(8,128)S(1)}, f32[4,16,128]{2,1,0:T(8,128)S(1)}, f3...) custom-call(s32[8]{0:T(128)} %refs_0_.1, ...), custom_call_target="tpu_custom_call" | custom-call | tf_op jit(solution)/shard_map/pack_moves/pallas_call | solution.py:725
  3.4 3.0 %collective-permute-start.20 = (f32[17,16,128]{2,1,0:T(8,128)S(1)}, f32[17,16,128]{2,1,0:T(8,128)S(1)}, u32[]{:S(2)}, u32[]{:S(2)}) collective-permute-start(f32[17,16,128]{2,1,0:T(8,128)S(1)} %get-tuple-element.67), channel_id=1, source_target_pairs={{0,1},{1,2},{2,3},{3,4},{4,5},{5,6},{6,7},{7,0},{8,9},{9,10},{10,1... | collective-permute-start | bytes 417800 | tf_op jit(solution)/shard_map/ppermute | solution.py:741
  6.4 3.1 %collective-permute-start.26 = (f32[17,16,128]{2,1,0:T(8,128)S(1)}, f32[17,16,128]{2,1,0:T(8,128)S(1)}, u32[]{:S(2)}, u32[]{:S(2)}) collective-permute-start(f32[17,16,128]{2,1,0:T(8,128)S(1)} %get-tuple-element.75), channel_id=1, source_target_pairs={{0,7},{1,0},{2,1},{3,2},{4,3},{5,4},{6,5},{7,6},{8,15},{9,8},{10,9... | collective-permute-start | bytes 417800 | tf_op jit(solution)/shard_map/ppermute | solution.py:741
  9.5 0.0 collective-permute-start.21
  9.5 2.5 %collective-permute-start.23 = (f32[4,16,128]{2,1,0:T(8,128)S(1)}, f32[4,16,128]{2,1,0:T(8,128)S(1)}, u32[]{:S(2)}, u32[]{:S(2)}) collective-permute-start(f32[4,16,128]{2,1,0:T(8,128)S(1)} %get-tuple-element.71), channel_id=1, source_target_pairs={{0,4},{1,5},{2,6},{3,7},{4,0},{5,1},{6,2},{7,3},{8,12},{9,13},{10,... | collective-permute-start | bytes 98312 | tf_op jit(solution)/shard_map/ppermute | solution.py:741
  12.0 1.3 %collective-permute-start.25 = (f32[5,16,128]{2,1,0:T(8,128)S(1)}, f32[5,16,128]{2,1,0:T(8,128)S(1)}, u32[]{:S(2)}, u32[]{:S(2)}) collective-permute-start(f32[5,16,128]{2,1,0:T(8,128)S(1)} %get-tuple-element.74), channel_id=1, source_target_pairs={{0,6},{1,7},{2,0},{3,1},{4,2},{5,3},{6,4},{7,5},{8,14},{9,15},{10,... | collective-permute-start | bytes 122888 | tf_op jit(solution)/shard_map/ppermute | solution.py:741
  13.4 3.0 %collective-permute-done.21.refs_6_ = f32[5,16,128]{2,1,0:T(8,128)S(1)} collective-permute-done((f32[5,16,128]{2,1,0:T(8,128)S(1)}, f32[5,16,128]{2,1,0:T(8,128)S(1)}, u32[]{:S(2)}, u32[]{:S(2)}) %collective-permute-start.21) | collective-permute-done | bytes 40992 | tf_op jit(solution)/shard_map/ppermute | solution.py:741
  16.4 0.0 collective-permute-start.22
  16.4 0.0 collective-permute-done.23.refs_8_
  16.4 3.8 %collective-permute-start.24 = (f32[3,16,128]{2,1,0:T(8,128)S(1)}, f32[3,16,128]{2,1,0:T(8,128)S(1)}, u32[]{:S(2)}, u32[]{:S(2)}) collective-permute-start(f32[3,16,128]{2,1,0:T(8,128)S(1)} %get-tuple-element.73), channel_id=1, source_target_pairs={{0,5},{1,6},{2,7},{3,0},{4,1},{5,2},{6,3},{7,4},{8,13},{9,14},{10,... | collective-permute-start | bytes 73736 | tf_op jit(solution)/shard_map/ppermute | solution.py:741
  20.2 0.0 collective-permute-done.25.refs_10_
  20.2 1.8 %collective-permute-done.22.refs_7_ = f32[3,16,128]{2,1,0:T(8,128)S(1)} collective-permute-done((f32[3,16,128]{2,1,0:T(8,128)S(1)}, f32[3,16,128]{2,1,0:T(8,128)S(1)}, u32[]{:S(2)}, u32[]{:S(2)}) %collective-permute-start.22) | collective-permute-done | bytes 24608 | tf_op jit(solution)/shard_map/ppermute | solution.py:741
  22.0 0.0 collective-permute-done.24.refs_9_
  22.0 0.0 collective-permute-done.20.refs_5_
  22.0 0.0 collective-permute-done.26.refs_11_
  22.0 2.4 %assemble_block.1 = (f32[3,5,32,512]{3,2,1,0:T(8,128)S(1)}, f32[19,8,128]{2,1,0:T(8,128)S(1)}, f32[19,8,128]{2,1,0:T(8,128)S(1)}, f32[8,128]{1,0:T(8,128)S(1)}) custom-call(s32[6,8]{1,0:T(8,128)S(1)} %get-tuple-element.65.refs_0_, f32[8,128]{1,0:T(8,128)S(1)} %get-tuple-element.66.refs_1_, f32[8,16,256]{2,1,0:T(8,128)S(1)} %copy-done.20, ...), custom_call_target="tpu_custom_call" | custom-call | tf_op jit(solution)/shard_map/assemble_block/pallas_call | solution.py:745
  24.4 0.1 collective-permute-start.27
  24.5 1.7 %collective-permute-start.28 = (f32[19,8,128]{2,1,0:T(8,128)S(1)}, f32[19,8,128]{2,1,0:T(8,128)S(1)}, u32[]{:S(2)}, u32[]{:S(2)}) collective-permute-start(f32[19,8,128]{2,1,0:T(8,128)S(1)} %get-tuple-element.78), channel_id=1, source_target_pairs={{0,24},{8,0},{16,8},{24,16},{1,25},{9,1},{17,9},{25,17},{2,26},{10... | collective-permute-start | bytes 233480 | tf_op jit(solution)/shard_map/ppermute | solution.py:763
  26.2 1.5 %collective-permute-start.29 = (f32[8,128]{1,0:T(8,128)S(1)}, f32[8,128]{1,0:T(8,128)S(1)}, u32[]{:S(2)}, u32[]{:S(2)}) collective-permute-start(f32[8,128]{1,0:T(8,128)S(1)} %get-tuple-element.79.refs_4_), channel_id=1, source_target_pairs={{0,16},{8,24},{16,0},{24,8},{1,17},{9,25},{17,1},{25,9},{2,18},{10... | collective-permute-start | bytes 12296 | tf_op jit(solution)/shard_map/ppermute | solution.py:764
  27.8 2.4 %collective-permute-done.29.refs_5_ = f32[8,128]{1,0:T(8,128)S(1)} collective-permute-done((f32[8,128]{1,0:T(8,128)S(1)}, f32[8,128]{1,0:T(8,128)S(1)}, u32[]{:S(2)}, u32[]{:S(2)}) %collective-permute-start.29) | collective-permute-done | bytes 4128 | tf_op jit(solution)/shard_map/ppermute | solution.py:764
  30.2 0.0 collective-permute-done.27.refs_2_
  30.2 6.1 %smooth_block.1 = (f32[8,16,256]{2,1,0:T(8,128)}, f32[8,512]{1,0:T(8,128)}, s32[1,1]{1,0:T(1,128)}) custom-call(s32[6,8]{1,0:T(8,128)S(1)} %get-tuple-element.65.refs_0_, f32[3,5,32,512]{3,2,1,0:T(8,128)S(1)} %get-tuple-element.76.refs_1_, f32[19,8,128]{2,1,0:T(8,128)S(1)} %collective-permute-done.27.refs_2_, ...), custom_call_target="tpu_custom_call" | custom-call | tf_op jit(solution)/shard_map/smooth_block/pallas_call | solution.py:767
  36.3 0.8 %while.12 = (f32[8,16,256]{2,1,0:T(8,128)}, f32[8,512]{1,0:T(8,128)}, s32[]{:T(128)}, s32[8]{0:T(128)}, f32[8,16,256]{2,1,0:T(8,128)S(1)}, /*index=5*/f32[8,16,2...) while((f32[8,16,256]{2,1,0:T(8,128)}, f32[8,512]{1,0:T(8,128)}, ...), condition=%region_7.8_spmd.clone, body=%region_0.7_spmd.sunk.clone | while | flops 21889904 | bytes 77572904 | solution.py:788
  (4 shorter events, 0.0 us)
Async XLA Ops:
  0.6 21.4 %copy-start = (f32[8,16,256]{2,1,0:T(8,128)S(1)}, f32[8,16,256]{2,1,0:T(8,128)}, u32[]{:S(2)}) copy-start(f32[8,16,256]{2,1,0:T(8,128)} %refs_4_.3) | copy-start | bytes 393220
  0.6 21.4 %copy-start.20 = (f32[8,16,256]{2,1,0:T(8,128)S(1)}, f32[8,16,256]{2,1,0:T(8,128)}, u32[]{:S(2)}) copy-start(f32[8,16,256]{2,1,0:T(8,128)} %refs_2_.3) | copy-start | bytes 393220
  3.4 18.6 %collective-permute-start.20 = (f32[17,16,128]{2,1,0:T(8,128)S(1)}, f32[17,16,128]{2,1,0:T(8,128)S(1)}, u32[]{:S(2)}, u32[]{:S(2)}) collective-permute-start(f32[17,16,128]{2,1,0:T(8,128)S(1)} %get-tuple-element.67), channel_id=1, source_target_pairs={{0,1},{1,2},{2,3},{3,4},{4,5},{5,6},{6,7},{7,0},{8,9},{9,10},{10,1... | collective-permute-start | bytes 417800 | tf_op jit(solution)/shard_map/ppermute | solution.py:741
  6.4 15.6 %collective-permute-start.26 = (f32[17,16,128]{2,1,0:T(8,128)S(1)}, f32[17,16,128]{2,1,0:T(8,128)S(1)}, u32[]{:S(2)}, u32[]{:S(2)}) collective-permute-start(f32[17,16,128]{2,1,0:T(8,128)S(1)} %get-tuple-element.75), channel_id=1, source_target_pairs={{0,7},{1,0},{2,1},{3,2},{4,3},{5,4},{6,5},{7,6},{8,15},{9,8},{10,9... | collective-permute-start | bytes 417800 | tf_op jit(solution)/shard_map/ppermute | solution.py:741
  9.5 6.9 %collective-permute-start.21 = (f32[5,16,128]{2,1,0:T(8,128)S(1)}, f32[5,16,128]{2,1,0:T(8,128)S(1)}, u32[]{:S(2)}, u32[]{:S(2)}) collective-permute-start(f32[5,16,128]{2,1,0:T(8,128)S(1)} %get-tuple-element.68), channel_id=1, source_target_pairs={{0,2},{1,3},{2,4},{3,5},{4,6},{5,7},{6,0},{7,1},{8,10},{9,11},{10,... | collective-permute-start | bytes 122888 | tf_op jit(solution)/shard_map/ppermute | solution.py:741
  9.5 6.9 %collective-permute-start.23 = (f32[4,16,128]{2,1,0:T(8,128)S(1)}, f32[4,16,128]{2,1,0:T(8,128)S(1)}, u32[]{:S(2)}, u32[]{:S(2)}) collective-permute-start(f32[4,16,128]{2,1,0:T(8,128)S(1)} %get-tuple-element.71), channel_id=1, source_target_pairs={{0,4},{1,5},{2,6},{3,7},{4,0},{5,1},{6,2},{7,3},{8,12},{9,13},{10,... | collective-permute-start | bytes 98312 | tf_op jit(solution)/shard_map/ppermute | solution.py:741
  12.0 8.2 %collective-permute-start.25 = (f32[5,16,128]{2,1,0:T(8,128)S(1)}, f32[5,16,128]{2,1,0:T(8,128)S(1)}, u32[]{:S(2)}, u32[]{:S(2)}) collective-permute-start(f32[5,16,128]{2,1,0:T(8,128)S(1)} %get-tuple-element.74), channel_id=1, source_target_pairs={{0,6},{1,7},{2,0},{3,1},{4,2},{5,3},{6,4},{7,5},{8,14},{9,15},{10,... | collective-permute-start | bytes 122888 | tf_op jit(solution)/shard_map/ppermute | solution.py:741
  16.4 5.6 %collective-permute-start.22 = (f32[3,16,128]{2,1,0:T(8,128)S(1)}, f32[3,16,128]{2,1,0:T(8,128)S(1)}, u32[]{:S(2)}, u32[]{:S(2)}) collective-permute-start(f32[3,16,128]{2,1,0:T(8,128)S(1)} %get-tuple-element.70), channel_id=1, source_target_pairs={{0,3},{1,4},{2,5},{3,6},{4,7},{5,0},{6,1},{7,2},{8,11},{9,12},{10,... | collective-permute-start | bytes 73736 | tf_op jit(solution)/shard_map/ppermute | solution.py:741
  16.4 5.6 %collective-permute-start.24 = (f32[3,16,128]{2,1,0:T(8,128)S(1)}, f32[3,16,128]{2,1,0:T(8,128)S(1)}, u32[]{:S(2)}, u32[]{:S(2)}) collective-permute-start(f32[3,16,128]{2,1,0:T(8,128)S(1)} %get-tuple-element.73), channel_id=1, source_target_pairs={{0,5},{1,6},{2,7},{3,0},{4,1},{5,2},{6,3},{7,4},{8,13},{9,14},{10,... | collective-permute-start | bytes 73736 | tf_op jit(solution)/shard_map/ppermute | solution.py:741
  24.4 5.7 %collective-permute-start.27 = (f32[19,8,128]{2,1,0:T(8,128)S(1)}, f32[19,8,128]{2,1,0:T(8,128)S(1)}, u32[]{:S(2)}, u32[]{:S(2)}) collective-permute-start(f32[19,8,128]{2,1,0:T(8,128)S(1)} %get-tuple-element.77), channel_id=1, source_target_pairs={{0,8},{8,16},{16,24},{24,0},{1,9},{9,17},{17,25},{25,1},{2,10},{10... | collective-permute-start | bytes 233480 | tf_op jit(solution)/shard_map/ppermute | solution.py:762
  24.5 5.7 %collective-permute-start.28 = (f32[19,8,128]{2,1,0:T(8,128)S(1)}, f32[19,8,128]{2,1,0:T(8,128)S(1)}, u32[]{:S(2)}, u32[]{:S(2)}) collective-permute-start(f32[19,8,128]{2,1,0:T(8,128)S(1)} %get-tuple-element.78), channel_id=1, source_target_pairs={{0,24},{8,0},{16,8},{24,16},{1,25},{9,1},{17,9},{25,17},{2,26},{10... | collective-permute-start | bytes 233480 | tf_op jit(solution)/shard_map/ppermute | solution.py:763
  26.2 3.9 %collective-permute-start.29 = (f32[8,128]{1,0:T(8,128)S(1)}, f32[8,128]{1,0:T(8,128)S(1)}, u32[]{:S(2)}, u32[]{:S(2)}) collective-permute-start(f32[8,128]{1,0:T(8,128)S(1)} %get-tuple-element.79.refs_4_), channel_id=1, source_target_pairs={{0,16},{8,24},{16,0},{24,8},{1,17},{9,25},{17,1},{25,9},{2,18},{10... | collective-permute-start | bytes 12296 | tf_op jit(solution)/shard_map/ppermute | solution.py:764

commit v4 on v3

v4 whole, which is shorter than its diff:
```python
import jax
import jax.numpy as jnp
from jax import lax
from jax.experimental import pallas as pl
from jax.experimental.pallas import tpu as pltpu
from jax.sharding import PartitionSpec as P

SWEEPS = 2


OPPOSITE = (1, 0, 3, 2, 5, 4)


def with_halo(block, sides, width):
    for axis, dim in sides:
        count = lax.axis_size(axis)
        forward = [(i, i + 1) for i in range(count - 1)]
        backward = [(target, source) for source, target in forward]
        low = lax.ppermute(
            lax.slice_in_dim(block, block.shape[dim] - width, None, axis=dim), axis, forward
        )
        high = lax.ppermute(lax.slice_in_dim(block, 0, width, axis=dim), axis, backward)
        block = jnp.concatenate([low, block, high], axis=dim)
    return block


def face_layers(values):
    boxes, side, plane = values.shape
    return jnp.stack(
        [
            values[:, 0],
            values[:, side - 1],
            values[:, :, :side].reshape(boxes, plane),
            values[:, :, plane - side :].reshape(boxes, plane),
            values[:, :, 0::side].reshape(boxes, plane),
            values[:, :, side - 1 :: side].reshape(boxes, plane),
        ],
        axis=1,
    )


def near_values(values, ghost):
    boxes, side, plane = values.shape
    lower_x = jnp.concatenate([ghost[:, 0][:, None, :], values[:, :-1]], axis=1)
    upper_x = jnp.concatenate([values[:, 1:], ghost[:, 1][:, None, :]], axis=1)
    lower_y = jnp.concatenate(
        [ghost[:, 2].reshape(boxes, side, side), values[:, :, : plane - side]], axis=2
    )
    upper_y = jnp.concatenate([values[:, :, side:], ghost[:, 3].reshape(boxes, side, side)], axis=2)
    depth = jnp.arange(plane) % side
    lower_z = jnp.where(
        depth == 0,
        jnp.repeat(ghost[:, 4].reshape(boxes, side, side), side, axis=2),
        jnp.roll(values, 1, axis=2),
    )
    upper_z = jnp.where(
        depth == side - 1,
        jnp.repeat(ghost[:, 5].reshape(boxes, side, side), side, axis=2),
        jnp.roll(values, -1, axis=2),
    )
    return [lower_x, upper_x, lower_y, upper_y, lower_z, upper_z]


def coefficients(diffusivity, beside):
    return [2.0 * diffusivity * other / (diffusivity + other) for other in beside]


def relax(values, source, couplings, beside, chosen):
    total = couplings[0]
    summed = source + couplings[0] * beside[0]
    for face in range(1, 6):
        total = total + couplings[face]
        summed = summed + couplings[face] * beside[face]
    return jnp.where(chosen, summed / total, values)


def defect_of(values, source, couplings, beside):
    total = couplings[0]
    summed = source + couplings[0] * beside[0]
    for face in range(1, 6):
        total = total + couplings[face]
        summed = summed + couplings[face] * beside[face]
    return summed - total * values


def colour_of(side, plane):
    rows = jnp.arange(side)[:, None]
    cells = jnp.arange(plane)[None, :]
    return (rows + cells // side + cells % side) % 2


def restrict(values):
    boxes, side, plane = values.shape
    half = side // 2
    paired = values.reshape(boxes, half, 2, plane).sum(axis=2)
    cells = jnp.arange(plane)
    coarse_cols = cells // side // 2 * half + cells % side // 2
    pooling = (coarse_cols[:, None] == jnp.arange(half * half)[None, :]).astype(jnp.float32)
    summed = jnp.einsum("bxp,pq->bxq", paired, pooling, precision=lax.Precision.HIGHEST)
    return (0.125 * summed).reshape(boxes, half * half * half)


def place(settled, arrived, tags):
    count = settled.shape[0]
    return settled.at[jnp.where(tags > 0, tags - 1, count)].set(arrived, mode="drop")


def general_body(old_field, old_source, diffusivity, target_box, neighbours):
    count, side, plane = old_field.shape
    lane_count = lax.axis_size("lane")
    lane_here = lax.axis_index("lane")
    own_device = lax.axis_index("node") * lane_count + lane_here
    dest_device = target_box // count
    dest_slot = target_box % count
    staying = dest_device == own_device
    cargo = jnp.stack([old_field, old_source], axis=1)
    settled = jnp.zeros_like(cargo).at[jnp.where(staying, dest_slot, count)].set(cargo, mode="drop")
    slots = jnp.arange(count)
    peers = own_device - lane_here + jnp.arange(lane_count)
    chosen = (dest_device[None, :] == peers[:, None]) & jnp.logical_not(staying)[None, :]
    filled = jnp.any(chosen, axis=1)
    picked = jnp.sum(jnp.where(chosen, slots[None, :], 0), axis=1)
    parcels = jnp.where(filled[:, None, None, None], cargo[picked], 0.0)
    labels = jnp.where(filled, jnp.sum(jnp.where(chosen, dest_slot[None, :], 0), axis=1) + 1, 0)
    arrived, tags = (
        lax.all_to_all(parcels, "lane", split_axis=0, concat_axis=0, tiled=True),
        lax.all_to_all(labels, "lane", split_axis=0, concat_axis=0, tiled=True),
    )
    settled = place(settled, arrived, tags)
    field = settled[:, 0]
    source = settled[:, 1]
    present = neighbours >= 0
    near_device = jnp.where(present, neighbours // count, own_device)
    local_row = neighbours % count * 6 + jnp.array(OPPOSITE, jnp.int32)[None, :]
    across = near_device - own_device
    anchor = jnp.where(
        across == -lane_count,
        1,
        jnp.where(
            across == lane_count, 2, jnp.where(across == -1, 3, jnp.where(across == 1, 4, 0))
        ),
    )
    index = anchor * (count * 6) + local_row
    width_out = count * 6

    def departing_boxes(layers):
        return layers.reshape(count * 6, plane)

    def incoming(received, start):
        return jnp.concatenate(
            [
                received[0, 1, start : start + width_out],
                received[2, 1, start : start + width_out],
                received[1, 0, start : start + width_out],
                received[1, 2, start : start + width_out],
            ],
            axis=0,
        )

    def trade(rows):
        return with_halo(rows[None, None], (("node", 0), ("lane", 1)), 1)

    def ghosts(layers, remote_rows, fallback):
        table = jnp.concatenate([layers.reshape(count * 6, plane), remote_rows], axis=0)
        return jnp.where(present[..., None], table[index], fallback)

    beta_layers = face_layers(diffusivity)
    layers = face_layers(field)
    received = trade(
        jnp.concatenate([departing_boxes(layers), departing_boxes(beta_layers)], axis=0)
    )
    beta_ghost = ghosts(beta_layers, incoming(received, width_out), beta_layers)
    couplings = coefficients(diffusivity, near_values(diffusivity, beta_ghost))
    colour = colour_of(side, plane)
    for sweep in range(SWEEPS):
        for colour_id in (0, 1):
            if sweep + colour_id > 0:
                layers = face_layers(field)
                received = trade(departing_boxes(layers))
            ghost = ghosts(layers, incoming(received, 0), jnp.zeros_like(layers))
            field = relax(field, source, couplings, near_values(field, ghost), colour == colour_id)
    layers = face_layers(field)
    received = trade(departing_boxes(layers))
    ghost = ghosts(layers, incoming(received, 0), jnp.zeros_like(layers))
    coarse = restrict(defect_of(field, source, couplings, near_values(field, ghost)))
    return (field, coarse)


BXD = 2
BZB = 4
PAD = 8
SIDE = 16
LOW, HIGH = "low", "high"


def lane_plan(lanes):
    half = lanes // 2
    moves = [1, lanes - 1, 2, lanes - 2, half]
    ends = {}
    for move in moves:
        for offset, part in ((move + 1, HIGH), (move - 1, LOW)):
            ends.setdefault(offset % lanes, []).append((move, part))
    bulk = {1: HIGH, lanes - 1: LOW}
    plan = {}
    for offset in sorted(set(moves) | set(ends)):
        if offset:
            plan[offset] = (bulk.get(offset), offset in moves, ends.get(offset, []))
    return moves, plan


def plan_units(count, bulk, whole, kept):
    return (count + count // 2 if bulk is not None else 0) + (3 if whole else 0) + len(kept) + 1


def cell_lanes(side):
    rows = lax.broadcasted_iota(jnp.int32, (side, 128), 0)
    cols = lax.broadcasted_iota(jnp.int32, (side, 128), 1)
    black = lax.rem(rows + lax.div(cols, side) + lax.rem(cols, side), 2) == 1
    return cols, black


def turn(values, shift):
    return pltpu.roll(values, shift % values.shape[-1], values.ndim - 1)


def pack_end(part, field, source, beta):
    side = field.shape[0]
    cols, black = cell_lanes(side)
    y = lax.div(cols, side)
    if part == HIGH:
        pairs = jnp.where(black, field, turn(field, side))
        out = jnp.where(y >= 4, source, pairs)
        out = jnp.where(y == 2, turn(beta, -side), out)
        out = jnp.where(y == 1, turn(pairs, -4 * side), out)
        return jnp.where(y == 0, turn(pairs, side), out)
    pairs = jnp.where(black, field, turn(field, -side))
    out = jnp.where(y < 4, source, pairs)
    out = jnp.where(y == 5, turn(beta, side), out)
    out = jnp.where(y == 6, turn(pairs, 4 * side), out)
    return jnp.where(y == 7, turn(pairs, -side), out)


def unpack_end(part, packed):
    side = packed.shape[0]
    y = lax.div(lax.broadcasted_iota(jnp.int32, packed.shape, 1), side)
    out = packed
    places = ((7, 7), (6, 6), (5, 4), (4, 3)) if part == HIGH else ((0, 1), (1, 2), (2, 4), (3, 5))
    for layer, shift in places:
        out = jnp.where(y == layer, turn(packed, shift * side), out)
    return out


def pack_whole(low, high):
    side = low.shape[0]
    cols, black = cell_lanes(side)
    even = lax.rem(lax.div(cols, side), 2) == 0
    low = jnp.where(black, low, turn(low, -side))
    high = jnp.where(black, high, turn(high, -side))
    return jnp.where(even, low, turn(high, side))


def unpack_whole(packed):
    side = packed.shape[0]
    even = lax.rem(lax.div(lax.broadcasted_iota(jnp.int32, packed.shape, 1), side), 2) == 0
    return jnp.where(even, packed, turn(packed, side)), jnp.where(even, turn(packed, -side), packed)


def part_lanes(part, plane):
    return slice(0, plane // 2) if part == LOW else slice(plane // 2, plane)


def pack_kernel(moves, plan, lanes, count, *refs):
    target, near = refs[:2]
    outs = refs[7 : 7 + len(plan)]
    held_here = refs[7 + len(plan) : 12 + len(plan)]
    table, slots, sems = refs[12 + len(plan) :]
    fetch = [pltpu.make_async_copy(src, dst, sems.at[k]) for k, (src, dst) in enumerate(zip(refs[2:7], held_here))]
    for copy in fetch:
        copy.start()
    field, source, beta = held_here[:3]
    side, plane = field.shape[1:]
    half = plane // 2
    lane = lax.axis_index("lane")
    first = (lax.axis_index("node") * lanes + lane) * count
    old_index = [jnp.int32(0)] * len(moves)
    new_slot = [jnp.int32(-1)] * len(moves)
    stay = []
    for i in range(count):
        there = target[i]
        slot = lax.rem(there, count)
        step = lax.rem(lax.rem(lax.div(there, count), lanes) - lane + lanes, lanes)
        stay.append(jnp.where(step == 0, slot, -1))
        for k, move in enumerate(moves):
            old_index[k] = jnp.where(step == move, i, old_index[k])
            new_slot[k] = jnp.where(step == move, slot, new_slot[k])
    for i in range(count):
        slots[i] = -1

    def local(index, face):
        there = near[index, face]
        inside = (there >= first) & (there < first + count)
        return inside, jnp.clip(there - first, 0, count - 1)

    place = []
    for i in range(count):
        inside, below = local(i, 0)
        depth = jnp.int32(0)
        live, at = local(i, 4)
        for _ in range(BZB - 1):
            depth = depth + jnp.where(live, 1, 0)
            further, onward = local(at, 4)
            live, at = live & further, onward
        spot = jnp.where(inside, BZB, 0) + depth
        place.append((depth, jnp.where(inside, side, 0)))
        slots[spot] = i
    rows = lax.broadcasted_iota(jnp.int32, (8, 128), 0)
    cols = lax.broadcasted_iota(jnp.int32, (8, 128), 1)
    spots = rows * 128 + cols
    held = jnp.zeros((8, 128), jnp.int32)

    def put(held, row, col, value):
        return jnp.where(spots == row * 128 + col, value, held)

    for i in range(count):
        slot = slots[i]
        held = put(held, i, 12, jnp.maximum(slot, 0))
        held = put(held, i, 0, jnp.where(slot < 0, -7, first + slot))
        for face in range(6):
            held = put(held, i, 1 + face, near[jnp.maximum(slot, 0), face])
        held = put(held, i, 7, place[i][0])
        held = put(held, i, 11, place[i][1])
        held = put(held, i, 9, stay[i])
    for k in range(len(moves)):
        held = put(held, k, 8, new_slot[k])
        held = put(held, k, 10, old_index[k])
    table[...] = held.astype(jnp.float32)
    for copy in fetch:
        copy.wait()
    left = lax.broadcasted_iota(jnp.int32, (side, 128), 1) < 64
    for out, (bulk, whole, kept) in zip(outs, plan.values()):
        if bulk is not None:
            cut = part_lanes(bulk, plane)
            for i in range(count):
                out[i] = pack_end(bulk, field[i, :, cut], source[i, :, cut], beta[i, :, cut])
            for i in range(0, count, 2):
                one, two = beta[i, :, cut], turn(beta[i + 1, :, cut], 64)
                out[count + i // 2] = jnp.where(left, two, one) if bulk == HIGH else jnp.where(left, one, two)
    for (offset, (bulk, whole, kept)), out in zip(plan.items(), outs):
        unit = count + count // 2 if bulk is not None else 0
        low, high = part_lanes(LOW, plane), part_lanes(HIGH, plane)
        if whole:
            box = old_index[moves.index(offset)]
            out[unit] = pack_whole(field[box, :, low], field[box, :, high])
            out[unit + 1] = source[box, :, low]
            out[unit + 2] = source[box, :, high]
            unit += 3
        for move, part in kept:
            box = old_index[moves.index(move)]
            cut = part_lanes(part, plane)
            out[unit] = pack_end(part, field[box, :, cut], source[box, :, cut], field[box, :, cut])
            unit += 1
    for out in outs:
        out[out.shape[0] - 1, 0:8] = table[...]


def assemble_kernel(moves, plan, lanes, count, *refs):
    own_table, field, source, beta = refs[:4]
    got = dict(zip(plan, refs[4 : 4 + len(plan)]))
    block, fifth, upward, downward, row_table, low_side, high_side, tables, table_sems = refs[4 + len(plan) :]
    side, plane = field.shape[1:]
    half = plane // 2
    order = list(plan) + [0]

    def table_of(offset):
        return got[offset].at[got[offset].shape[0] - 1, 0:8] if offset else own_table

    fetch = [
        pltpu.make_async_copy(table_of(offset), tables.at[k], table_sems.at[k]) for k, offset in enumerate(order)
    ]
    for copy in fetch:
        copy.start()

    cols = lax.broadcasted_iota(jnp.int32, (8, 128), 1)
    shown = [offset for offset in plan if lanes == 8 or offset in (1, lanes - 1)]
    joined = jnp.where(cols < 8, own_table[...], 0.0)
    for offset in shown:
        at = offset if offset < 7 else 7
        joined = joined + pltpu.roll(jnp.where(cols < 8, table_of(offset)[...], 0.0), 8 * at, 1)
    joined = joined + pltpu.roll(joined, 64, 1)
    row_table[...] = joined
    upward[upward.shape[0] - 1] = joined
    downward[downward.shape[0] - 1] = joined

    for copy in fetch:
        copy.wait()

    def said(offset, row, col):
        return tables[order.index(offset), row, col].astype(jnp.int32)

    def spot_at(offset, slot):
        at = jnp.maximum(slot, 0)
        return jnp.where(slot >= 0, said(offset, at, 7), BZB), jnp.where(slot >= 0, said(offset, at, 11), 0)

    def put(ref, array, spot, values, where=slice(None)):
        deep, row = spot
        ref[array, deep, pl.ds(pl.multiple_of(row, side), side), where] = values

    low, high, whole = slice(0, half), slice(half, plane), slice(0, plane)
    for i in range(count):
        put(block, 2, (said(0, i, 7), said(0, i, 11)), beta[i], whole)
        spot = spot_at(0, said(0, i, 9))
        put(block, 0, spot, field[i], whole)
        put(block, 1, spot, source[i], whole)

    below, above = 1, lanes - 1
    sides = {HIGH: (low_side, below, side), LOW: (high_side, above, -side)}

    def put_end(part, slot, layers, raw, sources):
        ref, offset, shift = sides[part]
        spot = spot_at(offset, slot)
        put(ref, 0, spot, layers)
        put(ref, 1, spot, sources)
        put(ref, 3, spot, turn(raw, shift))

    for move, part in ((1, LOW), (lanes - 1, HIGH)):
        k = moves.index(move)
        box, cut = said(0, k, 10), part_lanes(part, plane)
        raw = field[box, :, cut]
        put_end(part, said(0, k, 8), raw, raw, source[box, :, cut])

    for offset, (bulk, entire, kept) in plan.items():
        message = got[offset]
        unit = 0
        if bulk is not None:
            ref, _, shift = sides[bulk]
            for i in range(count):
                packed = message[i]
                put_end(bulk, said(offset, i, 9), unpack_end(bulk, packed), packed, packed)
                joint = message[count + i // 2]
                spot = said(offset, i, 7), said(offset, i, 11)
                put(ref, 2, spot, joint if i % 2 == 0 else turn(joint, 64))
                put(ref, 4, spot, turn(packed, 2 * shift))
            unit = count + count // 2
        if entire:
            spot = spot_at(0, said(offset, moves.index(offset), 8))
            first, second = unpack_whole(message[unit])
            put(block, 0, spot, first, low)
            put(block, 0, spot, second, high)
            put(block, 1, spot, message[unit + 1], low)
            put(block, 1, spot, message[unit + 2], high)
            unit += 3
        for move, part in kept:
            packed = message[unit]
            put_end(part, said(offset, moves.index(move), 8), unpack_end(part, packed), packed, packed)
            unit += 1

    rows, width = block.shape[2:]
    left = lax.broadcasted_iota(jnp.int32, (rows, 128), 1) < 64
    for d in range(BZB):
        for k in range(3):
            block[k, d, :, plane:width] = jnp.where(left, high_side[k, d], low_side[k, d])
        for k in range(2):
            fifth[k, d] = jnp.where(left, high_side[3 + k, d], low_side[3 + k, d])
    for message, start, up in ((upward, rows - 8, True), (downward, 0, False)):
        for deep in range(0, BZB, 2):
            tiles = []
            sources = []
            for d in (deep, deep + 1):
                f, s, b = (block[k, d, start : start + 8] for k in range(3))
                tiles.append(pack_rows(up, f, b))
                sources.append(s)
            tiles.append(pack_sources(up, *sources))
            for k, tile in enumerate(tiles):
                for part in range(width // 128):
                    message[(deep // 2 * 3 + k) * 3 + part] = tile[:, part * 128 : (part + 1) * 128]


def row_colours(width, side):
    rows = lax.broadcasted_iota(jnp.int32, (8, width), 0)
    cols = lax.broadcasted_iota(jnp.int32, (8, width), 1)
    return rows, lax.rem(rows + lax.div(cols, side) + lax.rem(cols, side), 2)


def fall(values, shift):
    return pltpu.roll(values, shift % 8, 0)


def pack_rows(up, field, beta):
    rows, colour = row_colours(field.shape[1], SIDE)
    if up:
        pairs = jnp.where(colour == 1, field, fall(field, 1))
        out = jnp.where(rows == 0, fall(pairs, 1), beta)
        out = jnp.where(rows == 1, fall(pairs, 4), out)
        return jnp.where(rows == 2, fall(pairs, 7), out)
    pairs = jnp.where(colour == 1, field, fall(field, 7))
    out = jnp.where(rows == 7, fall(pairs, 7), beta)
    out = jnp.where(rows == 6, fall(pairs, 4), out)
    return jnp.where(rows == 5, fall(pairs, 1), out)


def unpack_rows(below, above):
    rows = lax.broadcasted_iota(jnp.int32, below.shape, 0)
    field = fall(above, 1)
    for row, tile, shift in ((1, above, 2), (2, above, 4), (3, above, 5), (4, below, 3), (5, below, 4), (6, below, 6), (7, below, 7)):
        field = jnp.where(rows == row, fall(tile, shift), field)
    beta = jnp.where(rows < 4, above, below)
    fifth_field = jnp.where(rows < 4, fall(above, 6), fall(below, 2))
    fifth_beta = jnp.where(rows < 4, fall(above, 7), fall(below, 1))
    return field, beta, fifth_field, fifth_beta


def pack_sources(up, first, second):
    rows = lax.broadcasted_iota(jnp.int32, first.shape, 0)
    return jnp.where(rows >= 4, first, fall(second, 4)) if up else jnp.where(rows < 4, first, fall(second, 4))


class Stencil:
    def __init__(self, width, side, plane, lanes, nodes):
        self.width, self.side, self.plane = width, side, plane
        node, lane = lax.axis_index("node"), lax.axis_index("lane")
        self.first_node, self.last_node = node == 0, node == nodes - 1
        self.rows, self.colour = row_colours(width, side)
        cols = lax.broadcasted_iota(jnp.int32, (8, width), 1)
        depth = lax.rem(cols, side)
        self.at_front, self.at_back = depth == 0, depth == side - 1
        first_lane, last_lane = lane == 0, lane == lanes - 1
        self.low_edge = (cols < side) & first_lane
        self.high_edge = (cols >= plane - side) & (cols < plane) & last_lane
        self.seam = (cols >= plane + 3 * side) & (cols < plane + 4 * side)
        self.no_link = ((cols >= width - side) & first_lane) | self.high_edge | self.seam

    def after(self, values):
        return pltpu.roll(values, self.width - self.side, 1)

    def before(self, values):
        return pltpu.roll(values, self.side, 1)

    def beyond_z(self, values, afters):
        out = []
        for deep in range(BZB):
            joined = values[deep] if deep == 0 else jnp.where(self.at_back, afters[deep - 1], values[deep])
            out.append(pltpu.roll(joined, 1, 1))
        return out

    def ahead_z(self, values, befores):
        out = []
        for deep in range(BZB):
            joined = values[deep] if deep == BZB - 1 else jnp.where(self.at_front, befores[deep + 1], values[deep])
            out.append(pltpu.roll(joined, self.width - 1, 1))
        return out

    def across(self, held):
        befores = [self.before(v) for v in held]
        afters = [self.after(v) for v in held]
        aheads = self.ahead_z(held, befores)
        ky = [jnp.where(self.no_link, 0.0, mean(held[d], afters[d])) for d in range(BZB)]
        kz = [mean(held[d], aheads[d]) for d in range(BZB)]
        kz[BZB - 1] = jnp.where(self.at_back, 0.0, kz[BZB - 1])
        kzl = self.beyond_z(kz, [self.after(v) for v in kz])
        kzl[0] = jnp.where(self.at_front, 0.0, kzl[0])
        return [self.before(v) for v in ky], ky, kzl, kz

    def edges(self, d, held):
        out = jnp.where(self.low_edge | self.high_edge, held, 0.0)
        if d == 0:
            out = out + jnp.where(self.at_front, held, 0.0)
        if d == BZB - 1:
            out = out + jnp.where(self.at_back, held, 0.0)
        return out

    def sums(self, held, lowers, uppers, coefficient):
        afters = [self.after(v) for v in held]
        befores = [self.before(v) for v in held]
        behind = self.beyond_z(held, afters)
        aheads = self.ahead_z(held, befores)
        out = []
        for d in range(BZB):
            s, xl, xu, yl, yu, zl, zu = coefficient(d)
            part = s + xl * lowers[d] + xu * uppers[d]
            part = part + (yl * befores[d] + yu * afters[d])
            out.append(part + (zl * behind[d] + zu * aheads[d]))
        return out


def mean(one_side, other):
    return 2.0 * one_side * other / (one_side + other)


def couple_kernel(lanes, nodes, plane, block, fifth, f, s, xl, xu, yl, yu, zl, zu, total, inverse):
    width, own_rows = block.shape[3], block.shape[2]
    grid = Stencil(width, SIDE, plane, lanes, nodes)
    cols = lax.broadcasted_iota(jnp.int32, (8, 128), 1)
    seam = (cols >= 3 * SIDE) & (cols < 5 * SIDE)
    for r in range(0, own_rows, 8):
        here = slice(r, r + 8)
        held = [block[2, d, here] for d in range(BZB)]
        across = grid.across(held)
        for ref, values in zip((yl, yu, zl, zu), across):
            for d in range(BZB):
                ref[d, here] = values[d]
        for d in range(BZB):
            f[d, here] = block[0, d, here]
            if r + 8 < own_rows:
                xu[d, here] = mean(held[d], block[2, d, r + 1 : r + 9])
            else:
                xu[d, here] = jnp.where(grid.rows == 7, 0.0, mean(held[d], fall(held[d], 7)))
            link = jnp.where(seam, mean(held[d][:, plane:width], fifth[1, d, here]), 0.0)
            s[d, here, 0:plane] = block[1, d, here, 0:plane]
            s[d, here, plane:width] = block[1, d, here, plane:width] + link * jnp.where(seam, fifth[0, d, here], 0.0)
            part = across[0][d] + across[1][d] + across[2][d] + across[3][d] + grid.edges(d, held[d])
            part = jnp.concatenate([part[:, 0:plane], part[:, plane:width] + link], axis=1)
            if r:
                xl[d, here] = xu[d, r - 1 : r + 7]
            if 0 < r < own_rows - 8:
                part = part + xl[d, here] + xu[d, here]
                inverse[d, here] = 1.0 / part
            total[d, here] = part
    for r in range(8, own_rows - 8, 8):
        here = slice(r, r + 8)
        held = [f[d, here] for d in range(BZB)]
        lowers = [f[d, r - 1 : r + 7] for d in range(BZB)]
        uppers = [f[d, r + 1 : r + 9] for d in range(BZB)]
        parts = grid.sums(held, lowers, uppers, lambda d: tuple(ref[d, here] for ref in (s, xl, xu, yl, yu, zl, zu)))
        for d in range(BZB):
            f[d, here] = jnp.where(grid.colour == 0, parts[d] * inverse[d, here], held[d])


def smooth_kernel(lanes, nodes, covered, own_table, block, own_f, own_s, own_xl, own_xu, own_yl, own_yu, own_zl, own_zu,
                  own_total, own_inverse, from_below, from_above, row_table, two_on, smoothed, coarse, flag,
                  f, s, xl, xu, yl, yu, zl, zu, inverse, end_xl, end_xu, end_total, end_inverse, rest, labels, label_sem):
    width = block.shape[3]
    own_rows = block.shape[2]
    side = smoothed.shape[1]
    plane = smoothed.shape[2]
    node, lane = lax.axis_index("node"), lax.axis_index("lane")
    fetch = pltpu.make_async_copy(own_table, labels, label_sem)
    fetch.start()
    grid = Stencil(width, side, plane, lanes, nodes)
    rows = grid.rows
    halo = PAD + own_rows
    last = own_rows - 8
    halo_beta = []
    for d in range(BZB):
        f[d, PAD:halo] = own_f[d]
        strips = []
        for message in (from_below, from_above):
            for k in (d % 2, 2):
                unit = (d // 2 * 3 + k) * 3
                strips.append(jnp.concatenate([message[unit + part] for part in range(width // 128)], axis=1))
        field, beta, fifth_field, fifth_beta = unpack_rows(strips[0], strips[2])
        f[d, 0:8] = field
        f[d, halo : halo + 8] = field
        source = jnp.where(rows < 4, strips[3], strips[1])
        if d % 2:
            source = jnp.where(rows < 4, fall(strips[3], 4), fall(strips[1], 4))
        link = jnp.where((rows == 3) | (rows == 4), mean(beta, fifth_beta), 0.0)
        s[d] = source + link * fifth_field
        inverse[d] = link
        halo_beta.append(beta)
    across = grid.across(halo_beta)
    for ref, values in zip((yl, yu, zl, zu), across):
        for d in range(BZB):
            ref[d] = values[d]
    for d in range(BZB):
        held = halo_beta[d]
        up = mean(held, jnp.where(rows == 7, fall(block[2, d, 0:8], 7), fall(held, 7)))
        up = jnp.where((rows == 3) | ((rows == 7) & grid.first_node), 0.0, up)
        down = mean(held, fall(block[2, d, last:own_rows], 1))
        down = jnp.where(grid.last_node, 0.0, down)
        down = jnp.where(rows == 0, down, fall(up, 1))
        xl[d], xu[d] = down, up
        whole = inverse[d] + down + up + across[0][d] + across[1][d] + across[2][d] + across[3][d] + grid.edges(d, held)
        inverse[d] = 1.0 / whole
        end_xl[d, 0:8] = jnp.where(rows == 0, fall(up, 1), fall(own_xu[d, 0:8], 1))
        end_xu[d, 0:8] = own_xu[d, 0:8]
        end_xl[d, 8:16] = own_xl[d, last:own_rows]
        end_xu[d, 8:16] = jnp.where(rows == 7, fall(down, 7), own_xu[d, last:own_rows])
        for at, start, absent in (
            (slice(0, 8), 0, (rows == 0) & grid.first_node),
            (slice(8, 16), last, (rows == 7) & grid.last_node),
        ):
            whole = own_total[d, start : start + 8] + end_xl[d, at] + end_xu[d, at]
            whole = whole + jnp.where(absent, block[2, d, start : start + 8], 0.0)
            end_total[d, at] = whole
            end_inverse[d, at] = 1.0 / whole

    ends = {0: slice(0, 8), last: slice(8, 16)}

    def coefficients_at(r):
        here = slice(r, r + 8)
        across = (own_yl, own_yu, own_zl, own_zu)
        if r in ends:
            return lambda d: (own_s[d, here], end_xl[d, ends[r]], end_xu[d, ends[r]]) + tuple(ref[d, here] for ref in across)
        return lambda d: tuple(ref[d, here] for ref in (own_s, own_xl, own_xu) + across)

    def own_sums(r):
        held = [f[d, r + PAD : r + PAD + 8] for d in range(BZB)]
        lowers = [f[d, r + PAD - 1 : r + PAD + 7] for d in range(BZB)]
        uppers = [f[d, r + PAD + 1 : r + PAD + 9] for d in range(BZB)]
        return held, grid.sums(held, lowers, uppers, coefficients_at(r))

    for sweep in range(SWEEPS):
        for colour_id in (0, 1):
            chosen = grid.colour == colour_id
            held = [f[d, 0:8] for d in range(BZB)]
            lowers = [jnp.where(rows == 0, fall(f[d, halo - 8 : halo], 1), fall(held[d], 1)) for d in range(BZB)]
            uppers = [jnp.where(rows == 7, fall(f[d, PAD : PAD + 8], 7), fall(held[d], 7)) for d in range(BZB)]
            parts = grid.sums(held, lowers, uppers, lambda d: tuple(ref[d] for ref in (s, xl, xu, yl, yu, zl, zu)))
            halo_new = [jnp.where(chosen, parts[d] * inverse[d], held[d]) for d in range(BZB)]
            for r in range(0, own_rows, 8):
                if sweep + colour_id == 0 and r not in ends:
                    continue
                held, parts = own_sums(r)
                for d in range(BZB):
                    factor = end_inverse[d, ends[r]] if r in ends else own_inverse[d, r : r + 8]
                    f[d, r + PAD : r + PAD + 8] = jnp.where(chosen, parts[d] * factor, held[d])
            for d in range(BZB):
                f[d, 0:8] = halo_new[d]
                f[d, halo : halo + 8] = halo_new[d]

    fetch.wait()
    for r in range(0, own_rows, 8):
        held, parts = own_sums(r)
        wide, inner = divmod(r, side)
        for d in range(BZB):
            whole = end_total[d, ends[r]] if r in ends else own_total[d, r : r + 8]
            left = parts[d] - whole * held[d]
            slot = labels[wide * BZB + d, 12].astype(jnp.int32)
            smoothed[slot, inner : inner + 8] = held[d][:, 0:plane]
            for k in range(plane // 128):
                rest[k, pl.ds(pl.multiple_of(slot * side + inner, 8), 8), :] = left[:, k * 128 : (k + 1) * 128]

    count = smoothed.shape[0]
    small = side // 2
    cells = lax.broadcasted_iota(jnp.int32, (plane, 128), 0)
    slots = lax.broadcasted_iota(jnp.int32, (plane, 128), 1)
    goal = lax.div(lax.div(cells, side), 2) * small + lax.div(lax.rem(cells, side), 2)
    per = small * small
    acc = 0.0
    pairs = small * per // 128
    for inner in range(128 // per):
        stack = []
        for pair in range(pairs):
            i = pair * (128 // per) + inner
            even = [rest[k, pl.ds(2 * i, count, stride=side), :] for k in range(plane // 128)]
            odd = [rest[k, pl.ds(2 * i + 1, count, stride=side), :] for k in range(plane // 128)]
            stack.append(jnp.concatenate(even, axis=1) + jnp.concatenate(odd, axis=1))
        pooling = (goal + inner * per == slots).astype(jnp.float32)
        acc = acc + jnp.dot(
            jnp.concatenate(stack, axis=0), pooling, precision=lax.Precision.HIGHEST, preferred_element_type=jnp.float32
        )
    for pair in range(pairs):
        coarse[:, pair * 128 : (pair + 1) * 128] = 0.125 * acc[pair * count : (pair + 1) * count]

    mine = from_below.shape[0] - 1
    rows1 = lax.broadcasted_iota(jnp.int32, (8, 128), 0)
    cols1 = lax.broadcasted_iota(jnp.int32, (8, 128), 1)
    owner = lax.rem(lax.div(cols1, 8), 8)
    field_of = lax.rem(cols1, 8)
    table_here, opposite = row_table[...], two_on[...]
    lower, upper = from_below[mine], from_above[mine]
    rows_of = [(table_here, lower, upper, node), (lower, opposite, table_here, lax.rem(node + nodes - 1, nodes)),
               (upper, table_here, opposite, lax.rem(node + 1, nodes)), (opposite, upper, lower, lax.rem(node + 2, nodes))]
    if not covered:
        rows_of = rows_of[:1]
    lane_of = lax.rem(lane - jnp.where(owner > 4, owner - 8, owner) + 2 * lanes, lanes)
    wrong = jnp.zeros((8, 128), jnp.float32)
    for table, low, high, at_node in rows_of:
        turned = pltpu.roll(table, 4, 0)
        at_low = jnp.where(rows1 >= 4, turned, jnp.where(at_node == 0, -1.0, pltpu.roll(low, 4, 0)))
        at_high = jnp.where(rows1 < 4, turned, jnp.where(at_node == nodes - 1, -1.0, pltpu.roll(high, 4, 0)))
        y_low = jnp.where(lane_of == 0, -1.0, pltpu.roll(table, 128 - 8, 1))
        y_high = jnp.where(lane_of == lanes - 1, -1.0, pltpu.roll(table, 8, 1))
        z_low = jnp.where(lax.rem(rows1, BZB) == 0, -1.0, pltpu.roll(table, 1, 0))
        z_high = jnp.where(lax.rem(rows1, BZB) == BZB - 1, -1.0, pltpu.roll(table, 7, 0))
        bad = jnp.where((field_of == 0) & (table < 0), 1.0, 0.0)
        for face, expected in enumerate((at_low, at_high, y_low, y_high, z_low, z_high)):
            differs = table != pltpu.roll(expected, 1 + face, 1)
            bad = bad + jnp.where((field_of == 1 + face) & differs, 1.0, 0.0)
        if not covered:
            bad = jnp.where(owner == 0, bad, 0.0)
        wrong = wrong + bad
    flag[0, 0] = (jnp.sum(wrong) > 0).astype(jnp.int32)


ROOM = pltpu.CompilerParams(vmem_limit_bytes=32 * 2**20)
FULL = pltpu.CompilerParams(vmem_limit_bytes=60 * 2**20)
SCALARS = pl.BlockSpec(memory_space=pltpu.SMEM)
VECTORS = pl.BlockSpec(memory_space=pltpu.VMEM)


def fast_body(old_field, old_source, diffusivity, target_box, neighbours):
    count, side, plane = old_field.shape
    half = plane // 2
    lanes, nodes = lax.axis_size("lane"), lax.axis_size("node")
    arrays = (old_field, old_source, diffusivity, target_box, neighbours)
    moves, plan = lane_plan(lanes)
    covered = lanes == 8 and nodes == 4
    units = [plan_units(count, *parts) for parts in plan.values()]
    f32 = jnp.float32
    packed = pl.pallas_call(
        lambda *refs: pack_kernel(moves, plan, lanes, count, *refs),
        name="pack_moves",
        out_shape=[pltpu.VMEM((n, side, half), f32) for n in units]
        + [pltpu.VMEM(array.shape, array.dtype) for array in arrays]
        + [pltpu.VMEM((8, 128), f32)],
        in_specs=[SCALARS] * 2 + [pl.BlockSpec(memory_space=pltpu.HBM)] * 5,
        out_specs=[VECTORS] * (len(units) + 6),
        scratch_shapes=[pltpu.SMEM((count,), jnp.int32), pltpu.SemaphoreType.DMA((5,))],
        compiler_params=FULL,
    )(target_box, neighbours, *arrays)
    messages, own_table = packed[:-6], packed[-1]
    field, source, beta, target_held, neighbours_held = packed[-6:-1]
    got = {}
    early = [offset for offset in plan if offset in moves]
    for offset in early + [offset for offset in plan if offset not in moves]:
        message = messages[list(plan).index(offset)]
        if offset not in moves:
            message, _ = lax.optimization_barrier((message, got[2]))
        got[offset] = lax.ppermute(message, "lane", [(i, (i + offset) % lanes) for i in range(lanes)])
    got = [got[offset] for offset in plan]
    width = plane + 128
    strips = BZB // 2 * 9 + 1
    sides = pltpu.VMEM((5, BZB + 1, BXD * side, 128), f32)
    block, fifth, upward, downward, row_table = pl.pallas_call(
        lambda *refs: assemble_kernel(moves, plan, lanes, count, *refs),
        name="assemble_block",
        out_shape=[
            pltpu.VMEM((3, BZB + 1, BXD * side, width), f32),
            pltpu.VMEM((2, BZB, BXD * side, 128), f32),
            pltpu.VMEM((strips, 8, 128), f32),
            pltpu.VMEM((strips, 8, 128), f32),
            pltpu.VMEM((8, 128), f32),
        ],
        in_specs=[VECTORS] * (4 + len(units)),
        out_specs=[VECTORS] * 5,
        scratch_shapes=[
            sides,
            sides,
            pltpu.SMEM((len(units) + 1, 8, 128), f32),
            pltpu.SemaphoreType.DMA((len(units) + 1,)),
        ],
        compiler_params=ROOM,
    )(own_table, field, source, beta, *got)
    from_below = lax.ppermute(upward, "node", [(i, (i + 1) % nodes) for i in range(nodes)])
    from_above = lax.ppermute(downward, "node", [(i, (i - 1) % nodes) for i in range(nodes)])
    two_on = lax.ppermute(row_table, "node", [(i, (i + 2) % nodes) for i in range(nodes)])
    own_shape = pltpu.VMEM((BZB, BXD * side, width), f32)
    coupled = pl.pallas_call(
        lambda *refs: couple_kernel(lanes, nodes, plane, *refs),
        name="couple_block",
        out_shape=[own_shape] * 10,
        in_specs=[VECTORS] * 2,
        out_specs=[VECTORS] * 10,
        compiler_params=ROOM,
    )(block, fifth)
    tile, two_tiles = pltpu.VMEM((BZB, 8, width), f32), pltpu.VMEM((BZB, 16, width), f32)
    smoothed, coarse, flag = pl.pallas_call(
        lambda *refs: smooth_kernel(lanes, nodes, covered, *refs),
        name="smooth_block",
        out_shape=[
            jax.ShapeDtypeStruct((count, side, plane), f32),
            jax.ShapeDtypeStruct((count, (side // 2) ** 3), f32),
            jax.ShapeDtypeStruct((1, 1), jnp.int32),
        ],
        in_specs=[VECTORS] * 16,
        out_specs=[VECTORS, VECTORS, SCALARS],
        scratch_shapes=[pltpu.VMEM((BZB, BXD * side + 2 * PAD, width), f32)]
        + [tile] * 8
        + [two_tiles] * 4
        + [pltpu.VMEM((plane // 128, count * side, 128), f32), pltpu.SMEM((8, 128), f32), pltpu.SemaphoreType.DMA],
        compiler_params=ROOM,
    )(own_table, block, *coupled, from_below, from_above, row_table, two_on)
    irregular = flag[0, 0]
    if not covered:
        irregular = lax.pmax(irregular, ("node", "lane"))

    def again(carry):
        out = general_body(field, source, beta, target_held, neighbours_held)
        return (*out, jnp.int32(0))

    smoothed, coarse, _ = lax.while_loop(lambda carry: carry[2] > 0, again, (smoothed, coarse, irregular))
    return smoothed, coarse


def solution(mesh):
    in_specs = (
        P(("node", "lane"), None, None),
        P(("node", "lane"), None, None),
        P(("node", "lane"), None, None),
        P(("node", "lane")),
        P(("node", "lane"), None),
    )
    out_specs = (P(("node", "lane"), None, None), P(("node", "lane"), None))
    return jax.shard_map(fast_body, mesh=mesh, in_specs=in_specs, out_specs=out_specs, check_vma=False)
```

time: 37.3 us -> 33.9 us (0.909)
  Pallas kernels: 11.2 us -> 8.65 us
  waiting for transfers between devices: 7.24 us -> 6.39 us
    pallas_call x1, Pallas kernels: 6.06 us -> 3.15 us  [fast_body(): pl.pallas_call(lambda *refs: smooth_kernel(lanes, nodes, covered, *refs),...]
    ppermute x1, waiting for transfers between devices: 2.41 us -> 1.57 us  [fast_body(): lax.ppermute(row_table, 'node', [(i, (i + 2) % nodes) for i in range(node...]
    pallas_call x0 -> x1, Pallas kernels: none -> 0.84 us  [fast_body(): pl.pallas_call(lambda *refs: couple_kernel(lanes, nodes, plane, *refs), n...]
    pallas_call x1, Pallas kernels: 2.4 us -> 1.68 us  [fast_body(): pl.pallas_call(lambda *refs: assemble_kernel(moves, plan, lanes, count, *...]
  transfers between devices with their start and end apart: 10 -> 10, of which waited for: 3 -> 3; matrix products, arithmetic and copies ran while one was open for 0% -> 0% of each run, Pallas kernels for 0% -> 2%
where the time goes in v4:
time: 33.9 us; the launch traced here: 33.7 us
  starting transfers between devices  17.1 us (50%)
  Pallas kernels  8.65 us (26%)
  waiting for transfers between devices  6.39 us (19%)
  between operations  0.84 us (2%)
  loops' own time  0.76 us (2%)
    ppermute x7, starting transfers between devices, fast_body(): lax.ppermute(message, 'lane', [(i, (i + offset) % lanes) for i in range(l...  13.8 us
    ppermute x7, waiting for transfers between devices, fast_body(): lax.ppermute(message, 'lane', [(i, (i + offset) % lanes) for i in range(l...  4.82 us
    pallas_call x1, Pallas kernels, fast_body(): pl.pallas_call(lambda *refs: smooth_kernel(lanes, nodes, covered, *refs),...  3.15 us
    pallas_call x1, Pallas kernels, fast_body(): pl.pallas_call(lambda *refs: pack_kernel(moves, plan, lanes, count, *refs...  2.99 us
    ppermute x1, starting transfers between devices, fast_body(): lax.ppermute(downward, 'node', [(i, (i - 1) % nodes) for i in range(nodes)])  1.73 us
    pallas_call x1, Pallas kernels, fast_body(): pl.pallas_call(lambda *refs: assemble_kernel(moves, plan, lanes, count, *...  1.68 us
    ppermute x1, waiting for transfers between devices, fast_body(): lax.ppermute(row_table, 'node', [(i, (i + 2) % nodes) for i in range(node...  1.57 us
    ppermute x1, starting transfers between devices, fast_body(): lax.ppermute(row_table, 'node', [(i, (i + 2) % nodes) for i in range(node...  1.52 us
  transfers between devices with their start and end apart: 10, of which 3 were waited for; matrix products, arithmetic and copies ran while one was open for 0% of the time, Pallas kernels for 2%

profile of v4, /device:TPU:0, one launch (start us, length us, event | category | flops | bytes accessed | tf_op | source)
XLA Modules:
  0.0 33.7 jit_solution(421251590317165686)
XLA Ops:
  0.6 3.0 %pack_moves.1 = (f32[17,16,128]{2,1,0:T(8,128)S(1)}, f32[5,16,128]{2,1,0:T(8,128)S(1)}, f32[3,16,128]{2,1,0:T(8,128)S(1)}, f32[4,16,128]{2,1,0:T(8,128)S(1)}, f3...) custom-call(s32[8]{0:T(128)} %refs_5_.1, ...), custom_call_target="tpu_custom_call" | custom-call | tf_op jit(solution)/shard_map/pack_moves/pallas_call | solution.py:801
  3.6 3.0 %collective-permute-start.20 = (f32[17,16,128]{2,1,0:T(8,128)S(1)}, f32[17,16,128]{2,1,0:T(8,128)S(1)}, u32[]{:S(2)}, u32[]{:S(2)}) collective-permute-start(f32[17,16,128]{2,1,0:T(8,128)S(1)} %get-tuple-element.84), channel_id=1, source_target_pairs={{0,1},{1,2},{2,3},{3,4},{4,5},{5,6},{6,7},{7,0},{8,9},{9,10},{10,1... | collective-permute-start | bytes 417800 | tf_op jit(solution)/shard_map/ppermute | solution.py:820
  6.6 3.1 %collective-permute-start.26 = (f32[17,16,128]{2,1,0:T(8,128)S(1)}, f32[17,16,128]{2,1,0:T(8,128)S(1)}, u32[]{:S(2)}, u32[]{:S(2)}) collective-permute-start(f32[17,16,128]{2,1,0:T(8,128)S(1)} %get-tuple-element.92), channel_id=1, source_target_pairs={{0,7},{1,0},{2,1},{3,2},{4,3},{5,4},{6,5},{7,6},{8,15},{9,8},{10,9... | collective-permute-start | bytes 417800 | tf_op jit(solution)/shard_map/ppermute | solution.py:820
  9.7 0.0 collective-permute-start.21
  9.7 2.5 %collective-permute-start.23 = (f32[4,16,128]{2,1,0:T(8,128)S(1)}, f32[4,16,128]{2,1,0:T(8,128)S(1)}, u32[]{:S(2)}, u32[]{:S(2)}) collective-permute-start(f32[4,16,128]{2,1,0:T(8,128)S(1)} %get-tuple-element.88), channel_id=1, source_target_pairs={{0,4},{1,5},{2,6},{3,7},{4,0},{5,1},{6,2},{7,3},{8,12},{9,13},{10,... | collective-permute-start | bytes 98312 | tf_op jit(solution)/shard_map/ppermute | solution.py:820
  12.2 1.3 %collective-permute-start.25 = (f32[5,16,128]{2,1,0:T(8,128)S(1)}, f32[5,16,128]{2,1,0:T(8,128)S(1)}, u32[]{:S(2)}, u32[]{:S(2)}) collective-permute-start(f32[5,16,128]{2,1,0:T(8,128)S(1)} %get-tuple-element.91), channel_id=1, source_target_pairs={{0,6},{1,7},{2,0},{3,1},{4,2},{5,3},{6,4},{7,5},{8,14},{9,15},{10,... | collective-permute-start | bytes 122888 | tf_op jit(solution)/shard_map/ppermute | solution.py:820
  13.6 3.0 %collective-permute-done.21.refs_5_ = f32[5,16,128]{2,1,0:T(8,128)S(1)} collective-permute-done((f32[5,16,128]{2,1,0:T(8,128)S(1)}, f32[5,16,128]{2,1,0:T(8,128)S(1)}, u32[]{:S(2)}, u32[]{:S(2)}) %collective-permute-start.21) | collective-permute-done | bytes 40992 | tf_op jit(solution)/shard_map/ppermute | solution.py:820
  16.6 0.0 collective-permute-start.22
  16.6 0.0 collective-permute-done.23.refs_7_
  16.6 3.8 %collective-permute-start.24 = (f32[3,16,128]{2,1,0:T(8,128)S(1)}, f32[3,16,128]{2,1,0:T(8,128)S(1)}, u32[]{:S(2)}, u32[]{:S(2)}) collective-permute-start(f32[3,16,128]{2,1,0:T(8,128)S(1)} %get-tuple-element.90), channel_id=1, source_target_pairs={{0,5},{1,6},{2,7},{3,0},{4,1},{5,2},{6,3},{7,4},{8,13},{9,14},{10,... | collective-permute-start | bytes 73736 | tf_op jit(solution)/shard_map/ppermute | solution.py:820
  20.4 0.0 collective-permute-done.25.refs_9_
  20.4 1.8 %collective-permute-done.22.refs_6_ = f32[3,16,128]{2,1,0:T(8,128)S(1)} collective-permute-done((f32[3,16,128]{2,1,0:T(8,128)S(1)}, f32[3,16,128]{2,1,0:T(8,128)S(1)}, u32[]{:S(2)}, u32[]{:S(2)}) %collective-permute-start.22) | collective-permute-done | bytes 24608 | tf_op jit(solution)/shard_map/ppermute | solution.py:820
  22.2 0.0 collective-permute-done.20.refs_4_
  22.2 0.0 collective-permute-done.26.refs_10_
  22.2 1.7 %assemble_block.1 = (f32[3,5,32,384]{3,2,1,0:T(8,128)S(1)}, f32[2,4,32,128]{3,2,1,0:T(8,128)S(1)}, f32[19,8,128]{2,1,0:T(8,128)S(1)}, f32[19,8,128]{2,1,0:T(8,128)S(1)}, f32[8,128]{1,0:T(8,128)S(1)}) custom-call(f32[8,128]{1,0:T(8,128)S(1)} %get-tuple-element.80.refs_0_, f32[8,16,256]{2,1,0:T(8,128)S(1)} %get-tuple-element.329.refs_1_, ...), custom_call_target="tpu_custom_call" | custom-call | tf_op jit(solution)/shard_map/assemble_block/pallas_call | solution.py:825
  23.9 0.1 collective-permute-start.27
  24.0 1.7 %collective-permute-start.28 = (f32[19,8,128]{2,1,0:T(8,128)S(1)}, f32[19,8,128]{2,1,0:T(8,128)S(1)}, u32[]{:S(2)}, u32[]{:S(2)}) collective-permute-start(f32[19,8,128]{2,1,0:T(8,128)S(1)} %get-tuple-element.106), channel_id=1, source_target_pairs={{0,24},{8,0},{16,8},{24,16},{1,25},{9,1},{17,9},{25,17},{2,26},{10... | collective-permute-start | bytes 233480 | tf_op jit(solution)/shard_map/ppermute | solution.py:846
  25.7 1.5 %collective-permute-start.29 = (f32[8,128]{1,0:T(8,128)S(1)}, f32[8,128]{1,0:T(8,128)S(1)}, u32[]{:S(2)}, u32[]{:S(2)}) collective-permute-start(f32[8,128]{1,0:T(8,128)S(1)} %get-tuple-element.107.refs_14_), channel_id=1, source_target_pairs={{0,16},{8,24},{16,0},{24,8},{1,17},{9,25},{17,1},{25,9},{2,18},{10... | collective-permute-start | bytes 12296 | tf_op jit(solution)/shard_map/ppermute | solution.py:847
  27.2 0.8 %couple_block.1 = (f32[4,32,384]{2,1,0:T(8,128)S(1)}, f32[4,32,384]{2,1,0:T(8,128)S(1)}, f32[4,32,384]{2,1,0:T(8,128)S(1)}, f32[4,32,384]{2,1,0:T(8,128)S(1)}, f...) custom-call(f32[3,5,32,384]{3,2,1,0:T(8,128)S(1)} %get-tuple-element, ...), custom_call_target="tpu_custom_call" | custom-call | tf_op jit(solution)/shard_map/couple_block/pallas_call | solution.py:849
  28.1 1.6 %collective-permute-done.29.refs_15_ = f32[8,128]{1,0:T(8,128)S(1)} collective-permute-done((f32[8,128]{1,0:T(8,128)S(1)}, f32[8,128]{1,0:T(8,128)S(1)}, u32[]{:S(2)}, u32[]{:S(2)}) %collective-permute-start.29) | collective-permute-done | bytes 4128 | tf_op jit(solution)/shard_map/ppermute | solution.py:847
  29.6 0.0 collective-permute-done.27.refs_12_
  29.6 0.0 collective-permute-done.28.refs_13_
  29.6 3.1 %smooth_block.1 = (f32[8,16,256]{2,1,0:T(8,128)}, f32[8,512]{1,0:T(8,128)}, s32[1,1]{1,0:T(1,128)}) custom-call(f32[8,128]{1,0:T(8,128)S(1)} %get-tuple-element.80.refs_0_, f32[3,5,32,384]{3,2,1,0:T(8,128)S(1)} %get-tuple-element.93.refs_0_.refs_1_, f32[4,32,384]{2,1,0:T(8,128)S(1)} %get-tuple-element.95.refs_2_, ...), custom_call_target="tpu_custom_call" | custom-call | tf_op jit(solution)/shard_map/smooth_block/pallas_call | solution.py:858
  32.8 0.8 %while.12 = (f32[8,16,256]{2,1,0:T(8,128)}, f32[8,512]{1,0:T(8,128)}, s32[]{:T(128)}, s32[8]{0:T(128)S(1)}, f32[8,16,256]{2,1,0:T(8,128)S(1)}, /*index=5*/f32[8,...) while((f32[8,16,256]{2,1,0:T(8,128)}, f32[8,512]{1,0:T(8,128)}, s32[]{:T(128)}, ...), condition=%region_7.8_spmd.clone, body=%region_0.7_spmd.sunk.clone | while | flops 21889904 | bytes 78598984 | solution.py:882
  (1 shorter events, 0.0 us)
Async XLA Ops:
  3.6 18.6 %collective-permute-start.20 = (f32[17,16,128]{2,1,0:T(8,128)S(1)}, f32[17,16,128]{2,1,0:T(8,128)S(1)}, u32[]{:S(2)}, u32[]{:S(2)}) collective-permute-start(f32[17,16,128]{2,1,0:T(8,128)S(1)} %get-tuple-element.84), channel_id=1, source_target_pairs={{0,1},{1,2},{2,3},{3,4},{4,5},{5,6},{6,7},{7,0},{8,9},{9,10},{10,1... | collective-permute-start | bytes 417800 | tf_op jit(solution)/shard_map/ppermute | solution.py:820
  6.6 15.6 %collective-permute-start.26 = (f32[17,16,128]{2,1,0:T(8,128)S(1)}, f32[17,16,128]{2,1,0:T(8,128)S(1)}, u32[]{:S(2)}, u32[]{:S(2)}) collective-permute-start(f32[17,16,128]{2,1,0:T(8,128)S(1)} %get-tuple-element.92), channel_id=1, source_target_pairs={{0,7},{1,0},{2,1},{3,2},{4,3},{5,4},{6,5},{7,6},{8,15},{9,8},{10,9... | collective-permute-start | bytes 417800 | tf_op jit(solution)/shard_map/ppermute | solution.py:820
  9.7 6.9 %collective-permute-start.21 = (f32[5,16,128]{2,1,0:T(8,128)S(1)}, f32[5,16,128]{2,1,0:T(8,128)S(1)}, u32[]{:S(2)}, u32[]{:S(2)}) collective-permute-start(f32[5,16,128]{2,1,0:T(8,128)S(1)} %get-tuple-element.85), channel_id=1, source_target_pairs={{0,2},{1,3},{2,4},{3,5},{4,6},{5,7},{6,0},{7,1},{8,10},{9,11},{10,... | collective-permute-start | bytes 122888 | tf_op jit(solution)/shard_map/ppermute | solution.py:820
  9.7 6.9 %collective-permute-start.23 = (f32[4,16,128]{2,1,0:T(8,128)S(1)}, f32[4,16,128]{2,1,0:T(8,128)S(1)}, u32[]{:S(2)}, u32[]{:S(2)}) collective-permute-start(f32[4,16,128]{2,1,0:T(8,128)S(1)} %get-tuple-element.88), channel_id=1, source_target_pairs={{0,4},{1,5},{2,6},{3,7},{4,0},{5,1},{6,2},{7,3},{8,12},{9,13},{10,... | collective-permute-start | bytes 98312 | tf_op jit(solution)/shard_map/ppermute | solution.py:820
  12.2 8.2 %collective-permute-start.25 = (f32[5,16,128]{2,1,0:T(8,128)S(1)}, f32[5,16,128]{2,1,0:T(8,128)S(1)}, u32[]{:S(2)}, u32[]{:S(2)}) collective-permute-start(f32[5,16,128]{2,1,0:T(8,128)S(1)} %get-tuple-element.91), channel_id=1, source_target_pairs={{0,6},{1,7},{2,0},{3,1},{4,2},{5,3},{6,4},{7,5},{8,14},{9,15},{10,... | collective-permute-start | bytes 122888 | tf_op jit(solution)/shard_map/ppermute | solution.py:820
  16.6 5.6 %collective-permute-start.22 = (f32[3,16,128]{2,1,0:T(8,128)S(1)}, f32[3,16,128]{2,1,0:T(8,128)S(1)}, u32[]{:S(2)}, u32[]{:S(2)}) collective-permute-start(f32[3,16,128]{2,1,0:T(8,128)S(1)} %get-tuple-element.87), channel_id=1, source_target_pairs={{0,3},{1,4},{2,5},{3,6},{4,7},{5,0},{6,1},{7,2},{8,11},{9,12},{10,... | collective-permute-start | bytes 73736 | tf_op jit(solution)/shard_map/ppermute | solution.py:820
  16.6 5.6 %collective-permute-start.24 = (f32[3,16,128]{2,1,0:T(8,128)S(1)}, f32[3,16,128]{2,1,0:T(8,128)S(1)}, u32[]{:S(2)}, u32[]{:S(2)}) collective-permute-start(f32[3,16,128]{2,1,0:T(8,128)S(1)} %get-tuple-element.90), channel_id=1, source_target_pairs={{0,5},{1,6},{2,7},{3,0},{4,1},{5,2},{6,3},{7,4},{8,13},{9,14},{10,... | collective-permute-start | bytes 73736 | tf_op jit(solution)/shard_map/ppermute | solution.py:820
  23.9 5.7 %collective-permute-start.27 = (f32[19,8,128]{2,1,0:T(8,128)S(1)}, f32[19,8,128]{2,1,0:T(8,128)S(1)}, u32[]{:S(2)}, u32[]{:S(2)}) collective-permute-start(f32[19,8,128]{2,1,0:T(8,128)S(1)} %get-tuple-element.105), channel_id=1, source_target_pairs={{0,8},{8,16},{16,24},{24,0},{1,9},{9,17},{17,25},{25,1},{2,10},{10... | collective-permute-start | bytes 233480 | tf_op jit(solution)/shard_map/ppermute | solution.py:845
  24.0 5.7 %collective-permute-start.28 = (f32[19,8,128]{2,1,0:T(8,128)S(1)}, f32[19,8,128]{2,1,0:T(8,128)S(1)}, u32[]{:S(2)}, u32[]{:S(2)}) collective-permute-start(f32[19,8,128]{2,1,0:T(8,128)S(1)} %get-tuple-element.106), channel_id=1, source_target_pairs={{0,24},{8,0},{16,8},{24,16},{1,25},{9,1},{17,9},{25,17},{2,26},{10... | collective-permute-start | bytes 233480 | tf_op jit(solution)/shard_map/ppermute | solution.py:846
  25.7 3.9 %collective-permute-start.29 = (f32[8,128]{1,0:T(8,128)S(1)}, f32[8,128]{1,0:T(8,128)S(1)}, u32[]{:S(2)}, u32[]{:S(2)}) collective-permute-start(f32[8,128]{1,0:T(8,128)S(1)} %get-tuple-element.107.refs_14_), channel_id=1, source_target_pairs={{0,16},{8,24},{16,0},{24,8},{1,17},{9,25},{17,1},{25,9},{2,18},{10... | collective-permute-start | bytes 12296 | tf_op jit(solution)/shard_map/ppermute | solution.py:847

commit v5 on v4

--- a/solution.py
+++ b/solution.py
@@ -215,18 +215,18 @@
 def cell_lanes(side):
     rows = lax.broadcasted_iota(jnp.int32, (side, 128), 0)
     cols = lax.broadcasted_iota(jnp.int32, (side, 128), 1)
-    black = lax.rem(rows + lax.div(cols, side) + lax.rem(cols, side), 2) == 1
-    return cols, black
+    layer = cols >> (side.bit_length() - 1)
+    black = ((rows + layer + cols) & 1) == 1
+    return layer, black
 
 
 def turn(values, shift):
     return pltpu.roll(values, shift % values.shape[-1], values.ndim - 1)
 
 
-def pack_end(part, field, source, beta):
+def pack_end(part, field, source, beta, masks):
     side = field.shape[0]
-    cols, black = cell_lanes(side)
-    y = lax.div(cols, side)
+    y, black = masks
     if part == HIGH:
         pairs = jnp.where(black, field, turn(field, side))
         out = jnp.where(y >= 4, source, pairs)
@@ -242,7 +242,7 @@
 
 def unpack_end(part, packed):
     side = packed.shape[0]
-    y = lax.div(lax.broadcasted_iota(jnp.int32, packed.shape, 1), side)
+    y, _ = cell_lanes(side)
     out = packed
     places = ((7, 7), (6, 6), (5, 4), (4, 3)) if part == HIGH else ((0, 1), (1, 2), (2, 4), (3, 5))
     for layer, shift in places:
@@ -252,8 +252,8 @@
 
 def pack_whole(low, high):
     side = low.shape[0]
-    cols, black = cell_lanes(side)
-    even = lax.rem(lax.div(cols, side), 2) == 0
+    layer, black = cell_lanes(side)
+    even = (layer & 1) == 0
     low = jnp.where(black, low, turn(low, -side))
     high = jnp.where(black, high, turn(high, -side))
     return jnp.where(even, low, turn(high, side))
@@ -261,7 +261,7 @@
 
 def unpack_whole(packed):
     side = packed.shape[0]
-    even = lax.rem(lax.div(lax.broadcasted_iota(jnp.int32, packed.shape, 1), side), 2) == 0
+    even = (cell_lanes(side)[0] & 1) == 0
     return jnp.where(even, packed, turn(packed, side)), jnp.where(even, turn(packed, -side), packed)
 
 
@@ -270,13 +270,15 @@
 
 
 def pack_kernel(moves, plan, lanes, count, *refs):
-    target, near = refs[:2]
-    outs = refs[7 : 7 + len(plan)]
-    held_here = refs[7 + len(plan) : 12 + len(plan)]
-    table, slots, sems = refs[12 + len(plan) :]
-    fetch = [pltpu.make_async_copy(src, dst, sems.at[k]) for k, (src, dst) in enumerate(zip(refs[2:7], held_here))]
+    outs = refs[5 : 5 + len(plan)]
+    held_here = refs[5 + len(plan) : 10 + len(plan)]
+    table, target, near, slots, sems = refs[10 + len(plan) :]
+    pairs = [*zip(refs[3:5], (target, near)), *zip(refs[:5], held_here)]
+    fetch = [pltpu.make_async_copy(src, dst, sems.at[k]) for k, (src, dst) in enumerate(pairs)]
     for copy in fetch:
         copy.start()
+    for copy in fetch[:2]:
+        copy.wait()
     field, source, beta = held_here[:3]
     side, plane = field.shape[1:]
     half = plane // 2
@@ -334,14 +336,15 @@
         held = put(held, k, 8, new_slot[k])
         held = put(held, k, 10, old_index[k])
     table[...] = held.astype(jnp.float32)
-    for copy in fetch:
+    for copy in fetch[2:]:
         copy.wait()
+    masks = cell_lanes(side)
     left = lax.broadcasted_iota(jnp.int32, (side, 128), 1) < 64
     for out, (bulk, whole, kept) in zip(outs, plan.values()):
         if bulk is not None:
             cut = part_lanes(bulk, plane)
             for i in range(count):
-                out[i] = pack_end(bulk, field[i, :, cut], source[i, :, cut], beta[i, :, cut])
+                out[i] = pack_end(bulk, field[i, :, cut], source[i, :, cut], beta[i, :, cut], masks)
             for i in range(0, count, 2):
                 one, two = beta[i, :, cut], turn(beta[i + 1, :, cut], 64)
                 out[count + i // 2] = jnp.where(left, two, one) if bulk == HIGH else jnp.where(left, one, two)
@@ -357,7 +360,7 @@
         for move, part in kept:
             box = old_index[moves.index(move)]
             cut = part_lanes(part, plane)
-            out[unit] = pack_end(part, field[box, :, cut], source[box, :, cut], field[box, :, cut])
+            out[unit] = pack_end(part, field[box, :, cut], source[box, :, cut], field[box, :, cut], masks)
             unit += 1
     for out in outs:
         out[out.shape[0] - 1, 0:8] = table[...]
@@ -366,7 +369,7 @@
 def assemble_kernel(moves, plan, lanes, count, *refs):
     own_table, field, source, beta = refs[:4]
     got = dict(zip(plan, refs[4 : 4 + len(plan)]))
-    block, fifth, upward, downward, row_table, low_side, high_side, tables, table_sems = refs[4 + len(plan) :]
+    block, fifth, to_pair, to_other, row_table, low_side, high_side, tables, table_sems = refs[4 + len(plan) :]
     side, plane = field.shape[1:]
     half = plane // 2
     order = list(plan) + [0]
@@ -388,8 +391,8 @@
         joined = joined + pltpu.roll(jnp.where(cols < 8, table_of(offset)[...], 0.0), 8 * at, 1)
     joined = joined + pltpu.roll(joined, 64, 1)
     row_table[...] = joined
-    upward[upward.shape[0] - 1] = joined
-    downward[downward.shape[0] - 1] = joined
+    to_pair[to_pair.shape[0] - 1] = joined
+    to_other[to_other.shape[0] - 1] = joined
 
     for copy in fetch:
         copy.wait()
@@ -461,24 +464,28 @@
             block[k, d, :, plane:width] = jnp.where(left, high_side[k, d], low_side[k, d])
         for k in range(2):
             fifth[k, d] = jnp.where(left, high_side[3 + k, d], low_side[3 + k, d])
-    for message, start, up in ((upward, rows - 8, True), (downward, 0, False)):
-        for deep in range(0, BZB, 2):
+    even_node = (lax.axis_index("node") & 1) == 0
+    for deep in range(0, BZB, 2):
+        strips = []
+        for start, up in ((rows - 8, True), (0, False)):
             tiles = []
             sources = []
             for d in (deep, deep + 1):
                 f, s, b = (block[k, d, start : start + 8] for k in range(3))
                 tiles.append(pack_rows(up, f, b))
                 sources.append(s)
-            tiles.append(pack_sources(up, *sources))
-            for k, tile in enumerate(tiles):
-                for part in range(width // 128):
-                    message[(deep // 2 * 3 + k) * 3 + part] = tile[:, part * 128 : (part + 1) * 128]
+            strips.append(tiles + [pack_sources(up, *sources)])
+        for k, (up, down) in enumerate(zip(*strips)):
+            for part in range(width // 128):
+                cut, unit = slice(part * 128, (part + 1) * 128), (deep // 2 * 3 + k) * 3 + part
+                to_pair[unit] = jnp.where(even_node, up[:, cut], down[:, cut])
+                to_other[unit] = jnp.where(even_node, down[:, cut], up[:, cut])
 
 
 def row_colours(width, side):
     rows = lax.broadcasted_iota(jnp.int32, (8, width), 0)
     cols = lax.broadcasted_iota(jnp.int32, (8, width), 1)
-    return rows, lax.rem(rows + lax.div(cols, side) + lax.rem(cols, side), 2)
+    return rows, (rows + (cols >> (side.bit_length() - 1)) + cols) & 1
 
 
 def fall(values, shift):
@@ -523,6 +530,7 @@
         cols = lax.broadcasted_iota(jnp.int32, (8, width), 1)
         depth = lax.rem(cols, side)
         self.at_front, self.at_back = depth == 0, depth == side - 1
+        self.odd = (((cols >> (side.bit_length() - 1)) + cols) & 1) == 1
         first_lane, last_lane = lane == 0, lane == lanes - 1
         self.low_edge = (cols < side) & first_lane
         self.high_edge = (cols >= plane - side) & (cols < plane) & last_lane
@@ -568,25 +576,52 @@
             out = out + jnp.where(self.at_back, held, 0.0)
         return out
 
-    def sums(self, held, lowers, uppers, coefficient):
+    def sums(self, colour_id, held, downs, ups, behind_of, ahead_of, coefficient):
         afters = [self.after(v) for v in held]
         befores = [self.before(v) for v in held]
-        behind = self.beyond_z(held, afters)
-        aheads = self.ahead_z(held, befores)
+        behind = behind_of(held, afters)
+        aheads = ahead_of(held, befores)
         out = []
-        for d in range(BZB):
-            s, xl, xu, yl, yu, zl, zu = coefficient(d)
-            part = s + xl * lowers[d] + xu * uppers[d]
-            part = part + (yl * befores[d] + yu * afters[d])
-            out.append(part + (zl * behind[d] + zu * aheads[d]))
+        for at in range(len(held)):
+            s, same, other, yl, yu, zl, zu = coefficient(at)
+            across = jnp.where(self.odd == (colour_id == 1), downs[at], ups[at])
+            part = s + same * held[at] + other * across
+            part = part + (yl * befores[at] + yu * afters[at])
+            out.append(part + (zl * behind[at] + zu * aheads[at]))
         return out
+
+    def beyond_pairs(self, values, afters):
+        last = (fall(afters[1], 4), afters[0])
+        return [pltpu.roll(jnp.where(self.at_back, last[j], values[j]), 1, 1) for j in range(2)]
+
+    def ahead_pairs(self, values, befores):
+        following = (befores[1], fall(befores[0], 4))
+        return [pltpu.roll(jnp.where(self.at_front, following[j], values[j]), self.width - 1, 1) for j in range(2)]
+
+    def split(self, even, odd):
+        return jnp.where(self.odd, odd, even), jnp.where(self.odd, even, odd)
 
 
 def mean(one_side, other):
     return 2.0 * one_side * other / (one_side + other)
 
 
-def couple_kernel(lanes, nodes, plane, block, fifth, f, s, xl, xu, yl, yu, zl, zu, total, inverse):
+def scatter_tiles(ref, index, rows, values):
+    for k in range(ref.shape[0]):
+        ref[(k, index, rows)] = values[:, k * 128 : (k + 1) * 128]
+
+
+def every_other(ref, index, start, count):
+    tiles = [ref[k, index, pl.ds(start, count, stride=2), :] for k in range(ref.shape[0])]
+    return jnp.concatenate(tiles, axis=1)
+
+
+def couple_kernel(lanes, nodes, plane, block, fifth, *refs):
+    first, black, same = refs[:3]
+    red_refs, black_refs = refs[3:9], refs[9:15]
+    totals = refs[15:17]
+    natural = refs[17:]
+    f, s, xl, xu, yl, yu, zl, zu, total = natural
     width, own_rows = block.shape[3], block.shape[2]
     grid = Stencil(width, SIDE, plane, lanes, nodes)
     cols = lax.broadcasted_iota(jnp.int32, (8, 128), 1)
@@ -595,39 +630,60 @@
         here = slice(r, r + 8)
         held = [block[2, d, here] for d in range(BZB)]
         across = grid.across(held)
-        for ref, values in zip((yl, yu, zl, zu), across):
-            for d in range(BZB):
-                ref[d, here] = values[d]
         for d in range(BZB):
-            f[d, here] = block[0, d, here]
+            for ref, values in zip((yl, yu, zl, zu), across):
+                scatter_tiles(ref, d, here, values[d])
+            scatter_tiles(f, d, here, block[0, d, here])
             if r + 8 < own_rows:
-                xu[d, here] = mean(held[d], block[2, d, r + 1 : r + 9])
+                up = mean(held[d], block[2, d, r + 1 : r + 9])
             else:
-                xu[d, here] = jnp.where(grid.rows == 7, 0.0, mean(held[d], fall(held[d], 7)))
+                up = jnp.where(grid.rows == 7, 0.0, mean(held[d], fall(held[d], 7)))
+            if r:
+                down = mean(held[d], block[2, d, r - 1 : r + 7])
+            else:
+                down = jnp.where(grid.rows == 0, 0.0, mean(held[d], fall(held[d], 1)))
             link = jnp.where(seam, mean(held[d][:, plane:width], fifth[1, d, here]), 0.0)
-            s[d, here, 0:plane] = block[1, d, here, 0:plane]
-            s[d, here, plane:width] = block[1, d, here, plane:width] + link * jnp.where(seam, fifth[0, d, here], 0.0)
-            part = across[0][d] + across[1][d] + across[2][d] + across[3][d] + grid.edges(d, held[d])
-            part = jnp.concatenate([part[:, 0:plane], part[:, plane:width] + link], axis=1)
-            if r:
-                xl[d, here] = xu[d, r - 1 : r + 7]
-            if 0 < r < own_rows - 8:
-                part = part + xl[d, here] + xu[d, here]
-                inverse[d, here] = 1.0 / part
-            total[d, here] = part
-    for r in range(8, own_rows - 8, 8):
-        here = slice(r, r + 8)
-        held = [f[d, here] for d in range(BZB)]
-        lowers = [f[d, r - 1 : r + 7] for d in range(BZB)]
-        uppers = [f[d, r + 1 : r + 9] for d in range(BZB)]
-        parts = grid.sums(held, lowers, uppers, lambda d: tuple(ref[d, here] for ref in (s, xl, xu, yl, yu, zl, zu)))
+            extra = link * jnp.where(seam, fifth[0, d, here], 0.0)
+            source = block[1, d, here]
+            scatter_tiles(s, d, here, jnp.concatenate([source[:, 0:plane], source[:, plane:width] + extra], axis=1))
+            scatter_tiles(xl, d, here, down)
+            scatter_tiles(xu, d, here, up)
+            part = down + up + across[0][d] + across[1][d] + across[2][d] + across[3][d] + grid.edges(d, held[d])
+            scatter_tiles(total, d, here, jnp.concatenate([part[:, 0:plane], part[:, plane:width] + link], axis=1))
+    for d in range(BZB):
+        for t in range(own_rows // 16):
+            to = slice(8 * t, 8 * t + 8)
+            even = [every_other(ref, d, 16 * t, 8) for ref in natural]
+            odd = [every_other(ref, d, 16 * t + 1, 8) for ref in natural]
+            black[d, to] = grid.split(even[0], odd[0])[1]
+            same[d, to] = even[3]
+            pairs = [(even[1], odd[1]), (even[2], odd[3])] + [(even[k], odd[k]) for k in (4, 5, 6, 7)]
+            for red_ref, black_ref, pair in zip(red_refs, black_refs, pairs):
+                red_ref[d, to], black_ref[d, to] = grid.split(*pair)
+            totals[0][d, to], totals[1][d, to] = grid.split(even[8], odd[8])
+    for t in range(own_rows // 16):
+        to = slice(8 * t, 8 * t + 8)
+        held = [black[d, to] for d in range(BZB)]
+        downs = [black[d, to.start - 1 : to.stop - 1] if t else fall(held[d], 1) for d in range(BZB)]
+        ups = [black[d, to.start + 1 : to.stop + 1] if 8 * t + 8 < own_rows // 2 else fall(held[d], 7) for d in range(BZB)]
+        parts = grid.sums(
+            0, held, downs, ups, grid.beyond_z, grid.ahead_z,
+            lambda d: (red_refs[0][d, to], same[d, to]) + tuple(ref[d, to] for ref in red_refs[1:]),
+        )
         for d in range(BZB):
-            f[d, here] = jnp.where(grid.colour == 0, parts[d] * inverse[d, here], held[d])
-
-
-def smooth_kernel(lanes, nodes, covered, own_table, block, own_f, own_s, own_xl, own_xu, own_yl, own_yu, own_zl, own_zu,
-                  own_total, own_inverse, from_below, from_above, row_table, two_on, smoothed, coarse, flag,
-                  f, s, xl, xu, yl, yu, zl, zu, inverse, end_xl, end_xu, end_total, end_inverse, rest, labels, label_sem):
+            first[d, to] = parts[d]
+
+
+def smooth_kernel(lanes, nodes, covered, own_table, block, *refs):
+    first, own_black, own_same = refs[:3]
+    own = (refs[3:9], refs[9:15])
+    own_totals = refs[15:17]
+    from_pair, from_other, row_table, two_on, smoothed, coarse, flag = refs[17:24]
+    fields, halos, others, totals, inverses = refs[24:26], refs[26:28], refs[28:30], refs[30:32], refs[32:34]
+    halo_coefficients = (refs[34:41], refs[41:48])
+    halo_inverses = refs[48:50]
+    natural = refs[50:59]
+    shown, rest, labels, label_sem = refs[59:]
     width = block.shape[3]
     own_rows = block.shape[2]
     side = smoothed.shape[1]
@@ -637,100 +693,159 @@
     fetch.start()
     grid = Stencil(width, side, plane, lanes, nodes)
     rows = grid.rows
-    halo = PAD + own_rows
     last = own_rows - 8
-    halo_beta = []
+    compact = own_rows // 2
+    even_node = (node & 1) == 0
+    halo_beta, links = [], []
+    f, s, xl, xu, yl, yu, zl, zu, total = natural
+
+    def spot(d):
+        return d % 2, slice(d // 2 * 8, d // 2 * 8 + 8)
+
     for d in range(BZB):
-        f[d, PAD:halo] = own_f[d]
         strips = []
-        for message in (from_below, from_above):
-            for k in (d % 2, 2):
-                unit = (d // 2 * 3 + k) * 3
-                strips.append(jnp.concatenate([message[unit + part] for part in range(width // 128)], axis=1))
-        field, beta, fifth_field, fifth_beta = unpack_rows(strips[0], strips[2])
-        f[d, 0:8] = field
-        f[d, halo : halo + 8] = field
-        source = jnp.where(rows < 4, strips[3], strips[1])
-        if d % 2:
-            source = jnp.where(rows < 4, fall(strips[3], 4), fall(strips[1], 4))
+        for k in (d % 2, 2):
+            unit = (d // 2 * 3 + k) * 3
+            pair, other = (
+                jnp.concatenate([message[unit + part] for part in range(width // 128)], axis=1)
+                for message in (from_pair, from_other)
+            )
+            strips.append((jnp.where(even_node, other, pair), jnp.where(even_node, pair, other)))
+        below, above = strips[0]
+        field, beta, fifth_field, fifth_beta = unpack_rows(below, above)
+        scatter_tiles(f, *spot(d), field)
+        below, above = strips[1]
+        source = jnp.where(rows < 4, above, below) if d % 2 == 0 else jnp.where(rows < 4, fall(above, 4), fall(below, 4))
         link = jnp.where((rows == 3) | (rows == 4), mean(beta, fifth_beta), 0.0)
-        s[d] = source + link * fifth_field
-        inverse[d] = link
+        scatter_tiles(s, *spot(d), source + link * fifth_field)
+        links.append(link)
         halo_beta.append(beta)
     across = grid.across(halo_beta)
-    for ref, values in zip((yl, yu, zl, zu), across):
-        for d in range(BZB):
-            ref[d] = values[d]
     for d in range(BZB):
         held = halo_beta[d]
+        for ref, values in zip((yl, yu, zl, zu), across):
+            scatter_tiles(ref, *spot(d), values[d])
         up = mean(held, jnp.where(rows == 7, fall(block[2, d, 0:8], 7), fall(held, 7)))
         up = jnp.where((rows == 3) | ((rows == 7) & grid.first_node), 0.0, up)
-        down = mean(held, fall(block[2, d, last:own_rows], 1))
-        down = jnp.where(grid.last_node, 0.0, down)
+        down = jnp.where(grid.last_node, 0.0, mean(held, fall(block[2, d, last:own_rows], 1)))
         down = jnp.where(rows == 0, down, fall(up, 1))
-        xl[d], xu[d] = down, up
-        whole = inverse[d] + down + up + across[0][d] + across[1][d] + across[2][d] + across[3][d] + grid.edges(d, held)
-        inverse[d] = 1.0 / whole
-        end_xl[d, 0:8] = jnp.where(rows == 0, fall(up, 1), fall(own_xu[d, 0:8], 1))
-        end_xu[d, 0:8] = own_xu[d, 0:8]
-        end_xl[d, 8:16] = own_xl[d, last:own_rows]
-        end_xu[d, 8:16] = jnp.where(rows == 7, fall(down, 7), own_xu[d, last:own_rows])
-        for at, start, absent in (
-            (slice(0, 8), 0, (rows == 0) & grid.first_node),
-            (slice(8, 16), last, (rows == 7) & grid.last_node),
-        ):
-            whole = own_total[d, start : start + 8] + end_xl[d, at] + end_xu[d, at]
-            whole = whole + jnp.where(absent, block[2, d, start : start + 8], 0.0)
-            end_total[d, at] = whole
-            end_inverse[d, at] = 1.0 / whole
-
-    ends = {0: slice(0, 8), last: slice(8, 16)}
-
-    def coefficients_at(r):
-        here = slice(r, r + 8)
-        across = (own_yl, own_yu, own_zl, own_zu)
-        if r in ends:
-            return lambda d: (own_s[d, here], end_xl[d, ends[r]], end_xu[d, ends[r]]) + tuple(ref[d, here] for ref in across)
-        return lambda d: tuple(ref[d, here] for ref in (own_s, own_xl, own_xu) + across)
-
-    def own_sums(r):
-        held = [f[d, r + PAD : r + PAD + 8] for d in range(BZB)]
-        lowers = [f[d, r + PAD - 1 : r + PAD + 7] for d in range(BZB)]
-        uppers = [f[d, r + PAD + 1 : r + PAD + 9] for d in range(BZB)]
-        return held, grid.sums(held, lowers, uppers, coefficients_at(r))
-
+        scatter_tiles(xl, *spot(d), down)
+        scatter_tiles(xu, *spot(d), up)
+        whole = links[d] + down + up + across[0][d] + across[1][d] + across[2][d] + across[3][d] + grid.edges(d, held)
+        scatter_tiles(total, *spot(d), whole)
+        low_link = jnp.where(rows == 0, fall(up, 1), 0.0)
+        high_link = jnp.where(rows == 7, fall(down, 7), 0.0)
+        low_whole = low_link + jnp.where((rows == 0) & grid.first_node, block[2, d, 0:8], 0.0)
+        high_whole = high_link + jnp.where((rows == 7) & grid.last_node, block[2, d, last:own_rows], 0.0)
+        for c in range(2):
+            at_low, at_high = grid.odd == (c == 1), grid.odd == (c == 0)
+            for t in range(compact // 8):
+                to = slice(8 * t, 8 * t + 8)
+                other, whole = own[c][1][d, to], own_totals[c][d, to]
+                if t == 0:
+                    other = other + jnp.where(at_low, low_link, 0.0)
+                    whole = whole + jnp.where(at_low, low_whole, 0.0)
+                if t == compact // 8 - 1:
+                    other = other + jnp.where(at_high, high_link, 0.0)
+                    whole = whole + jnp.where(at_high, high_whole, 0.0)
+                others[c][d, to] = other
+                totals[c][d, to] = whole
+                inverses[c][d, to] = 1.0 / whole
+        fields[1][d, 8 : 8 + compact] = own_black[d]
+
+    def spread(c, j):
+        tile = halos[c][j]
+        turned = fall(tile, 4)
+        fields[c][j, 8 + compact : 16 + compact] = tile
+        fields[c][j, 0:8] = turned
+        fields[c][j + 2, 8 + compact : 16 + compact] = turned
+        fields[c][j + 2, 0:8] = tile
+
+    for j in range(2):
+        even = [every_other(ref, j, 0, 8) for ref in natural]
+        odd = [every_other(ref, j, 1, 8) for ref in natural]
+        halos[1][j] = grid.split(even[0], odd[0])[1]
+        spread(1, j)
+        pairs = [(even[1], odd[1]), (even[2], odd[3])] + [(even[k], odd[k]) for k in (4, 5, 6, 7)]
+        for k, pair in enumerate(pairs):
+            at = k if k == 0 else k + 1
+            halo_coefficients[0][at][j], halo_coefficients[1][at][j] = grid.split(*pair)
+        for c in range(2):
+            halo_coefficients[c][1][j] = even[3]
+        for c, whole in enumerate(grid.split(even[8], odd[8])):
+            halo_inverses[c][j] = 1.0 / whole
+
+    def own_sums(c, t):
+        opposite = fields[1 - c]
+        start = 8 + 8 * t
+        held = [opposite[d, start : start + 8] for d in range(BZB)]
+        downs = [opposite[d, start - 1 : start + 7] for d in range(BZB)]
+        ups = [opposite[d, start + 1 : start + 9] for d in range(BZB)]
+        to = slice(8 * t, 8 * t + 8)
+
+        def coefficient(d):
+            return (own[c][0][d, to], own_same[d, to], others[c][d, to]) + tuple(ref[d, to] for ref in own[c][2:])
+
+        return grid.sums(c, held, downs, ups, grid.beyond_z, grid.ahead_z, coefficient)
+
+    def end_terms(t):
+        out = []
+        for d in range(BZB):
+            part = 0.0
+            to = slice(8 * t, 8 * t + 8)
+            if t == 0:
+                low = others[0][d, to] * fields[1][d, 7:15]
+                part = part + jnp.where((rows == 0) & ~grid.odd, low, 0.0)
+            if t == compact // 8 - 1:
+                high = others[0][d, to] * fields[1][d, 9 + 8 * t : 17 + 8 * t]
+                part = part + jnp.where((rows == 7) & grid.odd, high, 0.0)
+            out.append(first[d, to] + part)
+        return out
+
+    quarter = rows & 3
     for sweep in range(SWEEPS):
-        for colour_id in (0, 1):
-            chosen = grid.colour == colour_id
-            held = [f[d, 0:8] for d in range(BZB)]
-            lowers = [jnp.where(rows == 0, fall(f[d, halo - 8 : halo], 1), fall(held[d], 1)) for d in range(BZB)]
-            uppers = [jnp.where(rows == 7, fall(f[d, PAD : PAD + 8], 7), fall(held[d], 7)) for d in range(BZB)]
-            parts = grid.sums(held, lowers, uppers, lambda d: tuple(ref[d] for ref in (s, xl, xu, yl, yu, zl, zu)))
-            halo_new = [jnp.where(chosen, parts[d] * inverse[d], held[d]) for d in range(BZB)]
-            for r in range(0, own_rows, 8):
-                if sweep + colour_id == 0 and r not in ends:
-                    continue
-                held, parts = own_sums(r)
+        for c in (0, 1):
+            held = [halos[1 - c][j] for j in range(2)]
+            opposite = fields[1 - c]
+            downs, ups = [], []
+            for j in range(2):
+                lows = [opposite[d, compact : compact + 8] for d in (j, j + 2)]
+                highs = [opposite[d, 8:16] for d in (j, j + 2)]
+                joined = jnp.where(rows < 4, fall(lows[0], 1), fall(lows[1], 5))
+                downs.append(jnp.where(quarter == 0, joined, fall(held[j], 1)))
+                joined = jnp.where(rows < 4, fall(highs[0], 3), fall(highs[1], 7))
+                ups.append(jnp.where(quarter == 3, joined, fall(held[j], 7)))
+            parts = grid.sums(
+                c, held, downs, ups, grid.beyond_pairs, grid.ahead_pairs,
+                lambda j: tuple(ref[j] for ref in halo_coefficients[c]),
+            )
+            for j in range(2):
+                halos[c][j] = parts[j] * halo_inverses[c][j]
+                spread(c, j)
+            for t in range(compact // 8):
+                parts = end_terms(t) if sweep + c == 0 else own_sums(c, t)
                 for d in range(BZB):
-                    factor = end_inverse[d, ends[r]] if r in ends else own_inverse[d, r : r + 8]
-                    f[d, r + PAD : r + PAD + 8] = jnp.where(chosen, parts[d] * factor, held[d])
-            for d in range(BZB):
-                f[d, 0:8] = halo_new[d]
-                f[d, halo : halo + 8] = halo_new[d]
+                    fields[c][d, 8 + 8 * t : 16 + 8 * t] = parts[d] * inverses[c][d, 8 * t : 8 * t + 8]
 
     fetch.wait()
-    for r in range(0, own_rows, 8):
-        held, parts = own_sums(r)
-        wide, inner = divmod(r, side)
+    count = smoothed.shape[0]
+    for t in range(compact // 8):
+        to, own_to = slice(8 * t, 8 * t + 8), slice(8 + 8 * t, 16 + 8 * t)
+        left = [own_sums(c, t) for c in range(2)]
         for d in range(BZB):
-            whole = end_total[d, ends[r]] if r in ends else own_total[d, r : r + 8]
-            left = parts[d] - whole * held[d]
-            slot = labels[wide * BZB + d, 12].astype(jnp.int32)
-            smoothed[slot, inner : inner + 8] = held[d][:, 0:plane]
+            slot = labels[t * BZB + d, 12].astype(jnp.int32)
+            now = [fields[c][d, own_to] for c in range(2)]
+            both = left[0][d] - totals[0][d, to] * now[0] + (left[1][d] - totals[1][d, to] * now[1])
+            even, odd = grid.split(*now)
             for k in range(plane // 128):
-                rest[k, pl.ds(pl.multiple_of(slot * side + inner, 8), 8), :] = left[:, k * 128 : (k + 1) * 128]
-
-    count = smoothed.shape[0]
+                cut = slice(k * 128, (k + 1) * 128)
+                rest[k, pl.ds(pl.multiple_of(slot * 8, 8), 8), :] = both[:, cut]
+                shown[k, pl.ds(slot * side, 8, stride=2), :] = even[:, cut]
+                shown[k, pl.ds(slot * side + 1, 8, stride=2), :] = odd[:, cut]
+    for i in range(count):
+        for k in range(plane // 128):
+            smoothed[i, :, k * 128 : (k + 1) * 128] = shown[k, i * side : (i + 1) * side]
+
     small = side // 2
     cells = lax.broadcasted_iota(jnp.int32, (plane, 128), 0)
     slots = lax.broadcasted_iota(jnp.int32, (plane, 128), 1)
@@ -742,9 +857,8 @@
         stack = []
         for pair in range(pairs):
             i = pair * (128 // per) + inner
-            even = [rest[k, pl.ds(2 * i, count, stride=side), :] for k in range(plane // 128)]
-            odd = [rest[k, pl.ds(2 * i + 1, count, stride=side), :] for k in range(plane // 128)]
-            stack.append(jnp.concatenate(even, axis=1) + jnp.concatenate(odd, axis=1))
+            tiles = [rest[k, pl.ds(i, count, stride=small), :] for k in range(plane // 128)]
+            stack.append(jnp.concatenate(tiles, axis=1))
         pooling = (goal + inner * per == slots).astype(jnp.float32)
         acc = acc + jnp.dot(
             jnp.concatenate(stack, axis=0), pooling, precision=lax.Precision.HIGHEST, preferred_element_type=jnp.float32
@@ -752,13 +866,14 @@
     for pair in range(pairs):
         coarse[:, pair * 128 : (pair + 1) * 128] = 0.125 * acc[pair * count : (pair + 1) * count]
 
-    mine = from_below.shape[0] - 1
+    mine = from_pair.shape[0] - 1
     rows1 = lax.broadcasted_iota(jnp.int32, (8, 128), 0)
     cols1 = lax.broadcasted_iota(jnp.int32, (8, 128), 1)
     owner = lax.rem(lax.div(cols1, 8), 8)
     field_of = lax.rem(cols1, 8)
     table_here, opposite = row_table[...], two_on[...]
-    lower, upper = from_below[mine], from_above[mine]
+    pair, other = from_pair[mine], from_other[mine]
+    lower, upper = jnp.where(even_node, other, pair), jnp.where(even_node, pair, other)
     rows_of = [(table_here, lower, upper, node), (lower, opposite, table_here, lax.rem(node + nodes - 1, nodes)),
                (upper, table_here, opposite, lax.rem(node + 1, nodes)), (opposite, upper, lower, lax.rem(node + 2, nodes))]
     if not covered:
@@ -804,11 +919,16 @@
         out_shape=[pltpu.VMEM((n, side, half), f32) for n in units]
         + [pltpu.VMEM(array.shape, array.dtype) for array in arrays]
         + [pltpu.VMEM((8, 128), f32)],
-        in_specs=[SCALARS] * 2 + [pl.BlockSpec(memory_space=pltpu.HBM)] * 5,
+        in_specs=[pl.BlockSpec(memory_space=pltpu.HBM)] * 5,
         out_specs=[VECTORS] * (len(units) + 6),
-        scratch_shapes=[pltpu.SMEM((count,), jnp.int32), pltpu.SemaphoreType.DMA((5,))],
+        scratch_shapes=[
+            pltpu.SMEM(target_box.shape, jnp.int32),
+            pltpu.SMEM(neighbours.shape, jnp.int32),
+            pltpu.SMEM((count,), jnp.int32),
+            pltpu.SemaphoreType.DMA((7,)),
+        ],
         compiler_params=FULL,
-    )(target_box, neighbours, *arrays)
+    )(*arrays)
     messages, own_table = packed[:-6], packed[-1]
     field, source, beta, target_held, neighbours_held = packed[-6:-1]
     got = {}
@@ -822,7 +942,7 @@
     width = plane + 128
     strips = BZB // 2 * 9 + 1
     sides = pltpu.VMEM((5, BZB + 1, BXD * side, 128), f32)
-    block, fifth, upward, downward, row_table = pl.pallas_call(
+    block, fifth, to_pair, to_other, row_table = pl.pallas_call(
         lambda *refs: assemble_kernel(moves, plan, lanes, count, *refs),
         name="assemble_block",
         out_shape=[
@@ -842,19 +962,21 @@
         ],
         compiler_params=ROOM,
     )(own_table, field, source, beta, *got)
-    from_below = lax.ppermute(upward, "node", [(i, (i + 1) % nodes) for i in range(nodes)])
-    from_above = lax.ppermute(downward, "node", [(i, (i - 1) % nodes) for i in range(nodes)])
+    from_pair = lax.ppermute(to_pair, "node", [(i, i ^ 1) for i in range(nodes)])
+    from_other = lax.ppermute(to_other, "node", [(i, (i - 1 + 2 * (i % 2)) % nodes) for i in range(nodes)])
     two_on = lax.ppermute(row_table, "node", [(i, (i + 2) % nodes) for i in range(nodes)])
-    own_shape = pltpu.VMEM((BZB, BXD * side, width), f32)
+    tiles, rows = width // 128, BXD * side
+    half_rows = pltpu.VMEM((BZB, rows // 2, width), f32)
     coupled = pl.pallas_call(
         lambda *refs: couple_kernel(lanes, nodes, plane, *refs),
         name="couple_block",
-        out_shape=[own_shape] * 10,
+        out_shape=[half_rows] * 17,
         in_specs=[VECTORS] * 2,
-        out_specs=[VECTORS] * 10,
+        out_specs=[VECTORS] * 17,
+        scratch_shapes=[pltpu.VMEM((tiles, BZB, rows, 128), f32)] * 9,
         compiler_params=ROOM,
     )(block, fifth)
-    tile, two_tiles = pltpu.VMEM((BZB, 8, width), f32), pltpu.VMEM((BZB, 16, width), f32)
+    pair_tile = pltpu.VMEM((2, 8, width), f32)
     smoothed, coarse, flag = pl.pallas_call(
         lambda *refs: smooth_kernel(lanes, nodes, covered, *refs),
         name="smooth_block",
@@ -863,14 +985,17 @@
             jax.ShapeDtypeStruct((count, (side // 2) ** 3), f32),
             jax.ShapeDtypeStruct((1, 1), jnp.int32),
         ],
-        in_specs=[VECTORS] * 16,
+        in_specs=[VECTORS] * (2 + 17 + 4),
         out_specs=[VECTORS, VECTORS, SCALARS],
-        scratch_shapes=[pltpu.VMEM((BZB, BXD * side + 2 * PAD, width), f32)]
-        + [tile] * 8
-        + [two_tiles] * 4
-        + [pltpu.VMEM((plane // 128, count * side, 128), f32), pltpu.SMEM((8, 128), f32), pltpu.SemaphoreType.DMA],
+        scratch_shapes=[pltpu.VMEM((BZB, rows // 2 + 16, width), f32)] * 2
+        + [pair_tile] * 2
+        + [half_rows] * 6
+        + [pair_tile] * 16
+        + [pltpu.VMEM((tiles, 2, 16, 128), f32)] * 9
+        + [pltpu.VMEM((plane // 128, count * side, 128), f32), pltpu.VMEM((plane // 128, count * side // 2, 128), f32)]
+        + [pltpu.SMEM((8, 128), f32), pltpu.SemaphoreType.DMA],
         compiler_params=ROOM,
-    )(own_table, block, *coupled, from_below, from_above, row_table, two_on)
+    )(own_table, block, *coupled, from_pair, from_other, row_table, two_on)
     irregular = flag[0, 0]
     if not covered:
         irregular = lax.pmax(irregular, ("node", "lane"))

time: 33.9 us -> 31.9 us (0.941)
  Pallas kernels: 8.65 us -> 7.22 us
  starting transfers between devices: 17.1 us -> 16 us
  waiting for transfers between devices: 6.39 us -> 6.95 us
    ppermute x1, starting transfers between devices: 1.52 us -> 0.51 us  [fast_body(): lax.ppermute(row_table, 'node', [(i, (i + 2) % nodes) for i in range(node...]
    pallas_call x1, Pallas kernels: 3.15 us -> 2.29 us  [fast_body(): pl.pallas_call(lambda *refs: smooth_kernel(lanes, nodes, covered, *refs),...]
    pallas_call x1, Pallas kernels: 2.99 us -> 2.28 us  [fast_body(): pl.pallas_call(lambda *refs: pack_kernel(moves, plan, lanes, count, *refs...]
    ppermute x1, waiting for transfers between devices: 1.57 us -> 2.13 us  [fast_body(): lax.ppermute(row_table, 'node', [(i, (i + 2) % nodes) for i in range(node...]
  transfers between devices with their start and end apart: 10 -> 10, of which waited for: 3 -> 3; matrix products, arithmetic and copies ran while one was open for 0% -> 0% of each run, Pallas kernels for 2% -> 3%
where the time goes in v5:
time: 31.9 us; the launch traced here: 31.7 us
  starting transfers between devices  16 us (50%)
  Pallas kernels  7.22 us (23%)
  waiting for transfers between devices  6.95 us (22%)
  between operations  0.84 us (3%)
  loops' own time  0.76 us (2%)
    ppermute x7, starting transfers between devices, fast_body(): lax.ppermute(message, 'lane', [(i, (i + offset) % lanes) for i in range(l...  13.8 us
    ppermute x7, waiting for transfers between devices, fast_body(): lax.ppermute(message, 'lane', [(i, (i + offset) % lanes) for i in range(l...  4.82 us
    pallas_call x1, Pallas kernels, fast_body(): pl.pallas_call(lambda *refs: smooth_kernel(lanes, nodes, covered, *refs),...  2.29 us
    pallas_call x1, Pallas kernels, fast_body(): pl.pallas_call(lambda *refs: pack_kernel(moves, plan, lanes, count, *refs...  2.28 us
    ppermute x1, waiting for transfers between devices, fast_body(): lax.ppermute(row_table, 'node', [(i, (i + 2) % nodes) for i in range(node...  2.13 us
    pallas_call x1, Pallas kernels, fast_body(): pl.pallas_call(lambda *refs: assemble_kernel(moves, plan, lanes, count, *...  1.68 us
    ppermute x1, starting transfers between devices, fast_body(): lax.ppermute(to_other, 'node', [(i, (i - 1 + 2 * (i % 2)) % nodes) for i...  1.64 us
    pallas_call x1, Pallas kernels, fast_body(): pl.pallas_call(lambda *refs: couple_kernel(lanes, nodes, plane, *refs), n...  0.96 us
  transfers between devices with their start and end apart: 10, of which 3 were waited for; matrix products, arithmetic and copies ran while one was open for 0% of the time, Pallas kernels for 3%

profile of v5, /device:TPU:0, one launch (start us, length us, event | category | flops | bytes accessed | tf_op | source)
XLA Modules:
  0.0 31.7 jit_solution(16909591516419622863)
XLA Ops:
  0.6 2.3 %pack_moves.1 = (f32[17,16,128]{2,1,0:T(8,128)S(1)}, f32[5,16,128]{2,1,0:T(8,128)S(1)}, f32[3,16,128]{2,1,0:T(8,128)S(1)}, f32[4,16,128]{2,1,0:T(8,128)S(1)}, f3...) custom-call(f32[8,16,256]{2,1,0:T(8,128)} %refs_0_.1, ...), custom_call_target="tpu_custom_call" | custom-call | tf_op jit(solution)/shard_map/pack_moves/pallas_call | solution.py:916
  2.9 3.0 %collective-permute-start.20 = (f32[17,16,128]{2,1,0:T(8,128)S(1)}, f32[17,16,128]{2,1,0:T(8,128)S(1)}, u32[]{:S(2)}, u32[]{:S(2)}) collective-permute-start(f32[17,16,128]{2,1,0:T(8,128)S(1)} %get-tuple-element.91), channel_id=1, source_target_pairs={{0,1},{1,2},{2,3},{3,4},{4,5},{5,6},{6,7},{7,0},{8,9},{9,10},{10,1... | collective-permute-start | bytes 417800 | tf_op jit(solution)/shard_map/ppermute | solution.py:940
  5.9 3.1 %collective-permute-start.26 = (f32[17,16,128]{2,1,0:T(8,128)S(1)}, f32[17,16,128]{2,1,0:T(8,128)S(1)}, u32[]{:S(2)}, u32[]{:S(2)}) collective-permute-start(f32[17,16,128]{2,1,0:T(8,128)S(1)} %get-tuple-element.99), channel_id=1, source_target_pairs={{0,7},{1,0},{2,1},{3,2},{4,3},{5,4},{6,5},{7,6},{8,15},{9,8},{10,9... | collective-permute-start | bytes 417800 | tf_op jit(solution)/shard_map/ppermute | solution.py:940
  9.0 0.0 collective-permute-start.21
  9.0 2.5 %collective-permute-start.23 = (f32[4,16,128]{2,1,0:T(8,128)S(1)}, f32[4,16,128]{2,1,0:T(8,128)S(1)}, u32[]{:S(2)}, u32[]{:S(2)}) collective-permute-start(f32[4,16,128]{2,1,0:T(8,128)S(1)} %get-tuple-element.95), channel_id=1, source_target_pairs={{0,4},{1,5},{2,6},{3,7},{4,0},{5,1},{6,2},{7,3},{8,12},{9,13},{10,... | collective-permute-start | bytes 98312 | tf_op jit(solution)/shard_map/ppermute | solution.py:940
  11.5 1.3 %collective-permute-start.25 = (f32[5,16,128]{2,1,0:T(8,128)S(1)}, f32[5,16,128]{2,1,0:T(8,128)S(1)}, u32[]{:S(2)}, u32[]{:S(2)}) collective-permute-start(f32[5,16,128]{2,1,0:T(8,128)S(1)} %get-tuple-element.98), channel_id=1, source_target_pairs={{0,6},{1,7},{2,0},{3,1},{4,2},{5,3},{6,4},{7,5},{8,14},{9,15},{10,... | collective-permute-start | bytes 122888 | tf_op jit(solution)/shard_map/ppermute | solution.py:940
  12.9 3.0 %collective-permute-done.21.refs_5_ = f32[5,16,128]{2,1,0:T(8,128)S(1)} collective-permute-done((f32[5,16,128]{2,1,0:T(8,128)S(1)}, f32[5,16,128]{2,1,0:T(8,128)S(1)}, u32[]{:S(2)}, u32[]{:S(2)}) %collective-permute-start.21) | collective-permute-done | bytes 40992 | tf_op jit(solution)/shard_map/ppermute | solution.py:940
  15.9 0.0 collective-permute-start.22
  15.9 0.0 collective-permute-done.23.refs_7_
  15.9 3.8 %collective-permute-start.24 = (f32[3,16,128]{2,1,0:T(8,128)S(1)}, f32[3,16,128]{2,1,0:T(8,128)S(1)}, u32[]{:S(2)}, u32[]{:S(2)}) collective-permute-start(f32[3,16,128]{2,1,0:T(8,128)S(1)} %get-tuple-element.97), channel_id=1, source_target_pairs={{0,5},{1,6},{2,7},{3,0},{4,1},{5,2},{6,3},{7,4},{8,13},{9,14},{10,... | collective-permute-start | bytes 73736 | tf_op jit(solution)/shard_map/ppermute | solution.py:940
  19.7 0.0 collective-permute-done.25.refs_9_
  19.7 1.8 %collective-permute-done.22.refs_6_ = f32[3,16,128]{2,1,0:T(8,128)S(1)} collective-permute-done((f32[3,16,128]{2,1,0:T(8,128)S(1)}, f32[3,16,128]{2,1,0:T(8,128)S(1)}, u32[]{:S(2)}, u32[]{:S(2)}) %collective-permute-start.22) | collective-permute-done | bytes 24608 | tf_op jit(solution)/shard_map/ppermute | solution.py:940
  21.5 0.0 collective-permute-done.24.refs_8_
  21.5 0.0 collective-permute-done.20.refs_4_
  21.5 1.7 %assemble_block.1 = (f32[3,5,32,384]{3,2,1,0:T(8,128)S(1)}, f32[2,4,32,128]{3,2,1,0:T(8,128)S(1)}, f32[19,8,128]{2,1,0:T(8,128)S(1)}, f32[19,8,128]{2,1,0:T(8,128)S(1)}, f32[8,128]{1,0:T(8,128)S(1)}) custom-call(f32[8,128]{1,0:T(8,128)S(1)} %get-tuple-element.87.refs_0_, f32[8,16,256]{2,1,0:T(8,128)S(1)} %get-tuple-element.343.refs_1_, ...), custom_call_target="tpu_custom_call" | custom-call | tf_op jit(solution)/shard_map/assemble_block/pallas_call | solution.py:945
  23.2 0.1 collective-permute-start.27
  23.3 1.6 %collective-permute-start.28 = (f32[19,8,128]{2,1,0:T(8,128)S(1)}, f32[19,8,128]{2,1,0:T(8,128)S(1)}, u32[]{:S(2)}, u32[]{:S(2)}) collective-permute-start(f32[19,8,128]{2,1,0:T(8,128)S(1)} %get-tuple-element.120), channel_id=1, source_target_pairs={{0,24},{8,16},{16,8},{24,0},{1,25},{9,17},{17,9},{25,1},{2,26},{10... | collective-permute-start | bytes 233480 | tf_op jit(solution)/shard_map/ppermute | solution.py:966
  24.9 0.5 %collective-permute-start.29 = (f32[8,128]{1,0:T(8,128)S(1)}, f32[8,128]{1,0:T(8,128)S(1)}, u32[]{:S(2)}, u32[]{:S(2)}) collective-permute-start(f32[8,128]{1,0:T(8,128)S(1)} %get-tuple-element.121.refs_21_), channel_id=1, source_target_pairs={{0,16},{8,24},{16,0},{24,8},{1,17},{9,25},{17,1},{25,9},{2,18},{10... | collective-permute-start | bytes 12296 | tf_op jit(solution)/shard_map/ppermute | solution.py:967
  25.4 1.0 %couple_block.1 = (f32[4,16,384]{2,1,0:T(8,128)S(1)}, f32[4,16,384]{2,1,0:T(8,128)S(1)}, f32[4,16,384]{2,1,0:T(8,128)S(1)}, f32[4,16,384]{2,1,0:T(8,128)S(1)}, f...) custom-call(f32[3,5,32,384]{3,2,1,0:T(8,128)S(1)} %get-tuple-element, ...), custom_call_target="tpu_custom_call" | custom-call | tf_op jit(solution)/shard_map/couple_block/pallas_call | solution.py:970
  26.4 2.1 %collective-permute-done.29.refs_22_ = f32[8,128]{1,0:T(8,128)S(1)} collective-permute-done((f32[8,128]{1,0:T(8,128)S(1)}, f32[8,128]{1,0:T(8,128)S(1)}, u32[]{:S(2)}, u32[]{:S(2)}) %collective-permute-start.29) | collective-permute-done | bytes 4128 | tf_op jit(solution)/shard_map/ppermute | solution.py:967
  28.5 0.0 collective-permute-done.27.refs_19_
  28.5 0.0 collective-permute-done.28.refs_20_
  28.5 2.3 %smooth_block.1 = (f32[8,16,256]{2,1,0:T(8,128)}, f32[8,512]{1,0:T(8,128)}, s32[1,1]{1,0:T(1,128)}) custom-call(f32[8,128]{1,0:T(8,128)S(1)} %get-tuple-element.87.refs_0_, f32[3,5,32,384]{3,2,1,0:T(8,128)S(1)} %get-tuple-element.100.refs_0_.refs_1_, f32[4,16,384]{2,1,0:T(8,128)S(1)} %get-tuple-element.102.refs_2_, ...), custom_call_target="tpu_custom_call" | custom-call | tf_op jit(solution)/shard_map/smooth_block/pallas_call | solution.py:980
  30.8 0.8 %while.12 = (f32[8,16,256]{2,1,0:T(8,128)}, f32[8,512]{1,0:T(8,128)}, s32[]{:T(128)}, s32[8]{0:T(128)S(1)}, f32[8,16,256]{2,1,0:T(8,128)S(1)}, /*index=5*/f32[8,...) while((f32[8,16,256]{2,1,0:T(8,128)}, f32[8,512]{1,0:T(8,128)}, s32[]{:T(128)}, ...), condition=%region_7.8_spmd.clone, body=%region_0.7_spmd.sunk.clone | while | flops 21889904 | bytes 78598984 | solution.py:1007
  (1 shorter events, 0.0 us)
Async XLA Ops:
  2.9 18.6 %collective-permute-start.20 = (f32[17,16,128]{2,1,0:T(8,128)S(1)}, f32[17,16,128]{2,1,0:T(8,128)S(1)}, u32[]{:S(2)}, u32[]{:S(2)}) collective-permute-start(f32[17,16,128]{2,1,0:T(8,128)S(1)} %get-tuple-element.91), channel_id=1, source_target_pairs={{0,1},{1,2},{2,3},{3,4},{4,5},{5,6},{6,7},{7,0},{8,9},{9,10},{10,1... | collective-permute-start | bytes 417800 | tf_op jit(solution)/shard_map/ppermute | solution.py:940
  5.9 15.6 %collective-permute-start.26 = (f32[17,16,128]{2,1,0:T(8,128)S(1)}, f32[17,16,128]{2,1,0:T(8,128)S(1)}, u32[]{:S(2)}, u32[]{:S(2)}) collective-permute-start(f32[17,16,128]{2,1,0:T(8,128)S(1)} %get-tuple-element.99), channel_id=1, source_target_pairs={{0,7},{1,0},{2,1},{3,2},{4,3},{5,4},{6,5},{7,6},{8,15},{9,8},{10,9... | collective-permute-start | bytes 417800 | tf_op jit(solution)/shard_map/ppermute | solution.py:940
  9.0 6.9 %collective-permute-start.21 = (f32[5,16,128]{2,1,0:T(8,128)S(1)}, f32[5,16,128]{2,1,0:T(8,128)S(1)}, u32[]{:S(2)}, u32[]{:S(2)}) collective-permute-start(f32[5,16,128]{2,1,0:T(8,128)S(1)} %get-tuple-element.92), channel_id=1, source_target_pairs={{0,2},{1,3},{2,4},{3,5},{4,6},{5,7},{6,0},{7,1},{8,10},{9,11},{10,... | collective-permute-start | bytes 122888 | tf_op jit(solution)/shard_map/ppermute | solution.py:940
  9.0 6.9 %collective-permute-start.23 = (f32[4,16,128]{2,1,0:T(8,128)S(1)}, f32[4,16,128]{2,1,0:T(8,128)S(1)}, u32[]{:S(2)}, u32[]{:S(2)}) collective-permute-start(f32[4,16,128]{2,1,0:T(8,128)S(1)} %get-tuple-element.95), channel_id=1, source_target_pairs={{0,4},{1,5},{2,6},{3,7},{4,0},{5,1},{6,2},{7,3},{8,12},{9,13},{10,... | collective-permute-start | bytes 98312 | tf_op jit(solution)/shard_map/ppermute | solution.py:940
  11.5 8.2 %collective-permute-start.25 = (f32[5,16,128]{2,1,0:T(8,128)S(1)}, f32[5,16,128]{2,1,0:T(8,128)S(1)}, u32[]{:S(2)}, u32[]{:S(2)}) collective-permute-start(f32[5,16,128]{2,1,0:T(8,128)S(1)} %get-tuple-element.98), channel_id=1, source_target_pairs={{0,6},{1,7},{2,0},{3,1},{4,2},{5,3},{6,4},{7,5},{8,14},{9,15},{10,... | collective-permute-start | bytes 122888 | tf_op jit(solution)/shard_map/ppermute | solution.py:940
  15.9 5.6 %collective-permute-start.22 = (f32[3,16,128]{2,1,0:T(8,128)S(1)}, f32[3,16,128]{2,1,0:T(8,128)S(1)}, u32[]{:S(2)}, u32[]{:S(2)}) collective-permute-start(f32[3,16,128]{2,1,0:T(8,128)S(1)} %get-tuple-element.94), channel_id=1, source_target_pairs={{0,3},{1,4},{2,5},{3,6},{4,7},{5,0},{6,1},{7,2},{8,11},{9,12},{10,... | collective-permute-start | bytes 73736 | tf_op jit(solution)/shard_map/ppermute | solution.py:940
  15.9 5.6 %collective-permute-start.24 = (f32[3,16,128]{2,1,0:T(8,128)S(1)}, f32[3,16,128]{2,1,0:T(8,128)S(1)}, u32[]{:S(2)}, u32[]{:S(2)}) collective-permute-start(f32[3,16,128]{2,1,0:T(8,128)S(1)} %get-tuple-element.97), channel_id=1, source_target_pairs={{0,5},{1,6},{2,7},{3,0},{4,1},{5,2},{6,3},{7,4},{8,13},{9,14},{10,... | collective-permute-start | bytes 73736 | tf_op jit(solution)/shard_map/ppermute | solution.py:940
  23.2 5.3 %collective-permute-start.27 = (f32[19,8,128]{2,1,0:T(8,128)S(1)}, f32[19,8,128]{2,1,0:T(8,128)S(1)}, u32[]{:S(2)}, u32[]{:S(2)}) collective-permute-start(f32[19,8,128]{2,1,0:T(8,128)S(1)} %get-tuple-element.119), channel_id=1, source_target_pairs={{0,8},{8,0},{16,24},{24,16},{1,9},{9,1},{17,25},{25,17},{2,10},{10... | collective-permute-start | bytes 233480 | tf_op jit(solution)/shard_map/ppermute | solution.py:965
  23.3 5.2 %collective-permute-start.28 = (f32[19,8,128]{2,1,0:T(8,128)S(1)}, f32[19,8,128]{2,1,0:T(8,128)S(1)}, u32[]{:S(2)}, u32[]{:S(2)}) collective-permute-start(f32[19,8,128]{2,1,0:T(8,128)S(1)} %get-tuple-element.120), channel_id=1, source_target_pairs={{0,24},{8,16},{16,8},{24,0},{1,25},{9,17},{17,9},{25,1},{2,26},{10... | collective-permute-start | bytes 233480 | tf_op jit(solution)/shard_map/ppermute | solution.py:966
  24.9 3.6 %collective-permute-start.29 = (f32[8,128]{1,0:T(8,128)S(1)}, f32[8,128]{1,0:T(8,128)S(1)}, u32[]{:S(2)}, u32[]{:S(2)}) collective-permute-start(f32[8,128]{1,0:T(8,128)S(1)} %get-tuple-element.121.refs_21_), channel_id=1, source_target_pairs={{0,16},{8,24},{16,0},{24,8},{1,17},{9,25},{17,1},{25,9},{2,18},{10... | collective-permute-start | bytes 12296 | tf_op jit(solution)/shard_map/ppermute | solution.py:967

commit v6 on v5

--- a/solution.py
+++ b/solution.py
@@ -313,7 +313,7 @@
             further, onward = local(at, 4)
             live, at = live & further, onward
         spot = jnp.where(inside, BZB, 0) + depth
-        place.append((depth, jnp.where(inside, side, 0)))
+        place.append(spot)
         slots[spot] = i
     rows = lax.broadcasted_iota(jnp.int32, (8, 128), 0)
     cols = lax.broadcasted_iota(jnp.int32, (8, 128), 1)
@@ -329,12 +329,15 @@
         held = put(held, i, 0, jnp.where(slot < 0, -7, first + slot))
         for face in range(6):
             held = put(held, i, 1 + face, near[jnp.maximum(slot, 0), face])
-        held = put(held, i, 7, place[i][0])
-        held = put(held, i, 11, place[i][1])
-        held = put(held, i, 9, stay[i])
-    for k in range(len(moves)):
-        held = put(held, k, 8, new_slot[k])
-        held = put(held, k, 10, old_index[k])
+    words = [
+        sum(place[i] << 3 * i for i in range(count)),
+        sum((stay[i] + 1) << 4 * i for i in range(count // 2)),
+        sum((stay[i] + 1) << 4 * (i - count // 2) for i in range(count // 2, count)),
+        sum((new_slot[k] + 1) << 4 * k for k in range(len(moves))),
+        sum(old_index[k] << 3 * k for k in range(len(moves))),
+    ]
+    for k, word in enumerate(words):
+        held = put(held, 0, 16 + k, word)
     table[...] = held.astype(jnp.float32)
     for copy in fetch[2:]:
         copy.wait()
@@ -369,19 +372,17 @@
 def assemble_kernel(moves, plan, lanes, count, *refs):
     own_table, field, source, beta = refs[:4]
     got = dict(zip(plan, refs[4 : 4 + len(plan)]))
-    block, fifth, to_pair, to_other, row_table, low_side, high_side, tables, table_sems = refs[4 + len(plan) :]
+    block, fifth, to_pair, to_other, row_table, low_side, high_side = refs[4 + len(plan) :]
     side, plane = field.shape[1:]
     half = plane // 2
-    order = list(plan) + [0]
 
     def table_of(offset):
         return got[offset].at[got[offset].shape[0] - 1, 0:8] if offset else own_table
 
-    fetch = [
-        pltpu.make_async_copy(table_of(offset), tables.at[k], table_sems.at[k]) for k, offset in enumerate(order)
-    ]
-    for copy in fetch:
-        copy.start()
+    words = {}
+    for offset in (0, *plan):
+        line = table_of(offset)[0:1, :].astype(jnp.int32)
+        words[offset] = [line[0, 16 + k] for k in range(5)]
 
     cols = lax.broadcasted_iota(jnp.int32, (8, 128), 1)
     shown = [offset for offset in plan if lanes == 8 or offset in (1, lanes - 1)]
@@ -394,15 +395,19 @@
     to_pair[to_pair.shape[0] - 1] = joined
     to_other[to_other.shape[0] - 1] = joined
 
-    for copy in fetch:
-        copy.wait()
-
-    def said(offset, row, col):
-        return tables[order.index(offset), row, col].astype(jnp.int32)
+    def place_of(offset, slot):
+        code = (words[offset][0] >> 3 * slot) & 7
+        return code & (BZB - 1), (code >> 2) * side
+
+    def stays(offset, i):
+        return ((words[offset][1 + i // (count // 2)] >> 4 * (i % (count // 2))) & 15) - 1
+
+    def moved(offset, k):
+        return ((words[offset][3] >> 4 * k) & 15) - 1
 
     def spot_at(offset, slot):
-        at = jnp.maximum(slot, 0)
-        return jnp.where(slot >= 0, said(offset, at, 7), BZB), jnp.where(slot >= 0, said(offset, at, 11), 0)
+        deep, row = place_of(offset, jnp.maximum(slot, 0))
+        return jnp.where(slot >= 0, deep, BZB), jnp.where(slot >= 0, row, 0)
 
     def put(ref, array, spot, values, where=slice(None)):
         deep, row = spot
@@ -410,8 +415,8 @@
 
     low, high, whole = slice(0, half), slice(half, plane), slice(0, plane)
     for i in range(count):
-        put(block, 2, (said(0, i, 7), said(0, i, 11)), beta[i], whole)
-        spot = spot_at(0, said(0, i, 9))
+        put(block, 2, place_of(0, i), beta[i], whole)
+        spot = spot_at(0, stays(0, i))
         put(block, 0, spot, field[i], whole)
         put(block, 1, spot, source[i], whole)
 
@@ -427,9 +432,9 @@
 
     for move, part in ((1, LOW), (lanes - 1, HIGH)):
         k = moves.index(move)
-        box, cut = said(0, k, 10), part_lanes(part, plane)
+        box, cut = (words[0][4] >> 3 * k) & 7, part_lanes(part, plane)
         raw = field[box, :, cut]
-        put_end(part, said(0, k, 8), raw, raw, source[box, :, cut])
+        put_end(part, moved(0, k), raw, raw, source[box, :, cut])
 
     for offset, (bulk, entire, kept) in plan.items():
         message = got[offset]
@@ -438,14 +443,14 @@
             ref, _, shift = sides[bulk]
             for i in range(count):
                 packed = message[i]
-                put_end(bulk, said(offset, i, 9), unpack_end(bulk, packed), packed, packed)
+                put_end(bulk, stays(offset, i), unpack_end(bulk, packed), packed, packed)
                 joint = message[count + i // 2]
-                spot = said(offset, i, 7), said(offset, i, 11)
+                spot = place_of(offset, i)
                 put(ref, 2, spot, joint if i % 2 == 0 else turn(joint, 64))
                 put(ref, 4, spot, turn(packed, 2 * shift))
             unit = count + count // 2
         if entire:
-            spot = spot_at(0, said(offset, moves.index(offset), 8))
+            spot = spot_at(0, moved(offset, moves.index(offset)))
             first, second = unpack_whole(message[unit])
             put(block, 0, spot, first, low)
             put(block, 0, spot, second, high)
@@ -454,7 +459,7 @@
             unit += 3
         for move, part in kept:
             packed = message[unit]
-            put_end(part, said(offset, moves.index(move), 8), unpack_end(part, packed), packed, packed)
+            put_end(part, moved(offset, moves.index(move)), unpack_end(part, packed), packed, packed)
             unit += 1
 
     rows, width = block.shape[2:]
@@ -932,10 +937,11 @@
     messages, own_table = packed[:-6], packed[-1]
     field, source, beta, target_held, neighbours_held = packed[-6:-1]
     got = {}
-    early = [offset for offset in plan if offset in moves]
-    for offset in early + [offset for offset in plan if offset not in moves]:
+    late = [lanes // 2, lanes // 2 + 1]
+    near = [1, lanes - 1, 2, lanes - 2]
+    for offset in near + [offset for offset in plan if offset not in near + late] + late:
         message = messages[list(plan).index(offset)]
-        if offset not in moves:
+        if offset in late:
             message, _ = lax.optimization_barrier((message, got[2]))
         got[offset] = lax.ppermute(message, "lane", [(i, (i + offset) % lanes) for i in range(lanes)])
     got = [got[offset] for offset in plan]
@@ -957,8 +963,6 @@
         scratch_shapes=[
             sides,
             sides,
-            pltpu.SMEM((len(units) + 1, 8, 128), f32),
-            pltpu.SemaphoreType.DMA((len(units) + 1,)),
         ],
         compiler_params=ROOM,
     )(own_table, field, source, beta, *got)

time: 31.9 us -> 29.9 us (0.937)
  starting transfers between devices: 16 us -> 14.1 us
  Pallas kernels: 7.22 us -> 6.12 us
  waiting for transfers between devices: 6.95 us -> 7.98 us
    ppermute x7, starting transfers between devices: 13.8 us -> 11.9 us  [fast_body(): lax.ppermute(message, 'lane', [(i, (i + offset) % lanes) for i in range(l...]
    pallas_call x1, Pallas kernels: 1.68 us -> 0.59 us  [fast_body(): pl.pallas_call(lambda *refs: assemble_kernel(moves, plan, lanes, count, *...]
    ppermute x7, waiting for transfers between devices: 4.82 us -> 5.84 us  [fast_body(): lax.ppermute(message, 'lane', [(i, (i + offset) % lanes) for i in range(l...]
  transfers between devices with their start and end apart: 10 -> 10, of which waited for: 3 -> 4; matrix products, arithmetic and copies ran while one was open for 0% -> 0% of each run, Pallas kernels for 3% -> 3%
where the time goes in v6:
time: 29.9 us; the launch traced here: 29.8 us
  starting transfers between devices  14.1 us (47%)
  waiting for transfers between devices  7.98 us (27%)
  Pallas kernels  6.12 us (20%)
  between operations  0.84 us (3%)
  loops' own time  0.76 us (3%)
    ppermute x7, starting transfers between devices, fast_body(): lax.ppermute(message, 'lane', [(i, (i + offset) % lanes) for i in range(l...  11.9 us
    ppermute x7, waiting for transfers between devices, fast_body(): lax.ppermute(message, 'lane', [(i, (i + offset) % lanes) for i in range(l...  5.84 us
    pallas_call x1, Pallas kernels, fast_body(): pl.pallas_call(lambda *refs: smooth_kernel(lanes, nodes, covered, *refs),...  2.29 us
    pallas_call x1, Pallas kernels, fast_body(): pl.pallas_call(lambda *refs: pack_kernel(moves, plan, lanes, count, *refs...  2.27 us
    ppermute x1, waiting for transfers between devices, fast_body(): lax.ppermute(row_table, 'node', [(i, (i + 2) % nodes) for i in range(node...  2.13 us
    ppermute x1, starting transfers between devices, fast_body(): lax.ppermute(to_other, 'node', [(i, (i - 1 + 2 * (i % 2)) % nodes) for i...  1.64 us
    pallas_call x1, Pallas kernels, fast_body(): pl.pallas_call(lambda *refs: couple_kernel(lanes, nodes, plane, *refs), n...  0.96 us
    another operation x1, loops' own time, fast_body(): lax.while_loop(lambda carry: carry[2] > 0, again, (smoothed, coarse, irre...  0.76 us
  transfers between devices with their start and end apart: 10, of which 4 were waited for; matrix products, arithmetic and copies ran while one was open for 0% of the time, Pallas kernels for 3%

profile of v6, /device:TPU:0, one launch (start us, length us, event | category | flops | bytes accessed | tf_op | source)
XLA Modules:
  0.0 29.8 jit_solution(1735126770668001825)
XLA Ops:
  0.6 2.3 %pack_moves.1 = (f32[17,16,128]{2,1,0:T(8,128)S(1)}, f32[5,16,128]{2,1,0:T(8,128)S(1)}, f32[3,16,128]{2,1,0:T(8,128)S(1)}, f32[4,16,128]{2,1,0:T(8,128)S(1)}, f3...) custom-call(f32[8,16,256]{2,1,0:T(8,128)} %refs_0_.1, ...), custom_call_target="tpu_custom_call" | custom-call | tf_op jit(solution)/shard_map/pack_moves/pallas_call | solution.py:921
  2.9 3.0 %collective-permute-start.20 = (f32[17,16,128]{2,1,0:T(8,128)S(1)}, f32[17,16,128]{2,1,0:T(8,128)S(1)}, u32[]{:S(2)}, u32[]{:S(2)}) collective-permute-start(f32[17,16,128]{2,1,0:T(8,128)S(1)} %get-tuple-element.91), channel_id=1, source_target_pairs={{0,1},{1,2},{2,3},{3,4},{4,5},{5,6},{6,7},{7,0},{8,9},{9,10},{10,1... | collective-permute-start | bytes 417800 | tf_op jit(solution)/shard_map/ppermute | solution.py:946
  5.9 3.1 %collective-permute-start.26 = (f32[17,16,128]{2,1,0:T(8,128)S(1)}, f32[17,16,128]{2,1,0:T(8,128)S(1)}, u32[]{:S(2)}, u32[]{:S(2)}) collective-permute-start(f32[17,16,128]{2,1,0:T(8,128)S(1)} %get-tuple-element.99), channel_id=1, source_target_pairs={{0,7},{1,0},{2,1},{3,2},{4,3},{5,4},{6,5},{7,6},{8,15},{9,8},{10,9... | collective-permute-start | bytes 417800 | tf_op jit(solution)/shard_map/ppermute | solution.py:946
  9.0 0.0 collective-permute-start.21
  9.0 1.5 %collective-permute-start.22 = (f32[3,16,128]{2,1,0:T(8,128)S(1)}, f32[3,16,128]{2,1,0:T(8,128)S(1)}, u32[]{:S(2)}, u32[]{:S(2)}) collective-permute-start(f32[3,16,128]{2,1,0:T(8,128)S(1)} %get-tuple-element.93), channel_id=1, source_target_pairs={{0,3},{1,4},{2,5},{3,6},{4,7},{5,0},{6,1},{7,2},{8,11},{9,12},{10,... | collective-permute-start | bytes 73736 | tf_op jit(solution)/shard_map/ppermute | solution.py:946
  10.5 2.3 %collective-permute-start.25 = (f32[5,16,128]{2,1,0:T(8,128)S(1)}, f32[5,16,128]{2,1,0:T(8,128)S(1)}, u32[]{:S(2)}, u32[]{:S(2)}) collective-permute-start(f32[5,16,128]{2,1,0:T(8,128)S(1)} %get-tuple-element.98), channel_id=1, source_target_pairs={{0,6},{1,7},{2,0},{3,1},{4,2},{5,3},{6,4},{7,5},{8,14},{9,15},{10,... | collective-permute-start | bytes 122888 | tf_op jit(solution)/shard_map/ppermute | solution.py:946
  12.8 2.9 %collective-permute-done.21.refs_5_ = f32[5,16,128]{2,1,0:T(8,128)S(1)} collective-permute-done((f32[5,16,128]{2,1,0:T(8,128)S(1)}, f32[5,16,128]{2,1,0:T(8,128)S(1)}, u32[]{:S(2)}, u32[]{:S(2)}) %collective-permute-start.21) | collective-permute-done | bytes 40992 | tf_op jit(solution)/shard_map/ppermute | solution.py:946
  15.8 0.0 collective-permute-start.23
  15.8 0.0 collective-permute-done.22.refs_6_
  15.8 1.9 %collective-permute-start.24 = (f32[3,16,128]{2,1,0:T(8,128)S(1)}, f32[3,16,128]{2,1,0:T(8,128)S(1)}, u32[]{:S(2)}, u32[]{:S(2)}) collective-permute-start(f32[3,16,128]{2,1,0:T(8,128)S(1)} %get-tuple-element.97), channel_id=1, source_target_pairs={{0,5},{1,6},{2,7},{3,0},{4,1},{5,2},{6,3},{7,4},{8,13},{9,14},{10,... | collective-permute-start | bytes 73736 | tf_op jit(solution)/shard_map/ppermute | solution.py:946
  17.7 0.0 collective-permute-done.25.refs_9_
  17.7 2.8 %collective-permute-done.24.refs_8_ = f32[3,16,128]{2,1,0:T(8,128)S(1)} collective-permute-done((f32[3,16,128]{2,1,0:T(8,128)S(1)}, f32[3,16,128]{2,1,0:T(8,128)S(1)}, u32[]{:S(2)}, u32[]{:S(2)}) %collective-permute-start.24) | collective-permute-done | bytes 24608 | tf_op jit(solution)/shard_map/ppermute | solution.py:946
  20.5 0.1 collective-permute-done.23.refs_7_
  20.6 0.0 collective-permute-done.20.refs_4_
  20.6 0.0 collective-permute-done.26.refs_10_
  20.6 0.6 %assemble_block.1 = (f32[3,5,32,384]{3,2,1,0:T(8,128)S(1)}, f32[2,4,32,128]{3,2,1,0:T(8,128)S(1)}, f32[19,8,128]{2,1,0:T(8,128)S(1)}, f32[19,8,128]{2,1,0:T(8,128)S(1)}, f32[8,128]{1,0:T(8,128)S(1)}) custom-call(f32[8,128]{1,0:T(8,128)S(1)} %get-tuple-element.87.refs_0_, f32[8,16,256]{2,1,0:T(8,128)S(1)} %get-tuple-element.343.refs_1_, ...), custom_call_target="tpu_custom_call" | custom-call | tf_op jit(solution)/shard_map/assemble_block/pallas_call | solution.py:951
  21.2 0.1 collective-permute-start.27
  21.3 1.6 %collective-permute-start.28 = (f32[19,8,128]{2,1,0:T(8,128)S(1)}, f32[19,8,128]{2,1,0:T(8,128)S(1)}, u32[]{:S(2)}, u32[]{:S(2)}) collective-permute-start(f32[19,8,128]{2,1,0:T(8,128)S(1)} %get-tuple-element.120), channel_id=1, source_target_pairs={{0,24},{8,16},{16,8},{24,0},{1,25},{9,17},{17,9},{25,1},{2,26},{10... | collective-permute-start | bytes 233480 | tf_op jit(solution)/shard_map/ppermute | solution.py:970
  22.9 0.5 %collective-permute-start.29 = (f32[8,128]{1,0:T(8,128)S(1)}, f32[8,128]{1,0:T(8,128)S(1)}, u32[]{:S(2)}, u32[]{:S(2)}) collective-permute-start(f32[8,128]{1,0:T(8,128)S(1)} %get-tuple-element.121.refs_21_), channel_id=1, source_target_pairs={{0,16},{8,24},{16,0},{24,8},{1,17},{9,25},{17,1},{25,9},{2,18},{10... | collective-permute-start | bytes 12296 | tf_op jit(solution)/shard_map/ppermute | solution.py:971
  23.4 1.0 %couple_block.1 = (f32[4,16,384]{2,1,0:T(8,128)S(1)}, f32[4,16,384]{2,1,0:T(8,128)S(1)}, f32[4,16,384]{2,1,0:T(8,128)S(1)}, f32[4,16,384]{2,1,0:T(8,128)S(1)}, f...) custom-call(f32[3,5,32,384]{3,2,1,0:T(8,128)S(1)} %get-tuple-element, ...), custom_call_target="tpu_custom_call" | custom-call | tf_op jit(solution)/shard_map/couple_block/pallas_call | solution.py:974
  24.4 2.1 %collective-permute-done.29.refs_22_ = f32[8,128]{1,0:T(8,128)S(1)} collective-permute-done((f32[8,128]{1,0:T(8,128)S(1)}, f32[8,128]{1,0:T(8,128)S(1)}, u32[]{:S(2)}, u32[]{:S(2)}) %collective-permute-start.29) | collective-permute-done | bytes 4128 | tf_op jit(solution)/shard_map/ppermute | solution.py:971
  26.5 0.0 collective-permute-done.27.refs_19_
  26.5 2.3 %smooth_block.1 = (f32[8,16,256]{2,1,0:T(8,128)}, f32[8,512]{1,0:T(8,128)}, s32[1,1]{1,0:T(1,128)}) custom-call(f32[8,128]{1,0:T(8,128)S(1)} %get-tuple-element.87.refs_0_, f32[3,5,32,384]{3,2,1,0:T(8,128)S(1)} %get-tuple-element.100.refs_0_.refs_1_, f32[4,16,384]{2,1,0:T(8,128)S(1)} %get-tuple-element.102.refs_2_, ...), custom_call_target="tpu_custom_call" | custom-call | tf_op jit(solution)/shard_map/smooth_block/pallas_call | solution.py:984
  28.8 0.8 %while.12 = (f32[8,16,256]{2,1,0:T(8,128)}, f32[8,512]{1,0:T(8,128)}, s32[]{:T(128)}, s32[8]{0:T(128)S(1)}, f32[8,16,256]{2,1,0:T(8,128)S(1)}, /*index=5*/f32[8,...) while((f32[8,16,256]{2,1,0:T(8,128)}, f32[8,512]{1,0:T(8,128)}, s32[]{:T(128)}, ...), condition=%region_7.8_spmd.clone, body=%region_0.7_spmd.sunk.clone | while | flops 21889904 | bytes 78598984 | solution.py:1011
  (1 shorter events, 0.0 us)
Async XLA Ops:
  2.9 17.7 %collective-permute-start.20 = (f32[17,16,128]{2,1,0:T(8,128)S(1)}, f32[17,16,128]{2,1,0:T(8,128)S(1)}, u32[]{:S(2)}, u32[]{:S(2)}) collective-permute-start(f32[17,16,128]{2,1,0:T(8,128)S(1)} %get-tuple-element.91), channel_id=1, source_target_pairs={{0,1},{1,2},{2,3},{3,4},{4,5},{5,6},{6,7},{7,0},{8,9},{9,10},{10,1... | collective-permute-start | bytes 417800 | tf_op jit(solution)/shard_map/ppermute | solution.py:946
  5.9 14.7 %collective-permute-start.26 = (f32[17,16,128]{2,1,0:T(8,128)S(1)}, f32[17,16,128]{2,1,0:T(8,128)S(1)}, u32[]{:S(2)}, u32[]{:S(2)}) collective-permute-start(f32[17,16,128]{2,1,0:T(8,128)S(1)} %get-tuple-element.99), channel_id=1, source_target_pairs={{0,7},{1,0},{2,1},{3,2},{4,3},{5,4},{6,5},{7,6},{8,15},{9,8},{10,9... | collective-permute-start | bytes 417800 | tf_op jit(solution)/shard_map/ppermute | solution.py:946
  9.0 6.8 %collective-permute-start.21 = (f32[5,16,128]{2,1,0:T(8,128)S(1)}, f32[5,16,128]{2,1,0:T(8,128)S(1)}, u32[]{:S(2)}, u32[]{:S(2)}) collective-permute-start(f32[5,16,128]{2,1,0:T(8,128)S(1)} %get-tuple-element.92), channel_id=1, source_target_pairs={{0,2},{1,3},{2,4},{3,5},{4,6},{5,7},{6,0},{7,1},{8,10},{9,11},{10,... | collective-permute-start | bytes 122888 | tf_op jit(solution)/shard_map/ppermute | solution.py:946
  9.0 6.8 %collective-permute-start.22 = (f32[3,16,128]{2,1,0:T(8,128)S(1)}, f32[3,16,128]{2,1,0:T(8,128)S(1)}, u32[]{:S(2)}, u32[]{:S(2)}) collective-permute-start(f32[3,16,128]{2,1,0:T(8,128)S(1)} %get-tuple-element.93), channel_id=1, source_target_pairs={{0,3},{1,4},{2,5},{3,6},{4,7},{5,0},{6,1},{7,2},{8,11},{9,12},{10,... | collective-permute-start | bytes 73736 | tf_op jit(solution)/shard_map/ppermute | solution.py:946
  10.5 7.2 %collective-permute-start.25 = (f32[5,16,128]{2,1,0:T(8,128)S(1)}, f32[5,16,128]{2,1,0:T(8,128)S(1)}, u32[]{:S(2)}, u32[]{:S(2)}) collective-permute-start(f32[5,16,128]{2,1,0:T(8,128)S(1)} %get-tuple-element.98), channel_id=1, source_target_pairs={{0,6},{1,7},{2,0},{3,1},{4,2},{5,3},{6,4},{7,5},{8,14},{9,15},{10,... | collective-permute-start | bytes 122888 | tf_op jit(solution)/shard_map/ppermute | solution.py:946
  15.8 4.8 %collective-permute-start.23 = (f32[4,16,128]{2,1,0:T(8,128)S(1)}, f32[4,16,128]{2,1,0:T(8,128)S(1)}, u32[]{:S(2)}, u32[]{:S(2)}) collective-permute-start(f32[4,16,128]{2,1,0:T(8,128)S(1)} %get-tuple-element.95), channel_id=1, source_target_pairs={{0,4},{1,5},{2,6},{3,7},{4,0},{5,1},{6,2},{7,3},{8,12},{9,13},{10,... | collective-permute-start | bytes 98312 | tf_op jit(solution)/shard_map/ppermute | solution.py:946
  15.8 4.7 %collective-permute-start.24 = (f32[3,16,128]{2,1,0:T(8,128)S(1)}, f32[3,16,128]{2,1,0:T(8,128)S(1)}, u32[]{:S(2)}, u32[]{:S(2)}) collective-permute-start(f32[3,16,128]{2,1,0:T(8,128)S(1)} %get-tuple-element.97), channel_id=1, source_target_pairs={{0,5},{1,6},{2,7},{3,0},{4,1},{5,2},{6,3},{7,4},{8,13},{9,14},{10,... | collective-permute-start | bytes 73736 | tf_op jit(solution)/shard_map/ppermute | solution.py:946
  21.2 5.3 %collective-permute-start.27 = (f32[19,8,128]{2,1,0:T(8,128)S(1)}, f32[19,8,128]{2,1,0:T(8,128)S(1)}, u32[]{:S(2)}, u32[]{:S(2)}) collective-permute-start(f32[19,8,128]{2,1,0:T(8,128)S(1)} %get-tuple-element.119), channel_id=1, source_target_pairs={{0,8},{8,0},{16,24},{24,16},{1,9},{9,1},{17,25},{25,17},{2,10},{10... | collective-permute-start | bytes 233480 | tf_op jit(solution)/shard_map/ppermute | solution.py:969
  21.3 5.2 %collective-permute-start.28 = (f32[19,8,128]{2,1,0:T(8,128)S(1)}, f32[19,8,128]{2,1,0:T(8,128)S(1)}, u32[]{:S(2)}, u32[]{:S(2)}) collective-permute-start(f32[19,8,128]{2,1,0:T(8,128)S(1)} %get-tuple-element.120), channel_id=1, source_target_pairs={{0,24},{8,16},{16,8},{24,0},{1,25},{9,17},{17,9},{25,1},{2,26},{10... | collective-permute-start | bytes 233480 | tf_op jit(solution)/shard_map/ppermute | solution.py:970
  22.9 3.6 %collective-permute-start.29 = (f32[8,128]{1,0:T(8,128)S(1)}, f32[8,128]{1,0:T(8,128)S(1)}, u32[]{:S(2)}, u32[]{:S(2)}) collective-permute-start(f32[8,128]{1,0:T(8,128)S(1)} %get-tuple-element.121.refs_21_), channel_id=1, source_target_pairs={{0,16},{8,24},{16,0},{24,8},{1,17},{9,25},{17,1},{25,9},{2,18},{10... | collective-permute-start | bytes 12296 | tf_op jit(solution)/shard_map/ppermute | solution.py:971

commit v7 on v6

--- a/solution.py
+++ b/solution.py
@@ -209,7 +209,7 @@
 
 
 def plan_units(count, bulk, whole, kept):
-    return (count + count // 2 if bulk is not None else 0) + (3 if whole else 0) + len(kept) + 1
+    return (count + count // 2 if bulk is not None else 0) + (4 if whole else 0) + len(kept) + 1
 
 
 def cell_lanes(side):
@@ -228,41 +228,22 @@
     side = field.shape[0]
     y, black = masks
     if part == HIGH:
-        pairs = jnp.where(black, field, turn(field, side))
+        pairs = turn(jnp.where(black, field, turn(field, -side)), 4 * side)
         out = jnp.where(y >= 4, source, pairs)
-        out = jnp.where(y == 2, turn(beta, -side), out)
-        out = jnp.where(y == 1, turn(pairs, -4 * side), out)
-        return jnp.where(y == 0, turn(pairs, side), out)
-    pairs = jnp.where(black, field, turn(field, -side))
+        out = jnp.where(y == 3, field, out)
+        return out if beta is None else jnp.where(y == 1, turn(beta, -2 * side), out)
+    pairs = turn(jnp.where(black, field, turn(field, side)), 4 * side)
     out = jnp.where(y < 4, source, pairs)
-    out = jnp.where(y == 5, turn(beta, side), out)
-    out = jnp.where(y == 6, turn(pairs, 4 * side), out)
-    return jnp.where(y == 7, turn(pairs, -side), out)
+    out = jnp.where(y == 4, field, out)
+    return out if beta is None else jnp.where(y == 6, turn(beta, 2 * side), out)
 
 
 def unpack_end(part, packed):
     side = packed.shape[0]
     y, _ = cell_lanes(side)
-    out = packed
-    places = ((7, 7), (6, 6), (5, 4), (4, 3)) if part == HIGH else ((0, 1), (1, 2), (2, 4), (3, 5))
-    for layer, shift in places:
-        out = jnp.where(y == layer, turn(packed, shift * side), out)
-    return out
-
-
-def pack_whole(low, high):
-    side = low.shape[0]
-    layer, black = cell_lanes(side)
-    even = (layer & 1) == 0
-    low = jnp.where(black, low, turn(low, -side))
-    high = jnp.where(black, high, turn(high, -side))
-    return jnp.where(even, low, turn(high, side))
-
-
-def unpack_whole(packed):
-    side = packed.shape[0]
-    even = (cell_lanes(side)[0] & 1) == 0
-    return jnp.where(even, packed, turn(packed, side)), jnp.where(even, turn(packed, -side), packed)
+    if part == HIGH:
+        return jnp.where((y & 1) == 0, turn(packed, 4 * side), turn(packed, 5 * side))
+    return jnp.where((y & 1) == 1, turn(packed, 4 * side), turn(packed, -5 * side))
 
 
 def part_lanes(part, plane):
@@ -356,14 +337,14 @@
         low, high = part_lanes(LOW, plane), part_lanes(HIGH, plane)
         if whole:
             box = old_index[moves.index(offset)]
-            out[unit] = pack_whole(field[box, :, low], field[box, :, high])
-            out[unit + 1] = source[box, :, low]
-            out[unit + 2] = source[box, :, high]
-            unit += 3
+            for k, array in enumerate((field, source)):
+                out[unit + 2 * k] = array[box, :, low]
+                out[unit + 2 * k + 1] = array[box, :, high]
+            unit += 4
         for move, part in kept:
             box = old_index[moves.index(move)]
             cut = part_lanes(part, plane)
-            out[unit] = pack_end(part, field[box, :, cut], source[box, :, cut], field[box, :, cut], masks)
+            out[unit] = pack_end(part, field[box, :, cut], source[box, :, cut], None, masks)
             unit += 1
     for out in outs:
         out[out.shape[0] - 1, 0:8] = table[...]
@@ -447,16 +428,14 @@
                 joint = message[count + i // 2]
                 spot = place_of(offset, i)
                 put(ref, 2, spot, joint if i % 2 == 0 else turn(joint, 64))
-                put(ref, 4, spot, turn(packed, 2 * shift))
+                put(ref, 4, spot, turn(packed, 3 * shift))
             unit = count + count // 2
         if entire:
             spot = spot_at(0, moved(offset, moves.index(offset)))
-            first, second = unpack_whole(message[unit])
-            put(block, 0, spot, first, low)
-            put(block, 0, spot, second, high)
-            put(block, 1, spot, message[unit + 1], low)
-            put(block, 1, spot, message[unit + 2], high)
-            unit += 3
+            for k in range(2):
+                put(block, k, spot, message[unit + 2 * k], low)
+                put(block, k, spot, message[unit + 2 * k + 1], high)
+            unit += 4
         for move, part in kept:
             packed = message[unit]
             put_end(part, moved(offset, moves.index(move)), unpack_end(part, packed), packed, packed)

time: 29.9 us -> 29.6 us (0.990)
  Pallas kernels: 6.12 us -> 5.22 us
  waiting for transfers between devices: 7.98 us -> 8.64 us
    pallas_call x1, Pallas kernels: 2.27 us -> 1.48 us  [fast_body(): pl.pallas_call(lambda *refs: pack_kernel(moves, plan, lanes, count, *refs...]
    ppermute x7, waiting for transfers between devices: 5.84 us -> 6.51 us  [fast_body(): lax.ppermute(message, 'lane', [(i, (i + offset) % lanes) for i in range(l...]
where the time goes in v7:
time: 29.6 us; the launch traced here: 29.5 us
  starting transfers between devices  14 us (47%)
  waiting for transfers between devices  8.64 us (29%)
  Pallas kernels  5.22 us (18%)
  between operations  0.84 us (3%)
  loops' own time  0.76 us (3%)
    ppermute x7, starting transfers between devices, fast_body(): lax.ppermute(message, 'lane', [(i, (i + offset) % lanes) for i in range(l...  11.8 us
    ppermute x7, waiting for transfers between devices, fast_body(): lax.ppermute(message, 'lane', [(i, (i + offset) % lanes) for i in range(l...  6.51 us
    pallas_call x1, Pallas kernels, fast_body(): pl.pallas_call(lambda *refs: smooth_kernel(lanes, nodes, covered, *refs),...  2.29 us
    ppermute x1, waiting for transfers between devices, fast_body(): lax.ppermute(row_table, 'node', [(i, (i + 2) % nodes) for i in range(node...  2.13 us
    ppermute x1, starting transfers between devices, fast_body(): lax.ppermute(to_other, 'node', [(i, (i - 1 + 2 * (i % 2)) % nodes) for i...  1.63 us
    pallas_call x1, Pallas kernels, fast_body(): pl.pallas_call(lambda *refs: pack_kernel(moves, plan, lanes, count, *refs...  1.48 us
    pallas_call x1, Pallas kernels, fast_body(): pl.pallas_call(lambda *refs: couple_kernel(lanes, nodes, plane, *refs), n...  0.96 us
    another operation x1, loops' own time, fast_body(): lax.while_loop(lambda carry: carry[2] > 0, again, (smoothed, coarse, irre...  0.76 us
  transfers between devices with their start and end apart: 10, of which 4 were waited for; matrix products, arithmetic and copies ran while one was open for 0% of the time, Pallas kernels for 3%

profile of v7, /device:TPU:0, one launch (start us, length us, event | category | flops | bytes accessed | tf_op | source)
XLA Modules:
  0.0 29.5 jit_solution(16220503526369502880)
XLA Ops:
  0.6 1.5 %pack_moves.1 = (f32[18,16,128]{2,1,0:T(8,128)S(1)}, f32[6,16,128]{2,1,0:T(8,128)S(1)}, f32[3,16,128]{2,1,0:T(8,128)S(1)}, f32[5,16,128]{2,1,0:T(8,128)S(1)}, f3...) custom-call(f32[8,16,256]{2,1,0:T(8,128)} %refs_0_.1, ...), custom_call_target="tpu_custom_call" | custom-call | tf_op jit(solution)/shard_map/pack_moves/pallas_call | solution.py:900
  2.1 3.0 %collective-permute-start.20 = (f32[18,16,128]{2,1,0:T(8,128)S(1)}, f32[18,16,128]{2,1,0:T(8,128)S(1)}, u32[]{:S(2)}, u32[]{:S(2)}) collective-permute-start(f32[18,16,128]{2,1,0:T(8,128)S(1)} %get-tuple-element.91), channel_id=1, source_target_pairs={{0,1},{1,2},{2,3},{3,4},{4,5},{5,6},{6,7},{7,0},{8,9},{9,10},{10,1... | collective-permute-start | bytes 442376 | tf_op jit(solution)/shard_map/ppermute | solution.py:925
  5.1 3.1 %collective-permute-start.26 = (f32[18,16,128]{2,1,0:T(8,128)S(1)}, f32[18,16,128]{2,1,0:T(8,128)S(1)}, u32[]{:S(2)}, u32[]{:S(2)}) collective-permute-start(f32[18,16,128]{2,1,0:T(8,128)S(1)} %get-tuple-element.99), channel_id=1, source_target_pairs={{0,7},{1,0},{2,1},{3,2},{4,3},{5,4},{6,5},{7,6},{8,15},{9,8},{10,9... | collective-permute-start | bytes 442376 | tf_op jit(solution)/shard_map/ppermute | solution.py:925
  8.2 0.0 collective-permute-start.21
  8.2 1.5 %collective-permute-start.22 = (f32[3,16,128]{2,1,0:T(8,128)S(1)}, f32[3,16,128]{2,1,0:T(8,128)S(1)}, u32[]{:S(2)}, u32[]{:S(2)}) collective-permute-start(f32[3,16,128]{2,1,0:T(8,128)S(1)} %get-tuple-element.93), channel_id=1, source_target_pairs={{0,3},{1,4},{2,5},{3,6},{4,7},{5,0},{6,1},{7,2},{8,11},{9,12},{10,... | collective-permute-start | bytes 73736 | tf_op jit(solution)/shard_map/ppermute | solution.py:925
  9.7 2.3 %collective-permute-start.25 = (f32[6,16,128]{2,1,0:T(8,128)S(1)}, f32[6,16,128]{2,1,0:T(8,128)S(1)}, u32[]{:S(2)}, u32[]{:S(2)}) collective-permute-start(f32[6,16,128]{2,1,0:T(8,128)S(1)} %get-tuple-element.98), channel_id=1, source_target_pairs={{0,6},{1,7},{2,0},{3,1},{4,2},{5,3},{6,4},{7,5},{8,14},{9,15},{10,... | collective-permute-start | bytes 147464 | tf_op jit(solution)/shard_map/ppermute | solution.py:925
  12.0 3.3 %collective-permute-done.21.refs_5_ = f32[6,16,128]{2,1,0:T(8,128)S(1)} collective-permute-done((f32[6,16,128]{2,1,0:T(8,128)S(1)}, f32[6,16,128]{2,1,0:T(8,128)S(1)}, u32[]{:S(2)}, u32[]{:S(2)}) %collective-permute-start.21) | collective-permute-done | bytes 49184 | tf_op jit(solution)/shard_map/ppermute | solution.py:925
  15.4 0.0 collective-permute-start.23
  15.4 0.0 collective-permute-done.22.refs_6_
  15.4 1.9 %collective-permute-start.24 = (f32[3,16,128]{2,1,0:T(8,128)S(1)}, f32[3,16,128]{2,1,0:T(8,128)S(1)}, u32[]{:S(2)}, u32[]{:S(2)}) collective-permute-start(f32[3,16,128]{2,1,0:T(8,128)S(1)} %get-tuple-element.97), channel_id=1, source_target_pairs={{0,5},{1,6},{2,7},{3,0},{4,1},{5,2},{6,3},{7,4},{8,13},{9,14},{10,... | collective-permute-start | bytes 73736 | tf_op jit(solution)/shard_map/ppermute | solution.py:925
  17.2 0.0 collective-permute-done.25.refs_9_
  17.2 2.9 %collective-permute-done.24.refs_8_ = f32[3,16,128]{2,1,0:T(8,128)S(1)} collective-permute-done((f32[3,16,128]{2,1,0:T(8,128)S(1)}, f32[3,16,128]{2,1,0:T(8,128)S(1)}, u32[]{:S(2)}, u32[]{:S(2)}) %collective-permute-start.24) | collective-permute-done | bytes 24608 | tf_op jit(solution)/shard_map/ppermute | solution.py:925
  20.1 0.3 %collective-permute-done.23.refs_7_ = f32[5,16,128]{2,1,0:T(8,128)S(1)} collective-permute-done((f32[5,16,128]{2,1,0:T(8,128)S(1)}, f32[5,16,128]{2,1,0:T(8,128)S(1)}, u32[]{:S(2)}, u32[]{:S(2)}) %collective-permute-start.23) | collective-permute-done | bytes 40992 | tf_op jit(solution)/shard_map/ppermute | solution.py:925
  20.4 0.0 collective-permute-done.20.refs_4_
  20.4 0.0 collective-permute-done.26.refs_10_
  20.4 0.5 %assemble_block.1 = (f32[3,5,32,384]{3,2,1,0:T(8,128)S(1)}, f32[2,4,32,128]{3,2,1,0:T(8,128)S(1)}, f32[19,8,128]{2,1,0:T(8,128)S(1)}, f32[19,8,128]{2,1,0:T(8,128)S(1)}, f32[8,128]{1,0:T(8,128)S(1)}) custom-call(f32[8,128]{1,0:T(8,128)S(1)} %get-tuple-element.87.refs_0_, f32[8,16,256]{2,1,0:T(8,128)S(1)} %get-tuple-element.343.refs_1_, ...), custom_call_target="tpu_custom_call" | custom-call | tf_op jit(solution)/shard_map/assemble_block/pallas_call | solution.py:930
  20.9 0.1 collective-permute-start.27
  21.0 1.6 %collective-permute-start.28 = (f32[19,8,128]{2,1,0:T(8,128)S(1)}, f32[19,8,128]{2,1,0:T(8,128)S(1)}, u32[]{:S(2)}, u32[]{:S(2)}) collective-permute-start(f32[19,8,128]{2,1,0:T(8,128)S(1)} %get-tuple-element.120), channel_id=1, source_target_pairs={{0,24},{8,16},{16,8},{24,0},{1,25},{9,17},{17,9},{25,1},{2,26},{10... | collective-permute-start | bytes 233480 | tf_op jit(solution)/shard_map/ppermute | solution.py:949
  22.6 0.5 %collective-permute-start.29 = (f32[8,128]{1,0:T(8,128)S(1)}, f32[8,128]{1,0:T(8,128)S(1)}, u32[]{:S(2)}, u32[]{:S(2)}) collective-permute-start(f32[8,128]{1,0:T(8,128)S(1)} %get-tuple-element.121.refs_21_), channel_id=1, source_target_pairs={{0,16},{8,24},{16,0},{24,8},{1,17},{9,25},{17,1},{25,9},{2,18},{10... | collective-permute-start | bytes 12296 | tf_op jit(solution)/shard_map/ppermute | solution.py:950
  23.1 1.0 %couple_block.1 = (f32[4,16,384]{2,1,0:T(8,128)S(1)}, f32[4,16,384]{2,1,0:T(8,128)S(1)}, f32[4,16,384]{2,1,0:T(8,128)S(1)}, f32[4,16,384]{2,1,0:T(8,128)S(1)}, f...) custom-call(f32[3,5,32,384]{3,2,1,0:T(8,128)S(1)} %get-tuple-element, ...), custom_call_target="tpu_custom_call" | custom-call | tf_op jit(solution)/shard_map/couple_block/pallas_call | solution.py:953
  24.1 2.1 %collective-permute-done.29.refs_22_ = f32[8,128]{1,0:T(8,128)S(1)} collective-permute-done((f32[8,128]{1,0:T(8,128)S(1)}, f32[8,128]{1,0:T(8,128)S(1)}, u32[]{:S(2)}, u32[]{:S(2)}) %collective-permute-start.29) | collective-permute-done | bytes 4128 | tf_op jit(solution)/shard_map/ppermute | solution.py:950
  26.2 0.0 collective-permute-done.27.refs_19_
  26.3 2.3 %smooth_block.1 = (f32[8,16,256]{2,1,0:T(8,128)}, f32[8,512]{1,0:T(8,128)}, s32[1,1]{1,0:T(1,128)}) custom-call(f32[8,128]{1,0:T(8,128)S(1)} %get-tuple-element.87.refs_0_, f32[3,5,32,384]{3,2,1,0:T(8,128)S(1)} %get-tuple-element.100.refs_0_.refs_1_, f32[4,16,384]{2,1,0:T(8,128)S(1)} %get-tuple-element.102.refs_2_, ...), custom_call_target="tpu_custom_call" | custom-call | tf_op jit(solution)/shard_map/smooth_block/pallas_call | solution.py:963
  28.6 0.8 %while.12 = (f32[8,16,256]{2,1,0:T(8,128)}, f32[8,512]{1,0:T(8,128)}, s32[]{:T(128)}, s32[8]{0:T(128)S(1)}, f32[8,16,256]{2,1,0:T(8,128)S(1)}, /*index=5*/f32[8,...) while((f32[8,16,256]{2,1,0:T(8,128)}, f32[8,512]{1,0:T(8,128)}, s32[]{:T(128)}, ...), condition=%region_7.8_spmd.clone, body=%region_0.7_spmd.sunk.clone | while | flops 21889904 | bytes 78660424 | solution.py:990
  (1 shorter events, 0.0 us)
Async XLA Ops:
  2.1 18.3 %collective-permute-start.20 = (f32[18,16,128]{2,1,0:T(8,128)S(1)}, f32[18,16,128]{2,1,0:T(8,128)S(1)}, u32[]{:S(2)}, u32[]{:S(2)}) collective-permute-start(f32[18,16,128]{2,1,0:T(8,128)S(1)} %get-tuple-element.91), channel_id=1, source_target_pairs={{0,1},{1,2},{2,3},{3,4},{4,5},{5,6},{6,7},{7,0},{8,9},{9,10},{10,1... | collective-permute-start | bytes 442376 | tf_op jit(solution)/shard_map/ppermute | solution.py:925
  5.1 15.3 %collective-permute-start.26 = (f32[18,16,128]{2,1,0:T(8,128)S(1)}, f32[18,16,128]{2,1,0:T(8,128)S(1)}, u32[]{:S(2)}, u32[]{:S(2)}) collective-permute-start(f32[18,16,128]{2,1,0:T(8,128)S(1)} %get-tuple-element.99), channel_id=1, source_target_pairs={{0,7},{1,0},{2,1},{3,2},{4,3},{5,4},{6,5},{7,6},{8,15},{9,8},{10,9... | collective-permute-start | bytes 442376 | tf_op jit(solution)/shard_map/ppermute | solution.py:925
  8.2 7.1 %collective-permute-start.21 = (f32[6,16,128]{2,1,0:T(8,128)S(1)}, f32[6,16,128]{2,1,0:T(8,128)S(1)}, u32[]{:S(2)}, u32[]{:S(2)}) collective-permute-start(f32[6,16,128]{2,1,0:T(8,128)S(1)} %get-tuple-element.92), channel_id=1, source_target_pairs={{0,2},{1,3},{2,4},{3,5},{4,6},{5,7},{6,0},{7,1},{8,10},{9,11},{10,... | collective-permute-start | bytes 147464 | tf_op jit(solution)/shard_map/ppermute | solution.py:925
  8.2 7.1 %collective-permute-start.22 = (f32[3,16,128]{2,1,0:T(8,128)S(1)}, f32[3,16,128]{2,1,0:T(8,128)S(1)}, u32[]{:S(2)}, u32[]{:S(2)}) collective-permute-start(f32[3,16,128]{2,1,0:T(8,128)S(1)} %get-tuple-element.93), channel_id=1, source_target_pairs={{0,3},{1,4},{2,5},{3,6},{4,7},{5,0},{6,1},{7,2},{8,11},{9,12},{10,... | collective-permute-start | bytes 73736 | tf_op jit(solution)/shard_map/ppermute | solution.py:925
  9.7 7.5 %collective-permute-start.25 = (f32[6,16,128]{2,1,0:T(8,128)S(1)}, f32[6,16,128]{2,1,0:T(8,128)S(1)}, u32[]{:S(2)}, u32[]{:S(2)}) collective-permute-start(f32[6,16,128]{2,1,0:T(8,128)S(1)} %get-tuple-element.98), channel_id=1, source_target_pairs={{0,6},{1,7},{2,0},{3,1},{4,2},{5,3},{6,4},{7,5},{8,14},{9,15},{10,... | collective-permute-start | bytes 147464 | tf_op jit(solution)/shard_map/ppermute | solution.py:925
  15.4 5.1 %collective-permute-start.23 = (f32[5,16,128]{2,1,0:T(8,128)S(1)}, f32[5,16,128]{2,1,0:T(8,128)S(1)}, u32[]{:S(2)}, u32[]{:S(2)}) collective-permute-start(f32[5,16,128]{2,1,0:T(8,128)S(1)} %get-tuple-element.95), channel_id=1, source_target_pairs={{0,4},{1,5},{2,6},{3,7},{4,0},{5,1},{6,2},{7,3},{8,12},{9,13},{10,... | collective-permute-start | bytes 122888 | tf_op jit(solution)/shard_map/ppermute | solution.py:925
  15.4 4.7 %collective-permute-start.24 = (f32[3,16,128]{2,1,0:T(8,128)S(1)}, f32[3,16,128]{2,1,0:T(8,128)S(1)}, u32[]{:S(2)}, u32[]{:S(2)}) collective-permute-start(f32[3,16,128]{2,1,0:T(8,128)S(1)} %get-tuple-element.97), channel_id=1, source_target_pairs={{0,5},{1,6},{2,7},{3,0},{4,1},{5,2},{6,3},{7,4},{8,13},{9,14},{10,... | collective-permute-start | bytes 73736 | tf_op jit(solution)/shard_map/ppermute | solution.py:925
  20.9 5.3 %collective-permute-start.27 = (f32[19,8,128]{2,1,0:T(8,128)S(1)}, f32[19,8,128]{2,1,0:T(8,128)S(1)}, u32[]{:S(2)}, u32[]{:S(2)}) collective-permute-start(f32[19,8,128]{2,1,0:T(8,128)S(1)} %get-tuple-element.119), channel_id=1, source_target_pairs={{0,8},{8,0},{16,24},{24,16},{1,9},{9,1},{17,25},{25,17},{2,10},{10... | collective-permute-start | bytes 233480 | tf_op jit(solution)/shard_map/ppermute | solution.py:948
  21.0 5.2 %collective-permute-start.28 = (f32[19,8,128]{2,1,0:T(8,128)S(1)}, f32[19,8,128]{2,1,0:T(8,128)S(1)}, u32[]{:S(2)}, u32[]{:S(2)}) collective-permute-start(f32[19,8,128]{2,1,0:T(8,128)S(1)} %get-tuple-element.120), channel_id=1, source_target_pairs={{0,24},{8,16},{16,8},{24,0},{1,25},{9,17},{17,9},{25,1},{2,26},{10... | collective-permute-start | bytes 233480 | tf_op jit(solution)/shard_map/ppermute | solution.py:949
  22.6 3.6 %collective-permute-start.29 = (f32[8,128]{1,0:T(8,128)S(1)}, f32[8,128]{1,0:T(8,128)S(1)}, u32[]{:S(2)}, u32[]{:S(2)}) collective-permute-start(f32[8,128]{1,0:T(8,128)S(1)} %get-tuple-element.121.refs_21_), channel_id=1, source_target_pairs={{0,16},{8,24},{16,0},{24,8},{1,17},{9,25},{17,1},{25,9},{2,18},{10... | collective-permute-start | bytes 12296 | tf_op jit(solution)/shard_map/ppermute | solution.py:950

commit v8 on v7

--- a/solution.py
+++ b/solution.py
@@ -479,23 +479,22 @@
 def pack_rows(up, field, beta):
     rows, colour = row_colours(field.shape[1], SIDE)
     if up:
-        pairs = jnp.where(colour == 1, field, fall(field, 1))
-        out = jnp.where(rows == 0, fall(pairs, 1), beta)
-        out = jnp.where(rows == 1, fall(pairs, 4), out)
-        return jnp.where(rows == 2, fall(pairs, 7), out)
-    pairs = jnp.where(colour == 1, field, fall(field, 7))
-    out = jnp.where(rows == 7, fall(pairs, 7), beta)
-    out = jnp.where(rows == 6, fall(pairs, 4), out)
-    return jnp.where(rows == 5, fall(pairs, 1), out)
+        pairs = fall(jnp.where(colour == 1, field, fall(field, 7)), 4)
+        out = jnp.where(rows < 3, pairs, beta)
+        return jnp.where(rows == 1, fall(field, 6), out)
+    pairs = fall(jnp.where(colour == 1, field, fall(field, 1)), 4)
+    out = jnp.where(rows > 4, pairs, beta)
+    return jnp.where(rows == 6, fall(field, 2), out)
 
 
 def unpack_rows(below, above):
     rows = lax.broadcasted_iota(jnp.int32, below.shape, 0)
-    field = fall(above, 1)
-    for row, tile, shift in ((1, above, 2), (2, above, 4), (3, above, 5), (4, below, 3), (5, below, 4), (6, below, 6), (7, below, 7)):
-        field = jnp.where(rows == row, fall(tile, shift), field)
+    odd = (rows & 1) == 1
+    first = jnp.where(odd, fall(above, 4), fall(above, 3))
+    second = jnp.where(odd, fall(below, 5), fall(below, 4))
+    field = jnp.where(rows < 4, first, second)
     beta = jnp.where(rows < 4, above, below)
-    fifth_field = jnp.where(rows < 4, fall(above, 6), fall(below, 2))
+    fifth_field = jnp.where(rows < 4, fall(above, 5), fall(below, 3))
     fifth_beta = jnp.where(rows < 4, fall(above, 7), fall(below, 1))
     return field, beta, fifth_field, fifth_beta
 

time: 29.6 us -> 29.6 us (level)
  no operation moved by 1% of the time
where the time goes in v8:
time: 29.6 us; the launch traced here: 29.5 us
  starting transfers between devices  14 us (47%)
  waiting for transfers between devices  8.64 us (29%)
  Pallas kernels  5.21 us (18%)
  between operations  0.84 us (3%)
  loops' own time  0.76 us (3%)
    ppermute x7, starting transfers between devices, fast_body(): lax.ppermute(message, 'lane', [(i, (i + offset) % lanes) for i in range(l...  11.8 us
    ppermute x7, waiting for transfers between devices, fast_body(): lax.ppermute(message, 'lane', [(i, (i + offset) % lanes) for i in range(l...  6.51 us
    pallas_call x1, Pallas kernels, fast_body(): pl.pallas_call(lambda *refs: smooth_kernel(lanes, nodes, covered, *refs),...  2.28 us
    ppermute x1, waiting for transfers between devices, fast_body(): lax.ppermute(row_table, 'node', [(i, (i + 2) % nodes) for i in range(node...  2.13 us
    ppermute x1, starting transfers between devices, fast_body(): lax.ppermute(to_other, 'node', [(i, (i - 1 + 2 * (i % 2)) % nodes) for i...  1.64 us
    pallas_call x1, Pallas kernels, fast_body(): pl.pallas_call(lambda *refs: pack_kernel(moves, plan, lanes, count, *refs...  1.48 us
    pallas_call x1, Pallas kernels, fast_body(): pl.pallas_call(lambda *refs: couple_kernel(lanes, nodes, plane, *refs), n...  0.96 us
    another operation x1, loops' own time, fast_body(): lax.while_loop(lambda carry: carry[2] > 0, again, (smoothed, coarse, irre...  0.76 us
  transfers between devices with their start and end apart: 10, of which 4 were waited for; matrix products, arithmetic and copies ran while one was open for 0% of the time, Pallas kernels for 3%

profile of v8, /device:TPU:0, one launch (start us, length us, event | category | flops | bytes accessed | tf_op | source)
XLA Modules:
  0.0 29.5 jit_solution(1320249527493590231)
XLA Ops:
  0.6 1.5 %pack_moves.1 = (f32[18,16,128]{2,1,0:T(8,128)S(1)}, f32[6,16,128]{2,1,0:T(8,128)S(1)}, f32[3,16,128]{2,1,0:T(8,128)S(1)}, f32[5,16,128]{2,1,0:T(8,128)S(1)}, f3...) custom-call(f32[8,16,256]{2,1,0:T(8,128)} %refs_0_.1, ...), custom_call_target="tpu_custom_call" | custom-call | tf_op jit(solution)/shard_map/pack_moves/pallas_call | solution.py:899
  2.1 3.0 %collective-permute-start.20 = (f32[18,16,128]{2,1,0:T(8,128)S(1)}, f32[18,16,128]{2,1,0:T(8,128)S(1)}, u32[]{:S(2)}, u32[]{:S(2)}) collective-permute-start(f32[18,16,128]{2,1,0:T(8,128)S(1)} %get-tuple-element.91), channel_id=1, source_target_pairs={{0,1},{1,2},{2,3},{3,4},{4,5},{5,6},{6,7},{7,0},{8,9},{9,10},{10,1... | collective-permute-start | bytes 442376 | tf_op jit(solution)/shard_map/ppermute | solution.py:924
  5.1 3.1 %collective-permute-start.26 = (f32[18,16,128]{2,1,0:T(8,128)S(1)}, f32[18,16,128]{2,1,0:T(8,128)S(1)}, u32[]{:S(2)}, u32[]{:S(2)}) collective-permute-start(f32[18,16,128]{2,1,0:T(8,128)S(1)} %get-tuple-element.99), channel_id=1, source_target_pairs={{0,7},{1,0},{2,1},{3,2},{4,3},{5,4},{6,5},{7,6},{8,15},{9,8},{10,9... | collective-permute-start | bytes 442376 | tf_op jit(solution)/shard_map/ppermute | solution.py:924
  8.2 0.0 collective-permute-start.21
  8.2 1.5 %collective-permute-start.22 = (f32[3,16,128]{2,1,0:T(8,128)S(1)}, f32[3,16,128]{2,1,0:T(8,128)S(1)}, u32[]{:S(2)}, u32[]{:S(2)}) collective-permute-start(f32[3,16,128]{2,1,0:T(8,128)S(1)} %get-tuple-element.93), channel_id=1, source_target_pairs={{0,3},{1,4},{2,5},{3,6},{4,7},{5,0},{6,1},{7,2},{8,11},{9,12},{10,... | collective-permute-start | bytes 73736 | tf_op jit(solution)/shard_map/ppermute | solution.py:924
  9.7 2.3 %collective-permute-start.25 = (f32[6,16,128]{2,1,0:T(8,128)S(1)}, f32[6,16,128]{2,1,0:T(8,128)S(1)}, u32[]{:S(2)}, u32[]{:S(2)}) collective-permute-start(f32[6,16,128]{2,1,0:T(8,128)S(1)} %get-tuple-element.98), channel_id=1, source_target_pairs={{0,6},{1,7},{2,0},{3,1},{4,2},{5,3},{6,4},{7,5},{8,14},{9,15},{10,... | collective-permute-start | bytes 147464 | tf_op jit(solution)/shard_map/ppermute | solution.py:924
  12.0 3.3 %collective-permute-done.21.refs_5_ = f32[6,16,128]{2,1,0:T(8,128)S(1)} collective-permute-done((f32[6,16,128]{2,1,0:T(8,128)S(1)}, f32[6,16,128]{2,1,0:T(8,128)S(1)}, u32[]{:S(2)}, u32[]{:S(2)}) %collective-permute-start.21) | collective-permute-done | bytes 49184 | tf_op jit(solution)/shard_map/ppermute | solution.py:924
  15.4 0.0 collective-permute-start.23
  15.4 0.0 collective-permute-done.22.refs_6_
  15.4 1.9 %collective-permute-start.24 = (f32[3,16,128]{2,1,0:T(8,128)S(1)}, f32[3,16,128]{2,1,0:T(8,128)S(1)}, u32[]{:S(2)}, u32[]{:S(2)}) collective-permute-start(f32[3,16,128]{2,1,0:T(8,128)S(1)} %get-tuple-element.97), channel_id=1, source_target_pairs={{0,5},{1,6},{2,7},{3,0},{4,1},{5,2},{6,3},{7,4},{8,13},{9,14},{10,... | collective-permute-start | bytes 73736 | tf_op jit(solution)/shard_map/ppermute | solution.py:924
  17.2 0.0 collective-permute-done.25.refs_9_
  17.2 2.9 %collective-permute-done.24.refs_8_ = f32[3,16,128]{2,1,0:T(8,128)S(1)} collective-permute-done((f32[3,16,128]{2,1,0:T(8,128)S(1)}, f32[3,16,128]{2,1,0:T(8,128)S(1)}, u32[]{:S(2)}, u32[]{:S(2)}) %collective-permute-start.24) | collective-permute-done | bytes 24608 | tf_op jit(solution)/shard_map/ppermute | solution.py:924
  20.1 0.3 %collective-permute-done.23.refs_7_ = f32[5,16,128]{2,1,0:T(8,128)S(1)} collective-permute-done((f32[5,16,128]{2,1,0:T(8,128)S(1)}, f32[5,16,128]{2,1,0:T(8,128)S(1)}, u32[]{:S(2)}, u32[]{:S(2)}) %collective-permute-start.23) | collective-permute-done | bytes 40992 | tf_op jit(solution)/shard_map/ppermute | solution.py:924
  20.4 0.0 collective-permute-done.20.refs_4_
  20.4 0.0 collective-permute-done.26.refs_10_
  20.4 0.5 %assemble_block.1 = (f32[3,5,32,384]{3,2,1,0:T(8,128)S(1)}, f32[2,4,32,128]{3,2,1,0:T(8,128)S(1)}, f32[19,8,128]{2,1,0:T(8,128)S(1)}, f32[19,8,128]{2,1,0:T(8,128)S(1)}, f32[8,128]{1,0:T(8,128)S(1)}) custom-call(f32[8,128]{1,0:T(8,128)S(1)} %get-tuple-element.87.refs_0_, f32[8,16,256]{2,1,0:T(8,128)S(1)} %get-tuple-element.343.refs_1_, ...), custom_call_target="tpu_custom_call" | custom-call | tf_op jit(solution)/shard_map/assemble_block/pallas_call | solution.py:929
  20.9 0.1 collective-permute-start.27
  21.0 1.6 %collective-permute-start.28 = (f32[19,8,128]{2,1,0:T(8,128)S(1)}, f32[19,8,128]{2,1,0:T(8,128)S(1)}, u32[]{:S(2)}, u32[]{:S(2)}) collective-permute-start(f32[19,8,128]{2,1,0:T(8,128)S(1)} %get-tuple-element.120), channel_id=1, source_target_pairs={{0,24},{8,16},{16,8},{24,0},{1,25},{9,17},{17,9},{25,1},{2,26},{10... | collective-permute-start | bytes 233480 | tf_op jit(solution)/shard_map/ppermute | solution.py:948
  22.6 0.5 %collective-permute-start.29 = (f32[8,128]{1,0:T(8,128)S(1)}, f32[8,128]{1,0:T(8,128)S(1)}, u32[]{:S(2)}, u32[]{:S(2)}) collective-permute-start(f32[8,128]{1,0:T(8,128)S(1)} %get-tuple-element.121.refs_21_), channel_id=1, source_target_pairs={{0,16},{8,24},{16,0},{24,8},{1,17},{9,25},{17,1},{25,9},{2,18},{10... | collective-permute-start | bytes 12296 | tf_op jit(solution)/shard_map/ppermute | solution.py:949
  23.1 1.0 %couple_block.1 = (f32[4,16,384]{2,1,0:T(8,128)S(1)}, f32[4,16,384]{2,1,0:T(8,128)S(1)}, f32[4,16,384]{2,1,0:T(8,128)S(1)}, f32[4,16,384]{2,1,0:T(8,128)S(1)}, f...) custom-call(f32[3,5,32,384]{3,2,1,0:T(8,128)S(1)} %get-tuple-element, ...), custom_call_target="tpu_custom_call" | custom-call | tf_op jit(solution)/shard_map/couple_block/pallas_call | solution.py:952
  24.1 2.1 %collective-permute-done.29.refs_22_ = f32[8,128]{1,0:T(8,128)S(1)} collective-permute-done((f32[8,128]{1,0:T(8,128)S(1)}, f32[8,128]{1,0:T(8,128)S(1)}, u32[]{:S(2)}, u32[]{:S(2)}) %collective-permute-start.29) | collective-permute-done | bytes 4128 | tf_op jit(solution)/shard_map/ppermute | solution.py:949
  26.2 0.0 collective-permute-done.27.refs_19_
  26.2 2.3 %smooth_block.1 = (f32[8,16,256]{2,1,0:T(8,128)}, f32[8,512]{1,0:T(8,128)}, s32[1,1]{1,0:T(1,128)}) custom-call(f32[8,128]{1,0:T(8,128)S(1)} %get-tuple-element.87.refs_0_, f32[3,5,32,384]{3,2,1,0:T(8,128)S(1)} %get-tuple-element.100.refs_0_.refs_1_, f32[4,16,384]{2,1,0:T(8,128)S(1)} %get-tuple-element.102.refs_2_, ...), custom_call_target="tpu_custom_call" | custom-call | tf_op jit(solution)/shard_map/smooth_block/pallas_call | solution.py:962
  28.5 0.8 %while.12 = (f32[8,16,256]{2,1,0:T(8,128)}, f32[8,512]{1,0:T(8,128)}, s32[]{:T(128)}, s32[8]{0:T(128)S(1)}, f32[8,16,256]{2,1,0:T(8,128)S(1)}, /*index=5*/f32[8,...) while((f32[8,16,256]{2,1,0:T(8,128)}, f32[8,512]{1,0:T(8,128)}, s32[]{:T(128)}, ...), condition=%region_7.8_spmd.clone, body=%region_0.7_spmd.sunk.clone | while | flops 21889904 | bytes 78660424 | solution.py:989
  (1 shorter events, 0.0 us)
Async XLA Ops:
  2.1 18.3 %collective-permute-start.20 = (f32[18,16,128]{2,1,0:T(8,128)S(1)}, f32[18,16,128]{2,1,0:T(8,128)S(1)}, u32[]{:S(2)}, u32[]{:S(2)}) collective-permute-start(f32[18,16,128]{2,1,0:T(8,128)S(1)} %get-tuple-element.91), channel_id=1, source_target_pairs={{0,1},{1,2},{2,3},{3,4},{4,5},{5,6},{6,7},{7,0},{8,9},{9,10},{10,1... | collective-permute-start | bytes 442376 | tf_op jit(solution)/shard_map/ppermute | solution.py:924
  5.1 15.3 %collective-permute-start.26 = (f32[18,16,128]{2,1,0:T(8,128)S(1)}, f32[18,16,128]{2,1,0:T(8,128)S(1)}, u32[]{:S(2)}, u32[]{:S(2)}) collective-permute-start(f32[18,16,128]{2,1,0:T(8,128)S(1)} %get-tuple-element.99), channel_id=1, source_target_pairs={{0,7},{1,0},{2,1},{3,2},{4,3},{5,4},{6,5},{7,6},{8,15},{9,8},{10,9... | collective-permute-start | bytes 442376 | tf_op jit(solution)/shard_map/ppermute | solution.py:924
  8.2 7.1 %collective-permute-start.21 = (f32[6,16,128]{2,1,0:T(8,128)S(1)}, f32[6,16,128]{2,1,0:T(8,128)S(1)}, u32[]{:S(2)}, u32[]{:S(2)}) collective-permute-start(f32[6,16,128]{2,1,0:T(8,128)S(1)} %get-tuple-element.92), channel_id=1, source_target_pairs={{0,2},{1,3},{2,4},{3,5},{4,6},{5,7},{6,0},{7,1},{8,10},{9,11},{10,... | collective-permute-start | bytes 147464 | tf_op jit(solution)/shard_map/ppermute | solution.py:924
  8.2 7.1 %collective-permute-start.22 = (f32[3,16,128]{2,1,0:T(8,128)S(1)}, f32[3,16,128]{2,1,0:T(8,128)S(1)}, u32[]{:S(2)}, u32[]{:S(2)}) collective-permute-start(f32[3,16,128]{2,1,0:T(8,128)S(1)} %get-tuple-element.93), channel_id=1, source_target_pairs={{0,3},{1,4},{2,5},{3,6},{4,7},{5,0},{6,1},{7,2},{8,11},{9,12},{10,... | collective-permute-start | bytes 73736 | tf_op jit(solution)/shard_map/ppermute | solution.py:924
  9.7 7.5 %collective-permute-start.25 = (f32[6,16,128]{2,1,0:T(8,128)S(1)}, f32[6,16,128]{2,1,0:T(8,128)S(1)}, u32[]{:S(2)}, u32[]{:S(2)}) collective-permute-start(f32[6,16,128]{2,1,0:T(8,128)S(1)} %get-tuple-element.98), channel_id=1, source_target_pairs={{0,6},{1,7},{2,0},{3,1},{4,2},{5,3},{6,4},{7,5},{8,14},{9,15},{10,... | collective-permute-start | bytes 147464 | tf_op jit(solution)/shard_map/ppermute | solution.py:924
  15.4 5.1 %collective-permute-start.23 = (f32[5,16,128]{2,1,0:T(8,128)S(1)}, f32[5,16,128]{2,1,0:T(8,128)S(1)}, u32[]{:S(2)}, u32[]{:S(2)}) collective-permute-start(f32[5,16,128]{2,1,0:T(8,128)S(1)} %get-tuple-element.95), channel_id=1, source_target_pairs={{0,4},{1,5},{2,6},{3,7},{4,0},{5,1},{6,2},{7,3},{8,12},{9,13},{10,... | collective-permute-start | bytes 122888 | tf_op jit(solution)/shard_map/ppermute | solution.py:924
  15.4 4.7 %collective-permute-start.24 = (f32[3,16,128]{2,1,0:T(8,128)S(1)}, f32[3,16,128]{2,1,0:T(8,128)S(1)}, u32[]{:S(2)}, u32[]{:S(2)}) collective-permute-start(f32[3,16,128]{2,1,0:T(8,128)S(1)} %get-tuple-element.97), channel_id=1, source_target_pairs={{0,5},{1,6},{2,7},{3,0},{4,1},{5,2},{6,3},{7,4},{8,13},{9,14},{10,... | collective-permute-start | bytes 73736 | tf_op jit(solution)/shard_map/ppermute | solution.py:924
  20.9 5.3 %collective-permute-start.27 = (f32[19,8,128]{2,1,0:T(8,128)S(1)}, f32[19,8,128]{2,1,0:T(8,128)S(1)}, u32[]{:S(2)}, u32[]{:S(2)}) collective-permute-start(f32[19,8,128]{2,1,0:T(8,128)S(1)} %get-tuple-element.119), channel_id=1, source_target_pairs={{0,8},{8,0},{16,24},{24,16},{1,9},{9,1},{17,25},{25,17},{2,10},{10... | collective-permute-start | bytes 233480 | tf_op jit(solution)/shard_map/ppermute | solution.py:947
  21.0 5.2 %collective-permute-start.28 = (f32[19,8,128]{2,1,0:T(8,128)S(1)}, f32[19,8,128]{2,1,0:T(8,128)S(1)}, u32[]{:S(2)}, u32[]{:S(2)}) collective-permute-start(f32[19,8,128]{2,1,0:T(8,128)S(1)} %get-tuple-element.120), channel_id=1, source_target_pairs={{0,24},{8,16},{16,8},{24,0},{1,25},{9,17},{17,9},{25,1},{2,26},{10... | collective-permute-start | bytes 233480 | tf_op jit(solution)/shard_map/ppermute | solution.py:948
  22.6 3.6 %collective-permute-start.29 = (f32[8,128]{1,0:T(8,128)S(1)}, f32[8,128]{1,0:T(8,128)S(1)}, u32[]{:S(2)}, u32[]{:S(2)}) collective-permute-start(f32[8,128]{1,0:T(8,128)S(1)} %get-tuple-element.121.refs_21_), channel_id=1, source_target_pairs={{0,16},{8,24},{16,0},{24,8},{1,17},{9,25},{17,1},{25,9},{2,18},{10... | collective-permute-start | bytes 12296 | tf_op jit(solution)/shard_map/ppermute | solution.py:949
